TPU v7x, 256 devices: a whole 4x4x8 slice. The times are simulated.
256 devices in a mesh: dp: 32 (over z_lo, y, core), mp: 8 (over x, z_hi).
Axes of the slice: x: 4, y: 4, z: 8 (z_hi: 2, z_lo: 4; z = z_hi * 4 + z_lo), core: 2. Of those that a mesh axis runs over, the one named last changes fastest.
Arguments:
- preactivation: bfloat16 [4096, 14336], P('dp', 'mp'), may hold values from -6 to 6
- keep_codes: int32 [4096, 3584], P('dp', 'mp'), may hold values from 0 to 5
- down_weight: bfloat16 [14336, 4096], P('mp', 'dp'), may hold values from -0.046875 to 0.046875
- output_grad: bfloat16 [4096, 4096], P(('dp', 'mp')), may hold values from -24 to 24
Outputs:
- output: bfloat16 [4096, 4096], P(('dp', 'mp'))
- weight_grad: bfloat16 [14336, 4096], P('mp', 'dp')
- input_grad: bfloat16 [4096, 14336], P('dp', 'mp')
Inputs may be any that keep to these rules, and one draw needn't show every extreme that they name: `keep_codes`: code of one token's group of four hidden units.
All inputs are finite; a program needn't handle non-finite values.
Results may differ from a plain program's by a relative error of at most 0.015.
Values may be sent and summed in bfloat16 or wider, within the bound.
No kernel may reach another device: no remote copies, remote signals or barrier semaphores. Data moves between devices by JAX's collectives and lax.ppermute only.
A program may use at most 128 MiB of HBM per device.

v0:
```python
import math

import jax
import jax.numpy as jnp
from jax import lax
from jax.sharding import PartitionSpec as P

PAIRS = ((0, 1), (0, 2), (0, 3), (1, 2), (1, 3), (2, 3))


def keep_mask(codes, width):
    expanded = jnp.repeat(codes, 4, axis=1)
    lane = jnp.arange(width) % 4
    keep = jnp.zeros(expanded.shape, jnp.float32)
    for pattern, pair in enumerate(PAIRS):
        inside = (lane == pair[0]) | (lane == pair[1])
        keep = keep + ((expanded == pattern) & inside[None, :]).astype(jnp.float32)
    return keep


def on_device(preactivation, keep_codes, down_weight, output_grad):
    group_rows, block_width = preactivation.shape
    grad_scale = 1.0 / math.sqrt(group_rows * lax.axis_size("dp"))
    keep = keep_mask(keep_codes, block_width)
    positive = jnp.maximum(preactivation.astype(jnp.float32), 0.0)
    hidden = (keep * positive * positive).astype(jnp.bfloat16)
    grad_group = lax.all_gather(output_grad, "mp", axis=0, tiled=True)
    piece = lax.all_gather(down_weight, "dp", axis=1, tiled=True)
    columns = jnp.dot(hidden, piece, preferred_element_type=jnp.float32)
    back_total = lax.dot_general(
        grad_group, piece, (((1,), (1,)), ((), ())), preferred_element_type=jnp.float32
    )
    output = lax.psum_scatter(columns.astype(jnp.bfloat16), "mp", scatter_dimension=0, tiled=True)
    input_grad = (2.0 * positive * keep * back_total).astype(jnp.bfloat16)
    output, input_grad = (output, input_grad)
    grad_columns = lax.all_to_all(grad_group, "dp", split_axis=1, concat_axis=0, tiled=True)
    summed = lax.dot_general(
        lax.all_gather(hidden, "dp", axis=0, tiled=True),
        grad_columns,
        (((0,), (0,)), ((), ())),
        preferred_element_type=jnp.float32,
    )
    weight_grad = (summed * grad_scale).astype(jnp.bfloat16)
    return (output, weight_grad, input_grad)


def solution(mesh):
    in_specs = (P("dp", "mp"), P("dp", "mp"), P("mp", "dp"), P(("dp", "mp"), None))
    out_specs = (P(("dp", "mp"), None), P("mp", "dp"), P("dp", "mp"))
    return jax.shard_map(
        on_device, mesh=mesh, in_specs=in_specs, out_specs=out_specs, check_vma=False
    )
```

profile of v0, /device:TPU:8, one launch (start us, length us, event | category | flops | bytes accessed | tf_op | source)
XLA Modules:
  0.0 390.8 jit_solution(15245613946331707203)
XLA Ops:
  7.2 0.0 all-gather.8.cloned.1.call-start
  7.2 0.7 all-gather.8.cloned.1.call-update
  7.9 0.0 all-gather.4.cloned.1.call-start
  7.9 0.7 all-gather.4.cloned.1.call-update
  8.6 0.0 all-gather.6.cloned.1.call-start
  8.7 1.1 broadcast_compare_fusion.5
  9.8 0.2 broadcast_in_dim.19
  10.1 0.3 copy.27
  10.4 0.2 broadcast_in_dim.22
  10.6 0.3 copy.30
  10.9 0.2 broadcast_in_dim.21
  11.1 0.3 copy.29
  11.5 0.2 broadcast_in_dim.20
  11.7 0.3 copy.28
  12.0 0.2 broadcast_in_dim.24
  12.2 0.3 copy.32
  12.6 0.2 broadcast_in_dim.23
  12.8 0.3 copy.31
  13.2 0.1 copy-done.7
  13.2 0.5 copy-done.9
  13.8 2.6 fusion.2
  16.4 0.0 reduce-scatter.2.cloned.1.call-start
  16.5 58.9 %all-gather.8.cloned.1.call-done = bf16[128,4096]{1,0:T(8,128)(2,1)} async-done(((bf16[16,4096]{1,0:T(8,128)(2,1)}), bf16[128,4096]{1,0:T(8,128)(2,1)}) %all-gather.8.cloned.1.call-update) | async-done | bytes 1048592 | tf_op jit(solution)/shard_map/all_gather | solution.py:27
  75.4 1.7 copy.33
  77.1 39.2 %all_to_all.19 = bf16[128,32,128]{0,2,1:T(8,128)(2,1)S(1)} all-to-all(bf16[128,32,128]{0,2,1:T(8,128)(2,1)S(1)} %bitcast.16), channel_id=1, replica_groups=mesh['dp'=32,'mp'=8] {'dp'}, dimensions={1} | all-to-all | bytes 2097152 | tf_op jit(solution)/shard_map/all_to_all | solution.py:36
  116.4 1.3 copy.34
  117.7 85.4 %all-gather.4.cloned.1.call-done = bf16[1792,4096]{1,0:T(8,128)(2,1)} async-done(((bf16[1792,128]{1,0:T(8,128)(2,1)}), bf16[1792,4096]{1,0:T(8,128)(2,1)}) %all-gather.4.cloned.1.call-update) | async-done | bytes 14680080 | tf_op jit(solution)/shard_map/all_gather | solution.py:28
  203.1 8.4 %convolution_convert_fusion = bf16[128,4096]{1,0:T(8,128)(2,1)} fusion(bf16[128,1792]{1,0:T(8,128)(2,1)} %fusion.2, bf16[1792,4096]{1,0:T(8,128)(2,1)} %all-gather.4.cloned.1.call-done), kind=kOutput, calls=%fused_computation | convolution fusion | flops 1879572480 | bytes 16187392 | tf_op jit(solution)/shard_map/dot_general | solution.py:29
  211.6 11.7 %fusion = bf16[128,1792]{1,0:T(8,128)(2,1)} fusion(bf16[128,4096]{1,0:T(8,128)(2,1)S(1)} %copy-done, bf16[1792,4096]{1,0:T(8,128)(2,1)} %all-gather.4.cloned.1.call-done, bf16[128,1792]{1,0:T(8,128)(2,1)S(1)} %copy-done.11, pred[128,1792]{1,0:T(32,128)(4,1)S(1)} %copy-done.8, pred[1792]{0:T(1024)(128)(4,1)S(1)} %get-tuple-element.14, ...), kind=kOutput, calls=%fused_computation.3 | convolution fusion | flops 1884323840 | bytes 18033152 | tf_op jit(solution)/shard_map/dot_general | solution.py:30
  223.3 69.0 %all-gather.6.cloned.1.call-done = bf16[4096,1792]{1,0:T(8,128)(2,1)} async-done(((bf16[128,1792]{1,0:T(8,128)(2,1)}), bf16[4096,1792]{1,0:T(8,128)(2,1)}) %all-gather.6.cloned.1.call-update) | async-done | bytes 14680080 | tf_op jit(solution)/shard_map/all_gather | solution.py:38
  292.3 10.2 %fusion.1 = bf16[1792,128]{1,0:T(8,128)(2,1)} fusion(bf16[4096,1792]{1,0:T(8,128)(2,1)} %all-gather.6.cloned.1.call-done, bf16[4096,128]{1,0:T(8,128)(2,1)} %bitcast.17), kind=kOutput, calls=%fused_computation.4 | convolution fusion | flops 1879506944 | bytes 16187392 | tf_op jit(solution)/shard_map/dot_general | solution.py:37
  302.5 81.8 %reduce-scatter.2.cloned.1.call-done = bf16[16,4096]{1,0:T(8,128)(2,1)} async-done(((bf16[128,4096]{1,0:T(8,128)(2,1)}), bf16[16,4096]{1,0:T(8,128)(2,1)}) %reduce-scatter.2.cloned.1.call-update) | async-done | bytes 131088 | tf_op jit(solution)/shard_map/reduce_scatter | solution.py:33
  (27 shorter events, 0.1 us)
Async XLA Ops:
  7.2 68.3 %all-gather.8.cloned.1.call-start = ((), (), s32[]{:S(2)}) async-start(), calls=%async_computation.5 | async-start | bytes 1179648 | tf_op jit(solution)/shard_map/all_gather | solution.py:27
  7.9 195.2 %all-gather.4.cloned.1.call-start = ((), (), s32[]{:S(2)}) async-start(), calls=%async_computation.2 | async-start | bytes 15138816 | tf_op jit(solution)/shard_map/all_gather | solution.py:28
  8.6 283.6 %all-gather.6.cloned.1.call-start = ((), (), s32[]{:S(2)}) async-start(), calls=%async_computation.4 | async-start | bytes 15138816 | tf_op jit(solution)/shard_map/all_gather | solution.py:38
  10.9 2.3 copy-start.1
  11.5 1.7 copy-start.3
  12.0 1.2 copy-start.5
  12.5 0.7 copy-start.7
  13.1 0.7 copy-start.9
  16.4 367.8 %reduce-scatter.2.cloned.1.call-start = ((), (), s32[]{:S(2)}) async-start(), calls=%async_computation.3 | async-start | bytes 1179648 | tf_op jit(solution)/shard_map/reduce_scatter | solution.py:33
  75.4 136.1 %copy-start = (bf16[128,4096]{1,0:T(8,128)(2,1)S(1)}, bf16[128,4096]{1,0:T(8,128)(2,1)}, u32[]{:S(2)}) copy-start(bf16[128,4096]{1,0:T(8,128)(2,1)} %all-gather.8.cloned.1.call-done) | copy-start | bytes 3145732
  116.4 95.2 %copy-start.2 = (pred[128,1792]{1,0:T(32,128)(4,1)S(1)}, pred[128,1792]{1,0:T(32,128)(4,1)}, u32[]{:S(2)}) copy-start(pred[128,1792]{1,0:T(32,128)(4,1)} %copy-done.1) | copy-start | bytes 688132
  116.4 95.2 %copy-start.4 = (pred[128,1792]{1,0:T(32,128)(4,1)S(1)}, pred[128,1792]{1,0:T(32,128)(4,1)}, u32[]{:S(2)}) copy-start(pred[128,1792]{1,0:T(32,128)(4,1)} %copy-done.3) | copy-start | bytes 688132
  116.4 95.2 %copy-start.6 = (pred[128,1792]{1,0:T(32,128)(4,1)S(1)}, pred[128,1792]{1,0:T(32,128)(4,1)}, u32[]{:S(2)}) copy-start(pred[128,1792]{1,0:T(32,128)(4,1)} %copy-done.5) | copy-start | bytes 688132
  116.4 95.2 %copy-start.8 = (pred[128,1792]{1,0:T(32,128)(4,1)S(1)}, pred[128,1792]{1,0:T(32,128)(4,1)}, u32[]{:S(2)}) copy-start(pred[128,1792]{1,0:T(32,128)(4,1)} %copy-done.7) | copy-start | bytes 688132
  117.7 93.9 %copy-start.10 = (pred[128,1792]{1,0:T(32,128)(4,1)S(1)}, pred[128,1792]{1,0:T(32,128)(4,1)}, u32[]{:S(2)}) copy-start(pred[128,1792]{1,0:T(32,128)(4,1)} %copy-done.9) | copy-start | bytes 688132
  117.7 93.9 %copy-start.11 = (bf16[128,1792]{1,0:T(8,128)(2,1)S(1)}, bf16[128,1792]{1,0:T(8,128)(2,1)}, u32[]{:S(2)}) copy-start(bf16[128,1792]{1,0:T(8,128)(2,1)} %param.4) | copy-start | bytes 1376260
Sparse Core Ops, SparseCore 0:
  10.6 64.7 all-gather.7
  77.2 125.8 all-gather.3
  205.5 86.6 all-gather.5
  296.6 87.5 reduce-scatter.1
where the time goes:
time: 391 us
  waiting for transfers between devices  297 us (76%)
  blocking collectives  39.2 us (10%)
  matrix products  30.3 us (8%)
  between operations  14 us (4%)
  local copies, waits for them, and re-layouts  6.8 us (2%)
    all_gather x1, waiting for transfers between devices, on_device(): piece = lax.all_gather(down_weight, 'dp', axis=1, tiled=True)  85.4 us
    reduce_scatter x1, waiting for transfers between devices, on_device(): lax.psum_scatter(columns.astype(jnp.bfloat16), 'mp', scatter_dimension=0,...  81.8 us
    all_gather x1, waiting for transfers between devices, on_device(): lax.all_gather(hidden, 'dp', axis=0, tiled=True)  69 us
    all_gather x1, waiting for transfers between devices, on_device(): grad_group = lax.all_gather(output_grad, 'mp', axis=0, tiled=True)  58.9 us
    all_to_all x1, blocking collectives, on_device(): lax.all_to_all(grad_group, 'dp', split_axis=1, concat_axis=0, tiled=True)  39.2 us
    dot_general x1, matrix products, on_device(): lax.dot_general(grad_group, piece, (((1,), (1,)), ((), ())), preferred_el...  11.7 us
    dot_general x1, matrix products, on_device(): lax.dot_general(lax.all_gather(hidden, 'dp', axis=0, tiled=True), grad_co...  10.2 us
    dot_general x1, matrix products, on_device(): columns = jnp.dot(hidden, piece, preferred_element_type=jnp.float32)  8.4 us
  transfers between devices with their start and end apart: 4, of which 4 were waited for; matrix products, arithmetic and copies ran while one was open for 10% of the time, Pallas kernels for 0%

commit v1 on v0

v1 whole, which is shorter than its diff:
```python
import math

import jax
import jax.numpy as jnp
from jax import lax
from jax.experimental import pallas as pl
from jax.experimental.pallas import tpu as pltpu
from jax.sharding import PartitionSpec as P

BF16 = jnp.bfloat16
F32 = jnp.float32

CORE = 1
ROWS_Y, ROWS_Z = 2, 16
COLS_Y, COLS_Z = 6, 8
TOKEN_PARTS = (0, ROWS_Y, ROWS_Z, ROWS_Y ^ ROWS_Z)
COLUMN_PARTS = (0, COLS_Y, COLS_Z, COLS_Y ^ COLS_Z)
COLUMN_BLOCKS = COLUMN_PARTS + tuple(k ^ CORE for k in COLUMN_PARTS)
STEP = 256


def swap(array, axis, size, k):
    return lax.ppermute(array, axis, [(i, i ^ k) for i in range(size)])


def dp_swap(array, k):
    return swap(array, "dp", 32, k)


def mp_swap(array, k):
    return swap(array, "mp", 8, k)


def place(axis):
    return jnp.reshape(lax.axis_index(axis).astype(jnp.int32), (1,))


def in_smem():
    return pl.BlockSpec(memory_space=pltpu.SMEM)


def whole():
    return pl.BlockSpec(memory_space=pltpu.VMEM)


def call(kernel, out_shape, scratch=(), grid=None, in_specs=None, out_specs=None, flops=0, moved=0):
    return pl.pallas_call(
        kernel,
        out_shape=out_shape,
        grid=grid or (),
        in_specs=in_specs,
        out_specs=out_specs,
        scratch_shapes=list(scratch),
        compiler_params=pltpu.CompilerParams(vmem_limit_bytes=40 * 2**20),
        cost_estimate=pl.CostEstimate(flops=flops, bytes_accessed=moved, transcendentals=0),
    )


def mask_kernel(pre_ref, code_ref, hidden_ref, slope_ref):
    rows, width = pre_ref.shape
    groups = code_ref.shape[1]
    for at in range(0, groups, 128):
        size = min(128, groups - at)
        spread = (
            lax.broadcasted_iota(jnp.int32, (size, 4 * size), 1) // 4
            == lax.broadcasted_iota(jnp.int32, (size, 4 * size), 0)
        ).astype(BF16)
        codes = code_ref[:, at : at + size].astype(F32).astype(BF16)
        code = jnp.dot(codes, spread, preferred_element_type=F32)
        lane = lax.broadcasted_iota(jnp.int32, code.shape, 1) % 4
        kept = (
            ((lane == 0) & (code < 2.5))
            | ((lane == 1) & ((code == 0.0) | (code == 3.0) | (code == 4.0)))
            | ((lane == 2) & ((code == 1.0) | (code == 3.0) | (code == 5.0)))
            | ((lane == 3) & ((code == 2.0) | (code > 3.5)))
        )
        columns = slice(4 * at, 4 * (at + size))
        positive = jnp.where(kept, jnp.maximum(pre_ref[:, columns].astype(F32), 0.0), 0.0)
        hidden_ref[:, columns] = (positive * positive).astype(BF16)
        slope_ref[:, columns] = (2.0 * positive).astype(BF16)


def split_kernel(place_ref, grad_ref, *out_refs):
    me = place_ref[0]
    for out_ref, token in zip(out_refs, TOKEN_PARTS):
        for n, column in enumerate(COLUMN_BLOCKS):
            at = pl.multiple_of((me ^ (token ^ column)) * 128, 128)
            out_ref[:, n * 128 : (n + 1) * 128] = grad_ref[:, pl.ds(at, 128)]


def join_kernel(place_ref, *refs):
    me = place_ref[0]
    out_ref = refs[-1]
    for part_ref, token in zip(refs[:-1], TOKEN_PARTS):
        for n, column in enumerate(COLUMN_BLOCKS):
            at = pl.multiple_of((me ^ (token ^ column)) * 128, 128)
            out_ref[:, pl.ds(at, 128)] = part_ref[:, n * 128 : (n + 1) * 128]


def gather_rows(me, grad_refs, rows_ref):
    for rx, ref in enumerate(grad_refs):
        for rz in range(2):
            for k in range(4):
                at = pl.multiple_of(k * 128 + (me ^ (2 * rx + rz)) * 16, 16)
                rows_ref[pl.ds(at, 16), :] = ref[rz, k]


def weight_grad_kernel(scale, place_ref, *refs):
    grad_refs, hidden_refs, (near_ref, far_ref), rows_ref = refs[:4], refs[4:8], refs[8:10], refs[10]

    @pl.when(pl.program_id(0) == 0)
    def _():
        gather_rows(place_ref[0], grad_refs, rows_ref)

    hidden = jnp.concatenate([ref[...] for ref in hidden_refs], axis=0)
    product = lax.dot_general(
        hidden, rows_ref[...], (((0,), (0,)), ((), ())), preferred_element_type=F32
    )
    product = (product * scale).astype(BF16)
    for n in range(4):
        near_ref[n] = product[:, n * 128 : (n + 1) * 128]
        far_ref[n] = product[:, (n + 4) * 128 : (n + 5) * 128]


def token_kernel(place_ref, *refs):
    grad_refs, hidden_refs, weight_refs = refs[:4], refs[4:8], refs[8:16]
    near_ref, far_ref = refs[16:18]
    out_refs, rows_ref, total_ref = refs[18:22], refs[22], refs[23]
    step = pl.program_id(0)
    me = place_ref[0]

    @pl.when(step == 0)
    def _():
        gather_rows(me, grad_refs, rows_ref)

    hidden = jnp.concatenate([ref[...] for ref in hidden_refs], axis=0)
    weight = jnp.concatenate([ref[...] for ref in weight_refs], axis=1)
    back = lax.dot_general(
        rows_ref[...], weight, (((1,), (1,)), ((), ())), preferred_element_type=F32
    ).astype(BF16)
    for n, (ref, at) in enumerate(((near_ref, 0), (far_ref, 0), (near_ref, 1), (far_ref, 1))):
        ref[at] = back[n * 128 : (n + 1) * 128]
    part = jnp.dot(hidden, weight, preferred_element_type=F32)

    @pl.when(step == 0)
    def _():
        total_ref[...] = part

    @pl.when(step > 0)
    def _():
        total_ref[...] += part

    @pl.when(step == pl.num_programs(0) - 1)
    def _():
        for rx, ref in enumerate(out_refs):
            for rz in range(2):
                for k in range(4):
                    at = pl.multiple_of(k * 128 + (me ^ (2 * rx + rz)) * 16, 16)
                    ref[rz, k] = total_ref[pl.ds(at, 16), :].astype(BF16)


def add(*arrays):
    total = arrays[0].astype(F32)
    for array in arrays[1:]:
        total = total + array.astype(F32)
    return total


def on_device(preactivation, keep_codes, down_weight, output_grad):
    rows, width = preactivation.shape
    scale = 1.0 / math.sqrt(rows * lax.axis_size("dp"))
    dp_place, mp_place = place("dp"), place("mp")
    shape = jax.ShapeDtypeStruct
    piece = shape((rows, width), BF16)

    grad_parts = call(
        split_kernel,
        [shape((16, 1024), BF16)] * 4,
        in_specs=[in_smem(), whole()],
        out_specs=[whole()] * 4,
        moved=2 * 131072,
    )(dp_place, output_grad)
    grad_parts = [grad_parts[0]] + [dp_swap(p, k) for p, k in zip(grad_parts[1:], TOKEN_PARTS[1:])]
    grad_own = jnp.stack(grad_parts)
    grad_pair = jnp.stack([grad_own, mp_swap(grad_own, 1)])
    grads = [grad_pair] + [mp_swap(grad_pair, 2 * rx) for rx in (1, 2, 3)]

    weight_z = dp_swap(down_weight, COLS_Z)
    weight_y = dp_swap(down_weight, COLS_Y)
    weight_yz = dp_swap(weight_z, COLS_Y)
    weights = [down_weight, weight_y, weight_z, weight_yz]
    weights = weights + [dp_swap(w, CORE) for w in weights]

    hidden, slope = call(
        mask_kernel,
        [piece, piece],
        in_specs=[whole()] * 2,
        out_specs=[whole()] * 2,
        flops=2 * rows * 448 * 512,
        moved=3 * 458752 + 229376,
    )(preactivation, keep_codes)
    hidden_z = dp_swap(hidden, ROWS_Z)
    hidden_y = dp_swap(hidden, ROWS_Y)
    hidden_yz = dp_swap(hidden_z, ROWS_Y)
    hiddens = [hidden, hidden_y, hidden_z, hidden_yz]

    grad_spec = pl.BlockSpec((2, 4, 16, 1024), lambda f: (0, 0, 0, 0))
    hidden_spec = pl.BlockSpec((rows, STEP), lambda f: (0, f))
    weight_spec = pl.BlockSpec((STEP, 128), lambda f: (f, 0))
    near, far = call(
        lambda *refs: weight_grad_kernel(scale, *refs),
        [shape((4, width, 128), BF16)] * 2,
        grid=(width // STEP,),
        in_specs=[in_smem()] + [grad_spec] * 4 + [hidden_spec] * 4,
        out_specs=[pl.BlockSpec((4, STEP, 128), lambda f: (0, f, 0))] * 2,
        scratch=[pltpu.VMEM((512, 1024), BF16)],
        flops=2 * 512 * 1024 * width,
        moved=6 * 2**20,
    )(mp_place, *grads, *hiddens)
    arrived = dp_swap(far, CORE)
    send = add(near[1::2], arrived[1::2]).astype(BF16)
    arrived_y = dp_swap(send, COLS_Y)
    send = add(near[2], arrived[2], arrived_y[1]).astype(BF16)
    weight_grad = add(near[0], arrived[0], arrived_y[0], dp_swap(send, COLS_Z)).astype(BF16)

    outs = call(
        token_kernel,
        [shape((2, rows, width), BF16)] * 2 + [shape((2, 4, 16, 1024), BF16)] * 4,
        grid=(width // STEP,),
        in_specs=[in_smem()] + [grad_spec] * 4 + [hidden_spec] * 4 + [weight_spec] * 8,
        out_specs=[pl.BlockSpec((2, rows, STEP), lambda f: (0, 0, f))] * 2 + [grad_spec] * 4,
        scratch=[pltpu.VMEM((512, 1024), BF16), pltpu.VMEM((512, 1024), F32)],
        flops=4 * 512 * 1024 * width,
        moved=9 * 2**20,
    )(mp_place, *grads, *hiddens, *weights)
    near, far, parts = outs[0], outs[1], outs[2:]
    arrived = dp_swap(far, ROWS_Y)
    send = add(near[1], arrived[1]).astype(BF16)
    back = add(near[0], arrived[0], dp_swap(send, ROWS_Z))
    input_grad = (slope.astype(F32) * back).astype(BF16)

    parts = [parts[0]] + [mp_swap(p, 2 * rx) for rx, p in zip((1, 2, 3), parts[1:])]
    pair = add(*parts)
    total = add(pair[0], mp_swap(pair[1].astype(BF16), 1)).astype(BF16)
    pieces = [total[0]] + [dp_swap(total[n], k) for n, k in enumerate(TOKEN_PARTS) if n]
    output = call(
        join_kernel,
        shape((16, 4096), BF16),
        in_specs=[in_smem()] + [whole()] * 4,
        out_specs=whole(),
        moved=2 * 131072,
    )(dp_place, *pieces)
    return (output, weight_grad, input_grad)


def solution(mesh):
    in_specs = (P("dp", "mp"), P("dp", "mp"), P("mp", "dp"), P(("dp", "mp"), None))
    out_specs = (P(("dp", "mp"), None), P("mp", "dp"), P("dp", "mp"))
    return jax.shard_map(
        on_device, mesh=mesh, in_specs=in_specs, out_specs=out_specs, check_vma=False
    )
```

time: 391 us -> 147 us (0.38)
  the two profiles are of different devices: /device:TPU:8 before, /device:TPU:97 now
where the time goes in v1:
time: 147 us
  waiting for transfers between devices  77.2 us (53%)
  starting transfers between devices  44 us (30%)
  Pallas kernels  15.7 us (11%)
  local copies, waits for them, and re-layouts  6.32 us (4%)
  other arithmetic  2.8 us (2%)
    ppermute x29, waiting for transfers between devices, swap(): return lax.ppermute(array, axis, [(i, i ^ k) for i in range(size)])  77.2 us
    ppermute x29, starting transfers between devices, swap(): return lax.ppermute(array, axis, [(i, i ^ k) for i in range(size)])  44 us
    pallas_call x1, Pallas kernels, on_device(): call(token_kernel, [shape((2, rows, width), BF16)] * 2 + [shape((2, 4, 16...  8.38 us
    unnamed x19, local copies, waits for them, and re-layouts  6.29 us
    pallas_call x1, Pallas kernels, on_device(): call(lambda *refs: weight_grad_kernel(scale, *refs), [shape((4, width, 12...  4.94 us
  transfers between devices with their start and end apart: 29, of which 15 were waited for; matrix products, arithmetic and copies ran while one was open for 2% of the time, Pallas kernels for 11%

profile of v1, /device:TPU:97, one launch (start us, length us, event | category | flops | bytes accessed | tf_op | source)
XLA Modules:
  0.0 146.8 jit_solution(15579675961598631816)
XLA Ops:
  1.6 1.4 collective-permute-start
  3.0 2.2 %collective-permute-start.2 = (bf16[16,1024]{1,0:T(8,128)(2,1)S(1)}, bf16[16,1024]{1,0:T(8,128)(2,1)S(1)}, u32[]{:S(2)}, u32[]{:S(2)}) collective-permute-start(bf16[16,1024]{1,0:T(8,128)(2,1)S(1)} %get-tuple-element.20), channel_id=1, source_target_pairs={{0,144},{8,152},{16,128},{24,136},{32,176},{40,184},{48,160},{56,1... | collective-permute-start | bytes 98312 | tf_op jit(solution)/shard_map/ppermute | solution.py:23
  7.3 1.6 %shard_map.68 = (bf16[128,1792]{1,0:T(8,128)(2,1)S(1)}, bf16[128,1792]{1,0:T(8,128)(2,1)S(1)}) custom-call(bf16[128,1792]{1,0:T(8,128)(2,1)S(1)} %copy-done, s32[128,448]{1,0:T(8,128)S(1)} %copy.7.code_ref), custom_call_target="tpu_custom_call" | custom-call | flops 58720256 | bytes 1605632 | tf_op jit(solution)/shard_map/pallas_call | solution.py:194
  9.2 5.4 %collective-permute-start.3 = (bf16[4,16,1024]{2,1,0:T(8,128)(2,1)S(1)}, bf16[4,16,1024]{2,1,0:T(8,128)(2,1)S(1)}, u32[]{:S(2)}, u32[]{:S(2)}) collective-permute-start(bf16[4,16,1024]{2,1,0:T(8,128)(2,1)S(1)} %get-tuple-element.36), channel_id=1, source_target_pairs={{0,1},{1,0},{2,3},{3,2},{4,5},{5,4},{6,7},{7,6},{8,9},{9,8},{10,11... | collective-permute-start | bytes 393224 | tf_op jit(solution)/shard_map/ppermute | solution.py:23
  14.6 14.4 %collective-permute-done.3 = bf16[4,16,1024]{2,1,0:T(8,128)(2,1)S(1)} collective-permute-done((bf16[4,16,1024]{2,1,0:T(8,128)(2,1)S(1)}, bf16[4,16,1024]{2,1,0:T(8,128)(2,1)S(1)}, u32[]{:S(2)}, u32[]{:S(2)}) %collective-permute-start.3) | collective-permute-done | bytes 131104 | tf_op jit(solution)/shard_map/ppermute | solution.py:23
  29.0 2.6 %collective-permute-start.6 = (bf16[2,4,16,1024]{3,2,1,0:T(8,128)(2,1)S(1)}, bf16[2,4,16,1024]{3,2,1,0:T(8,128)(2,1)S(1)}, u32[]{:S(2)}, u32[]{:S(2)}) collective-permute-start(bf16[2,4,16,1024]{3,2,1,0:T(8,128)(2,1)S(1)} %pad_maximum_fusion.refs_0_.refs_1_), channel_id=1, source_target_pairs={{0,6},{1,7},{2,4},{3,5},{4,2},{5,3},{6,0},{7,1},{8,14},{9,15},{10,... | collective-permute-start | bytes 786440 | tf_op jit(solution)/shard_map/ppermute | solution.py:23
  31.5 1.3 collective-permute-start.7
  32.8 4.6 %collective-permute-done.8.refs_6_.refs_7_ = bf16[128,1792]{1,0:T(8,128)(2,1)S(1)} collective-permute-done((bf16[128,1792]{1,0:T(8,128)(2,1)S(1)}, bf16[128,1792]{1,0:T(8,128)(2,1)S(1)}, u32[]{:S(2)}, u32[]{:S(2)}) %collective-permute-start.8) | collective-permute-done | bytes 458784 | tf_op jit(solution)/shard_map/ppermute | solution.py:23
  37.4 1.3 collective-permute-start.9
  38.7 2.7 %collective-permute-start.5 = (bf16[2,4,16,1024]{3,2,1,0:T(8,128)(2,1)S(1)}, bf16[2,4,16,1024]{3,2,1,0:T(8,128)(2,1)S(1)}, u32[]{:S(2)}, u32[]{:S(2)}) collective-permute-start(bf16[2,4,16,1024]{3,2,1,0:T(8,128)(2,1)S(1)} %pad_maximum_fusion.refs_0_.refs_1_), channel_id=1, source_target_pairs={{0,4},{1,5},{2,6},{3,7},{4,0},{5,1},{6,2},{7,3},{8,12},{9,13},{10,... | collective-permute-start | bytes 786440 | tf_op jit(solution)/shard_map/ppermute | solution.py:23
  42.5 4.7 %collective-permute-done.5.refs_2_.refs_3_ = bf16[2,4,16,1024]{3,2,1,0:T(8,128)(2,1)S(1)} collective-permute-done((bf16[2,4,16,1024]{3,2,1,0:T(8,128)(2,1)S(1)}, bf16[2,4,16,1024]{3,2,1,0:T(8,128)(2,1)S(1)}, u32[]{:S(2)}, u32[]{:S(2)}) %collective-permute-start.5) | collective-permute-done | bytes 262176 | tf_op jit(solution)/shard_map/ppermute | solution.py:23
  47.9 1.9 %collective-permute-start.10 = (bf16[1792,128]{1,0:T(8,128)(2,1)S(1)}, bf16[1792,128]{1,0:T(8,128)(2,1)}, u32[]{:S(2)}, u32[]{:S(2)}) collective-permute-start(bf16[1792,128]{1,0:T(8,128)(2,1)S(1)} %copy-done.2), channel_id=1, source_target_pairs={{0,48},{8,56},{16,32},{24,40},{32,16},{40,24},{48,0},{56,8},{64,11... | collective-permute-start | bytes 1376264 | tf_op jit(solution)/shard_map/ppermute | solution.py:23
  50.6 2.4 %collective-permute-done.4.refs_1_.refs_2_ = bf16[2,4,16,1024]{3,2,1,0:T(8,128)(2,1)} collective-permute-done((bf16[2,4,16,1024]{3,2,1,0:T(8,128)(2,1)S(1)}, bf16[2,4,16,1024]{3,2,1,0:T(8,128)(2,1)}, u32[]{:S(2)}, u32[]{:S(2)}) %collective-permute-start.4) | collective-permute-done | bytes 262176 | tf_op jit(solution)/shard_map/ppermute | solution.py:23
  54.9 4.9 %shard_map.71 = (bf16[4,1792,128]{2,1,0:T(8,128)(2,1)S(1)}, bf16[4,1792,128]{2,1,0:T(8,128)(2,1)S(1)}) custom-call(s32[1]{0:T(128)} %bitcast.1.place_ref.refs_0_, bf16[2,4,16,1024]{3,2,1,0:T(8,128)(2,1)S(1)} %pad_maximum_fusion.refs_0_.refs_1_, bf16[2,4,16,1024]{3,2,1,0:T(8,128)(2,1)} %collective-permute-done.4.refs_1_.refs_2_, ...), custom_call_target="tpu_custom_call" | custom-call | flops 1879048192 | bytes 6291456 | tf_op jit(solution)/shard_map/pallas_call | solution.py:210
  59.9 1.8 %collective-permute-start.24 = (bf16[4,1792,128]{2,1,0:T(8,128)(2,1)S(1)}, bf16[4,1792,128]{2,1,0:T(8,128)(2,1)S(1)}, u32[]{:S(2)}, u32[]{:S(2)}) collective-permute-start(bf16[4,1792,128]{2,1,0:T(8,128)(2,1)S(1)} %get-tuple-element.27), channel_id=1, source_target_pairs={{0,8},{8,0},{16,24},{24,16},{32,40},{40,32},{48,56},{56,48},{64,72... | collective-permute-start | bytes 5505032 | tf_op jit(solution)/shard_map/ppermute | solution.py:23
  62.2 3.5 %collective-permute-start.14 = (bf16[1792,128]{1,0:T(8,128)(2,1)}, bf16[1792,128]{1,0:T(8,128)(2,1)S(1)}, u32[]{:S(2)}, u32[]{:S(2)}) collective-permute-start(bf16[1792,128]{1,0:T(8,128)(2,1)} %collective-permute-done.10.refs_9_), channel_id=1, source_target_pairs={{0,8},{8,0},{16,24},{24,16},{32,40},{40,32},{48,56},{56,48},{64,72... | collective-permute-start | bytes 1376264 | tf_op jit(solution)/shard_map/ppermute | solution.py:23
  65.8 2.3 %collective-permute-done.12.refs_11_ = bf16[1792,128]{1,0:T(8,128)(2,1)} collective-permute-done((bf16[1792,128]{1,0:T(8,128)(2,1)S(1)}, bf16[1792,128]{1,0:T(8,128)(2,1)}, u32[]{:S(2)}, u32[]{:S(2)}) %collective-permute-start.12) | collective-permute-done | bytes 458784 | tf_op jit(solution)/shard_map/ppermute | solution.py:23
  68.0 4.0 %collective-permute-start.16 = (bf16[1792,128]{1,0:T(8,128)(2,1)}, bf16[1792,128]{1,0:T(8,128)(2,1)S(1)}, u32[]{:S(2)}, u32[]{:S(2)}) collective-permute-start(bf16[1792,128]{1,0:T(8,128)(2,1)} %collective-permute-done.12.refs_11_), channel_id=1, source_target_pairs={{0,8},{8,0},{16,24},{24,16},{32,40},{40,32},{48,56},{56,48},{64,72... | collective-permute-start | bytes 1376264 | tf_op jit(solution)/shard_map/ppermute | solution.py:23
  72.0 1.6 %collective-permute-done.16.refs_15_ = bf16[1792,128]{1,0:T(8,128)(2,1)S(1)} collective-permute-done((bf16[1792,128]{1,0:T(8,128)(2,1)}, bf16[1792,128]{1,0:T(8,128)(2,1)S(1)}, u32[]{:S(2)}, u32[]{:S(2)}) %collective-permute-start.16) | collective-permute-done | bytes 458784 | tf_op jit(solution)/shard_map/ppermute | solution.py:23
  73.7 8.4 %shard_map.69 = (bf16[2,128,1792]{2,1,0:T(8,128)(2,1)S(1)}, bf16[2,128,1792]{2,1,0:T(8,128)(2,1)S(1)}, bf16[2,4,16,1024]{3,2,1,0:T(8,128)(2,1)S(1)}, bf16[2,4,16...) custom-call(s32[1]{0:T(128)} %bitcast.1.place_ref.refs_0_, ...), custom_call_target="tpu_custom_call" | custom-call | flops 3758096384 | bytes 9437184 | tf_op jit(solution)/shard_map/pallas_call | solution.py:226
  83.3 2.5 %collective-permute-start.18 = (bf16[2,4,16,1024]{3,2,1,0:T(8,128)(2,1)S(1)}, bf16[2,4,16,1024]{3,2,1,0:T(8,128)(2,1)S(1)}, u32[]{:S(2)}, u32[]{:S(2)}) collective-permute-start(bf16[2,4,16,1024]{3,2,1,0:T(8,128)(2,1)S(1)} %get-tuple-element.24), channel_id=1, source_target_pairs={{0,4},{1,5},{2,6},{3,7},{4,0},{5,1},{6,2},{7,3},{8,12},{9,13},{10,... | collective-permute-start | bytes 786440 | tf_op jit(solution)/shard_map/ppermute | solution.py:23
  86.0 3.6 %collective-permute-done.17 = bf16[2,4,16,1024]{3,2,1,0:T(8,128)(2,1)S(1)} collective-permute-done((bf16[2,4,16,1024]{3,2,1,0:T(8,128)(2,1)S(1)}, bf16[2,4,16,1024]{3,2,1,0:T(8,128)(2,1)S(1)}, u32[]{:S(2)}, u32[]{:S(2)}) %collective-permute-start.17) | collective-permute-done | bytes 262176 | tf_op jit(solution)/shard_map/ppermute | solution.py:23
  89.6 7.9 %collective-permute-done.18 = bf16[2,4,16,1024]{3,2,1,0:T(8,128)(2,1)S(1)} collective-permute-done((bf16[2,4,16,1024]{3,2,1,0:T(8,128)(2,1)S(1)}, bf16[2,4,16,1024]{3,2,1,0:T(8,128)(2,1)S(1)}, u32[]{:S(2)}, u32[]{:S(2)}) %collective-permute-start.18) | collective-permute-done | bytes 262176 | tf_op jit(solution)/shard_map/ppermute | solution.py:23
  97.5 2.0 %collective-permute-done.19 = bf16[2,4,16,1024]{3,2,1,0:T(8,128)(2,1)S(1)} collective-permute-done((bf16[2,4,16,1024]{3,2,1,0:T(8,128)(2,1)S(1)}, bf16[2,4,16,1024]{3,2,1,0:T(8,128)(2,1)S(1)}, u32[]{:S(2)}, u32[]{:S(2)}) %collective-permute-start.19) | collective-permute-done | bytes 262176 | tf_op jit(solution)/shard_map/ppermute | solution.py:23
  99.7 3.7 %collective-permute-start.20 = (bf16[4,16,1024]{2,1,0:T(8,128)(2,1)S(1)}, bf16[4,16,1024]{2,1,0:T(8,128)(2,1)S(1)}, u32[]{:S(2)}, u32[]{:S(2)}) collective-permute-start(bf16[4,16,1024]{2,1,0:T(8,128)(2,1)S(1)} %fusion.7), channel_id=1, source_target_pairs={{0,1},{1,0},{2,3},{3,2},{4,5},{5,4},{6,7},{7,6},{8,9},{9,8},{10,11... | collective-permute-start | bytes 393224 | tf_op jit(solution)/shard_map/ppermute | solution.py:23
  103.6 2.0 %collective-permute-start.25 = (bf16[2,1792,128]{2,1,0:T(8,128)(2,1)S(1)}, bf16[2,1792,128]{2,1,0:T(8,128)(2,1)S(1)}, u32[]{:S(2)}, u32[]{:S(2)}) collective-permute-start(bf16[2,1792,128]{2,1,0:T(8,128)(2,1)S(1)} %add_convert_fusion), channel_id=1, source_target_pairs={{0,48},{8,56},{16,32},{24,40},{32,16},{40,24},{48,0},{56,8},{64,11... | collective-permute-start | bytes 2752520 | tf_op jit(solution)/shard_map/ppermute | solution.py:23
  105.6 4.7 %collective-permute-done.20 = bf16[4,16,1024]{2,1,0:T(8,128)(2,1)S(1)} collective-permute-done((bf16[4,16,1024]{2,1,0:T(8,128)(2,1)S(1)}, bf16[4,16,1024]{2,1,0:T(8,128)(2,1)S(1)}, u32[]{:S(2)}, u32[]{:S(2)}) %collective-permute-start.20) | collective-permute-done | bytes 131104 | tf_op jit(solution)/shard_map/ppermute | solution.py:23
  110.4 1.7 %collective-permute-start.22 = (bf16[16,1024]{1,0:T(8,128)(2,1)S(1)}, bf16[16,1024]{1,0:T(8,128)(2,1)S(1)}, u32[]{:S(2)}, u32[]{:S(2)}) collective-permute-start(bf16[16,1024]{1,0:T(8,128)(2,1)S(1)} %get-tuple-element.32), channel_id=1, source_target_pairs={{0,128},{8,136},{16,144},{24,152},{32,160},{40,168},{48,176},{56,1... | collective-permute-start | bytes 98312 | tf_op jit(solution)/shard_map/ppermute | solution.py:23
  112.1 1.8 %collective-permute-start.21 = (bf16[16,1024]{1,0:T(8,128)(2,1)S(1)}, bf16[16,1024]{1,0:T(8,128)(2,1)S(1)}, u32[]{:S(2)}, u32[]{:S(2)}) collective-permute-start(bf16[16,1024]{1,0:T(8,128)(2,1)S(1)} %get-tuple-element.33), channel_id=1, source_target_pairs={{0,16},{8,24},{16,0},{24,8},{32,48},{40,56},{48,32},{56,40},{64,80... | collective-permute-start | bytes 98312 | tf_op jit(solution)/shard_map/ppermute | solution.py:23
  117.2 7.4 %collective-permute-done.25 = bf16[2,1792,128]{2,1,0:T(8,128)(2,1)S(1)} collective-permute-done((bf16[2,1792,128]{2,1,0:T(8,128)(2,1)S(1)}, bf16[2,1792,128]{2,1,0:T(8,128)(2,1)S(1)}, u32[]{:S(2)}, u32[]{:S(2)}) %collective-permute-start.25) | collective-permute-done | bytes 917536 | tf_op jit(solution)/shard_map/ppermute | solution.py:23
  124.9 9.5 %collective-permute-done.28 = bf16[128,1792]{1,0:T(8,128)(2,1)S(1)} collective-permute-done((bf16[128,1792]{1,0:T(8,128)(2,1)S(1)}, bf16[128,1792]{1,0:T(8,128)(2,1)S(1)}, u32[]{:S(2)}, u32[]{:S(2)}) %collective-permute-start.28) | collective-permute-done | bytes 458784 | tf_op jit(solution)/shard_map/ppermute | solution.py:23
  135.5 10.4 %collective-permute-done.26 = bf16[1792,128]{1,0:T(8,128)(2,1)S(1)} collective-permute-done((bf16[1792,128]{1,0:T(8,128)(2,1)S(1)}, bf16[1792,128]{1,0:T(8,128)(2,1)S(1)}, u32[]{:S(2)}, u32[]{:S(2)}) %collective-permute-start.26) | collective-permute-done | bytes 458784 | tf_op jit(solution)/shard_map/ppermute | solution.py:23
  (61 shorter events, 15.8 us)
Async XLA Ops:
  1.5 30.0 %copy-start.2 = (bf16[1792,128]{1,0:T(8,128)(2,1)S(1)}, bf16[1792,128]{1,0:T(8,128)(2,1)}, u32[]{:S(2)}) copy-start(bf16[1792,128]{1,0:T(8,128)(2,1)} %refs_8_.1) | copy-start | bytes 1376260
  1.6 7.6 %collective-permute-start = (bf16[16,1024]{1,0:T(8,128)(2,1)S(1)}, bf16[16,1024]{1,0:T(8,128)(2,1)S(1)}, u32[]{:S(2)}, u32[]{:S(2)}) collective-permute-start(bf16[16,1024]{1,0:T(8,128)(2,1)S(1)} %get-tuple-element.18), channel_id=1, source_target_pairs={{0,16},{8,24},{16,0},{24,8},{32,48},{40,56},{48,32},{56,40},{64,80... | collective-permute-start | bytes 98312 | tf_op jit(solution)/shard_map/ppermute | solution.py:23
  3.0 6.2 %collective-permute-start.1 = (bf16[16,1024]{1,0:T(8,128)(2,1)S(1)}, bf16[16,1024]{1,0:T(8,128)(2,1)S(1)}, u32[]{:S(2)}, u32[]{:S(2)}) collective-permute-start(bf16[16,1024]{1,0:T(8,128)(2,1)S(1)} %get-tuple-element.19), channel_id=1, source_target_pairs={{0,128},{8,136},{16,144},{24,152},{32,160},{40,168},{48,176},{56,1... | collective-permute-start | bytes 98312 | tf_op jit(solution)/shard_map/ppermute | solution.py:23
  3.0 6.2 %collective-permute-start.2 = (bf16[16,1024]{1,0:T(8,128)(2,1)S(1)}, bf16[16,1024]{1,0:T(8,128)(2,1)S(1)}, u32[]{:S(2)}, u32[]{:S(2)}) collective-permute-start(bf16[16,1024]{1,0:T(8,128)(2,1)S(1)} %get-tuple-element.20), channel_id=1, source_target_pairs={{0,144},{8,152},{16,128},{24,136},{32,176},{40,184},{48,160},{56,1... | collective-permute-start | bytes 98312 | tf_op jit(solution)/shard_map/ppermute | solution.py:23
  9.0 28.5 %collective-permute-start.8 = (bf16[128,1792]{1,0:T(8,128)(2,1)S(1)}, bf16[128,1792]{1,0:T(8,128)(2,1)S(1)}, u32[]{:S(2)}, u32[]{:S(2)}) collective-permute-start(bf16[128,1792]{1,0:T(8,128)(2,1)S(1)} %get-tuple-element.21.refs_4_.refs_5_), channel_id=1, source_target_pairs={{0,128},{8,136},{16,144},{24,152},{32,160},{40,168},{48,176},{56,1... | collective-permute-start | bytes 1376264 | tf_op jit(solution)/shard_map/ppermute | solution.py:23
  9.2 19.7 %collective-permute-start.3 = (bf16[4,16,1024]{2,1,0:T(8,128)(2,1)S(1)}, bf16[4,16,1024]{2,1,0:T(8,128)(2,1)S(1)}, u32[]{:S(2)}, u32[]{:S(2)}) collective-permute-start(bf16[4,16,1024]{2,1,0:T(8,128)(2,1)S(1)} %get-tuple-element.36), channel_id=1, source_target_pairs={{0,1},{1,0},{2,3},{3,2},{4,5},{5,4},{6,7},{7,6},{8,9},{9,8},{10,11... | collective-permute-start | bytes 393224 | tf_op jit(solution)/shard_map/ppermute | solution.py:23
  29.0 12.5 %collective-permute-start.6 = (bf16[2,4,16,1024]{3,2,1,0:T(8,128)(2,1)S(1)}, bf16[2,4,16,1024]{3,2,1,0:T(8,128)(2,1)S(1)}, u32[]{:S(2)}, u32[]{:S(2)}) collective-permute-start(bf16[2,4,16,1024]{3,2,1,0:T(8,128)(2,1)S(1)} %pad_maximum_fusion.refs_0_.refs_1_), channel_id=1, source_target_pairs={{0,6},{1,7},{2,4},{3,5},{4,2},{5,3},{6,0},{7,1},{8,14},{9,15},{10,... | collective-permute-start | bytes 786440 | tf_op jit(solution)/shard_map/ppermute | solution.py:23
  31.5 18.3 %collective-permute-start.11 = (bf16[1792,128]{1,0:T(8,128)(2,1)S(1)}, bf16[1792,128]{1,0:T(8,128)(2,1)S(1)}, u32[]{:S(2)}, u32[]{:S(2)}) collective-permute-start(bf16[1792,128]{1,0:T(8,128)(2,1)S(1)} %copy-done.2), channel_id=1, source_target_pairs={{0,64},{8,72},{16,80},{24,88},{32,96},{40,104},{48,112},{56,120},{... | collective-permute-start | bytes 1376264 | tf_op jit(solution)/shard_map/ppermute | solution.py:23
  31.5 21.5 %collective-permute-start.7 = (bf16[128,1792]{1,0:T(8,128)(2,1)S(1)}, bf16[128,1792]{1,0:T(8,128)(2,1)S(1)}, u32[]{:S(2)}, u32[]{:S(2)}) collective-permute-start(bf16[128,1792]{1,0:T(8,128)(2,1)S(1)} %get-tuple-element.21.refs_4_.refs_5_), channel_id=1, source_target_pairs={{0,16},{8,24},{16,0},{24,8},{32,48},{40,56},{48,32},{56,40},{64,80... | collective-permute-start | bytes 1376264 | tf_op jit(solution)/shard_map/ppermute | solution.py:23
  37.4 15.6 %collective-permute-start.9 = (bf16[128,1792]{1,0:T(8,128)(2,1)S(1)}, bf16[128,1792]{1,0:T(8,128)(2,1)S(1)}, u32[]{:S(2)}, u32[]{:S(2)}) collective-permute-start(bf16[128,1792]{1,0:T(8,128)(2,1)S(1)} %collective-permute-done.8.refs_6_.refs_7_), channel_id=1, source_target_pairs={{0,16},{8,24},{16,0},{24,8},{32,48},{40,56},{48,32},{56,40},{64,80... | collective-permute-start | bytes 1376264 | tf_op jit(solution)/shard_map/ppermute | solution.py:23
  38.7 8.5 %collective-permute-start.5 = (bf16[2,4,16,1024]{3,2,1,0:T(8,128)(2,1)S(1)}, bf16[2,4,16,1024]{3,2,1,0:T(8,128)(2,1)S(1)}, u32[]{:S(2)}, u32[]{:S(2)}) collective-permute-start(bf16[2,4,16,1024]{3,2,1,0:T(8,128)(2,1)S(1)} %pad_maximum_fusion.refs_0_.refs_1_), channel_id=1, source_target_pairs={{0,4},{1,5},{2,6},{3,7},{4,0},{5,1},{6,2},{7,3},{8,12},{9,13},{10,... | collective-permute-start | bytes 786440 | tf_op jit(solution)/shard_map/ppermute | solution.py:23
  42.2 10.9 %collective-permute-start.4 = (bf16[2,4,16,1024]{3,2,1,0:T(8,128)(2,1)S(1)}, bf16[2,4,16,1024]{3,2,1,0:T(8,128)(2,1)}, u32[]{:S(2)}, u32[]{:S(2)}) collective-permute-start(bf16[2,4,16,1024]{3,2,1,0:T(8,128)(2,1)S(1)} %pad_maximum_fusion.refs_0_.refs_1_), channel_id=1, source_target_pairs={{0,2},{1,3},{2,0},{3,1},{4,6},{5,7},{6,4},{7,5},{8,10},{9,11},{10,... | collective-permute-start | bytes 786440 | tf_op jit(solution)/shard_map/ppermute | solution.py:23
  47.9 14.3 %collective-permute-start.10 = (bf16[1792,128]{1,0:T(8,128)(2,1)S(1)}, bf16[1792,128]{1,0:T(8,128)(2,1)}, u32[]{:S(2)}, u32[]{:S(2)}) collective-permute-start(bf16[1792,128]{1,0:T(8,128)(2,1)S(1)} %copy-done.2), channel_id=1, source_target_pairs={{0,48},{8,56},{16,32},{24,40},{32,16},{40,24},{48,0},{56,8},{64,11... | collective-permute-start | bytes 1376264 | tf_op jit(solution)/shard_map/ppermute | solution.py:23
  49.8 18.2 %collective-permute-start.12 = (bf16[1792,128]{1,0:T(8,128)(2,1)S(1)}, bf16[1792,128]{1,0:T(8,128)(2,1)}, u32[]{:S(2)}, u32[]{:S(2)}) collective-permute-start(bf16[1792,128]{1,0:T(8,128)(2,1)S(1)} %collective-permute-done.11.refs_10_), channel_id=1, source_target_pairs={{0,48},{8,56},{16,32},{24,40},{32,16},{40,24},{48,0},{56,8},{64,11... | collective-permute-start | bytes 1376264 | tf_op jit(solution)/shard_map/ppermute | solution.py:23
  54.9 18.7 %copy-start.5 = (bf16[2,4,16,1024]{3,2,1,0:T(8,128)(2,1)S(1)}, bf16[2,4,16,1024]{3,2,1,0:T(8,128)(2,1)}, u32[]{:S(2)}) copy-start(bf16[2,4,16,1024]{3,2,1,0:T(8,128)(2,1)} %copy-done.3) | copy-start | bytes 786436
  54.9 18.7 %copy-start.8 = (bf16[2,4,16,1024]{3,2,1,0:T(8,128)(2,1)S(1)}, bf16[2,4,16,1024]{3,2,1,0:T(8,128)(2,1)}, u32[]{:S(2)}) copy-start(bf16[2,4,16,1024]{3,2,1,0:T(8,128)(2,1)} %copy-done.6) | copy-start | bytes 786436
  59.9 43.5 %collective-permute-start.24 = (bf16[4,1792,128]{2,1,0:T(8,128)(2,1)S(1)}, bf16[4,1792,128]{2,1,0:T(8,128)(2,1)S(1)}, u32[]{:S(2)}, u32[]{:S(2)}) collective-permute-start(bf16[4,1792,128]{2,1,0:T(8,128)(2,1)S(1)} %get-tuple-element.27), channel_id=1, source_target_pairs={{0,8},{8,0},{16,24},{24,16},{32,40},{40,32},{48,56},{56,48},{64,72... | collective-permute-start | bytes 5505032 | tf_op jit(solution)/shard_map/ppermute | solution.py:23
  61.7 10.3 %collective-permute-start.13 = (bf16[1792,128]{1,0:T(8,128)(2,1)S(1)}, bf16[1792,128]{1,0:T(8,128)(2,1)S(1)}, u32[]{:S(2)}, u32[]{:S(2)}) collective-permute-start(bf16[1792,128]{1,0:T(8,128)(2,1)S(1)} %copy-done.2), channel_id=1, source_target_pairs={{0,8},{8,0},{16,24},{24,16},{32,40},{40,32},{48,56},{56,48},{64,72... | collective-permute-start | bytes 1376264 | tf_op jit(solution)/shard_map/ppermute | solution.py:23
  61.8 10.2 %collective-permute-start.15 = (bf16[1792,128]{1,0:T(8,128)(2,1)S(1)}, bf16[1792,128]{1,0:T(8,128)(2,1)S(1)}, u32[]{:S(2)}, u32[]{:S(2)}) collective-permute-start(bf16[1792,128]{1,0:T(8,128)(2,1)S(1)} %collective-permute-done.11.refs_10_), channel_id=1, source_target_pairs={{0,8},{8,0},{16,24},{24,16},{32,40},{40,32},{48,56},{56,48},{64,72... | collective-permute-start | bytes 1376264 | tf_op jit(solution)/shard_map/ppermute | solution.py:23
  62.2 9.8 %collective-permute-start.14 = (bf16[1792,128]{1,0:T(8,128)(2,1)}, bf16[1792,128]{1,0:T(8,128)(2,1)S(1)}, u32[]{:S(2)}, u32[]{:S(2)}) collective-permute-start(bf16[1792,128]{1,0:T(8,128)(2,1)} %collective-permute-done.10.refs_9_), channel_id=1, source_target_pairs={{0,8},{8,0},{16,24},{24,16},{32,40},{40,32},{48,56},{56,48},{64,72... | collective-permute-start | bytes 1376264 | tf_op jit(solution)/shard_map/ppermute | solution.py:23
  68.0 5.6 %collective-permute-start.16 = (bf16[1792,128]{1,0:T(8,128)(2,1)}, bf16[1792,128]{1,0:T(8,128)(2,1)S(1)}, u32[]{:S(2)}, u32[]{:S(2)}) collective-permute-start(bf16[1792,128]{1,0:T(8,128)(2,1)} %collective-permute-done.12.refs_11_), channel_id=1, source_target_pairs={{0,8},{8,0},{16,24},{24,16},{32,40},{40,32},{48,56},{56,48},{64,72... | collective-permute-start | bytes 1376264 | tf_op jit(solution)/shard_map/ppermute | solution.py:23
  82.1 7.6 %collective-permute-start.17 = (bf16[2,4,16,1024]{3,2,1,0:T(8,128)(2,1)S(1)}, bf16[2,4,16,1024]{3,2,1,0:T(8,128)(2,1)S(1)}, u32[]{:S(2)}, u32[]{:S(2)}) collective-permute-start(bf16[2,4,16,1024]{3,2,1,0:T(8,128)(2,1)S(1)} %get-tuple-element.23), channel_id=1, source_target_pairs={{0,2},{1,3},{2,0},{3,1},{4,6},{5,7},{6,4},{7,5},{8,10},{9,11},{10,... | collective-permute-start | bytes 786440 | tf_op jit(solution)/shard_map/ppermute | solution.py:23
  83.3 14.1 %collective-permute-start.18 = (bf16[2,4,16,1024]{3,2,1,0:T(8,128)(2,1)S(1)}, bf16[2,4,16,1024]{3,2,1,0:T(8,128)(2,1)S(1)}, u32[]{:S(2)}, u32[]{:S(2)}) collective-permute-start(bf16[2,4,16,1024]{3,2,1,0:T(8,128)(2,1)S(1)} %get-tuple-element.24), channel_id=1, source_target_pairs={{0,4},{1,5},{2,6},{3,7},{4,0},{5,1},{6,2},{7,3},{8,12},{9,13},{10,... | collective-permute-start | bytes 786440 | tf_op jit(solution)/shard_map/ppermute | solution.py:23
  85.8 13.7 %collective-permute-start.19 = (bf16[2,4,16,1024]{3,2,1,0:T(8,128)(2,1)S(1)}, bf16[2,4,16,1024]{3,2,1,0:T(8,128)(2,1)S(1)}, u32[]{:S(2)}, u32[]{:S(2)}) collective-permute-start(bf16[2,4,16,1024]{3,2,1,0:T(8,128)(2,1)S(1)} %get-tuple-element.25), channel_id=1, source_target_pairs={{0,6},{1,7},{2,4},{3,5},{4,2},{5,3},{6,0},{7,1},{8,14},{9,15},{10,... | collective-permute-start | bytes 786440 | tf_op jit(solution)/shard_map/ppermute | solution.py:23
  86.0 30.3 %collective-permute-start.27 = (bf16[2,128,1792]{2,1,0:T(8,128)(2,1)S(1)}, bf16[2,128,1792]{2,1,0:T(8,128)(2,1)S(1)}, u32[]{:S(2)}, u32[]{:S(2)}) collective-permute-start(bf16[2,128,1792]{2,1,0:T(8,128)(2,1)S(1)} %get-tuple-element.30), channel_id=1, source_target_pairs={{0,16},{8,24},{16,0},{24,8},{32,48},{40,56},{48,32},{56,40},{64,80... | collective-permute-start | bytes 2752520 | tf_op jit(solution)/shard_map/ppermute | solution.py:23
  99.7 10.6 %collective-permute-start.20 = (bf16[4,16,1024]{2,1,0:T(8,128)(2,1)S(1)}, bf16[4,16,1024]{2,1,0:T(8,128)(2,1)S(1)}, u32[]{:S(2)}, u32[]{:S(2)}) collective-permute-start(bf16[4,16,1024]{2,1,0:T(8,128)(2,1)S(1)} %fusion.7), channel_id=1, source_target_pairs={{0,1},{1,0},{2,3},{3,2},{4,5},{5,4},{6,7},{7,6},{8,9},{9,8},{10,11... | collective-permute-start | bytes 393224 | tf_op jit(solution)/shard_map/ppermute | solution.py:23
  103.6 21.0 %collective-permute-start.25 = (bf16[2,1792,128]{2,1,0:T(8,128)(2,1)S(1)}, bf16[2,1792,128]{2,1,0:T(8,128)(2,1)S(1)}, u32[]{:S(2)}, u32[]{:S(2)}) collective-permute-start(bf16[2,1792,128]{2,1,0:T(8,128)(2,1)S(1)} %add_convert_fusion), channel_id=1, source_target_pairs={{0,48},{8,56},{16,32},{24,40},{32,16},{40,24},{48,0},{56,8},{64,11... | collective-permute-start | bytes 2752520 | tf_op jit(solution)/shard_map/ppermute | solution.py:23
  110.3 4.7 %collective-permute-start.23 = (bf16[16,1024]{1,0:T(8,128)(2,1)S(1)}, bf16[16,1024]{1,0:T(8,128)(2,1)S(1)}, u32[]{:S(2)}, u32[]{:S(2)}) collective-permute-start(bf16[16,1024]{1,0:T(8,128)(2,1)S(1)} %get-tuple-element.31), channel_id=1, source_target_pairs={{0,144},{8,152},{16,128},{24,136},{32,176},{40,184},{48,160},{56,1... | collective-permute-start | bytes 98312 | tf_op jit(solution)/shard_map/ppermute | solution.py:23
  110.4 4.6 %collective-permute-start.22 = (bf16[16,1024]{1,0:T(8,128)(2,1)S(1)}, bf16[16,1024]{1,0:T(8,128)(2,1)S(1)}, u32[]{:S(2)}, u32[]{:S(2)}) collective-permute-start(bf16[16,1024]{1,0:T(8,128)(2,1)S(1)} %get-tuple-element.32), channel_id=1, source_target_pairs={{0,128},{8,136},{16,144},{24,152},{32,160},{40,168},{48,176},{56,1... | collective-permute-start | bytes 98312 | tf_op jit(solution)/shard_map/ppermute | solution.py:23
  112.1 3.5 %collective-permute-start.21 = (bf16[16,1024]{1,0:T(8,128)(2,1)S(1)}, bf16[16,1024]{1,0:T(8,128)(2,1)S(1)}, u32[]{:S(2)}, u32[]{:S(2)}) collective-permute-start(bf16[16,1024]{1,0:T(8,128)(2,1)S(1)} %get-tuple-element.33), channel_id=1, source_target_pairs={{0,16},{8,24},{16,0},{24,8},{32,48},{40,56},{48,32},{56,40},{64,80... | collective-permute-start | bytes 98312 | tf_op jit(solution)/shard_map/ppermute | solution.py:23
  116.4 18.0 %collective-permute-start.28 = (bf16[128,1792]{1,0:T(8,128)(2,1)S(1)}, bf16[128,1792]{1,0:T(8,128)(2,1)S(1)}, u32[]{:S(2)}, u32[]{:S(2)}) collective-permute-start(bf16[128,1792]{1,0:T(8,128)(2,1)S(1)} %fusion.4), channel_id=1, source_target_pairs={{0,128},{8,136},{16,144},{24,152},{32,160},{40,168},{48,176},{56,1... | collective-permute-start | bytes 1376264 | tf_op jit(solution)/shard_map/ppermute | solution.py:23
  124.8 21.0 %collective-permute-start.26 = (bf16[1792,128]{1,0:T(8,128)(2,1)S(1)}, bf16[1792,128]{1,0:T(8,128)(2,1)S(1)}, u32[]{:S(2)}, u32[]{:S(2)}) collective-permute-start(bf16[1792,128]{1,0:T(8,128)(2,1)S(1)} %fusion.3), channel_id=1, source_target_pairs={{0,64},{8,72},{16,80},{24,88},{32,96},{40,104},{48,112},{56,120},{... | collective-permute-start | bytes 1376264 | tf_op jit(solution)/shard_map/ppermute | solution.py:23
  (6 other events, 5.2 us)

commit v2 on v0

v2 whole, which is shorter than its diff:
```python
import math

import jax
import jax.numpy as jnp
from jax import lax
from jax.experimental import pallas as pl
from jax.experimental.pallas import tpu as pltpu
from jax.sharding import PartitionSpec as P

BF16 = jnp.bfloat16
F32 = jnp.float32

CORE = 1
ROWS_Y, ROWS_Z = 2, 16
COLS_Y, COLS_Z = 6, 8
TOKEN_PARTS = (0, ROWS_Y, ROWS_Z, ROWS_Y ^ ROWS_Z)
COLUMN_PARTS = (0, COLS_Y, COLS_Z, COLS_Y ^ COLS_Z)
COLUMN_BLOCKS = COLUMN_PARTS + tuple(k ^ CORE for k in COLUMN_PARTS)
STEP = 256
COST = 1
EARLY = 64


def swap(array, axis, size, k):
    return lax.ppermute(array, axis, [(i, i ^ k) for i in range(size)])


def dp_swap(array, k):
    return swap(array, "dp", 32, k)


def mp_swap(array, k):
    return swap(array, "mp", 8, k)


def place(axis):
    return jnp.reshape(lax.axis_index(axis).astype(jnp.int32), (1,))


def in_smem():
    return pl.BlockSpec(memory_space=pltpu.SMEM)


def whole():
    return pl.BlockSpec(memory_space=pltpu.VMEM)


def call(kernel, out_shape, scratch=(), grid=None, in_specs=None, out_specs=None, flops=0, moved=0, limit=16 * 2**20):
    return pl.pallas_call(
        kernel,
        out_shape=out_shape,
        grid=grid or (),
        in_specs=in_specs,
        out_specs=out_specs,
        scratch_shapes=list(scratch),
        compiler_params=pltpu.CompilerParams(vmem_limit_bytes=limit),
        cost_estimate=pl.CostEstimate(flops=flops, bytes_accessed=moved, transcendentals=0),
    )


def mask_kernel(pre_in, code_in, hidden_ref, slope_ref, pre_ref, code_ref, sems):
    copies = [
        pltpu.make_async_copy(pre_in, pre_ref, sems.at[0]),
        pltpu.make_async_copy(code_in, code_ref, sems.at[1]),
    ]
    for copy in copies:
        copy.start()
    for copy in copies:
        copy.wait()
    groups = code_ref.shape[0]
    for at in range(0, groups, 128):
        size = min(128, groups - at)
        spread = (
            lax.broadcasted_iota(jnp.int32, (size, 4 * size), 1) // 4
            == lax.broadcasted_iota(jnp.int32, (size, 4 * size), 0)
        ).astype(BF16)
        codes = code_ref[at : at + size, :].astype(F32).astype(BF16)
        code = lax.dot_general(
            codes, spread, (((0,), (0,)), ((), ())), preferred_element_type=F32
        )
        lane = lax.broadcasted_iota(jnp.int32, code.shape, 1) % 4
        kept = (
            ((lane == 0) & (code < 2.5))
            | ((lane == 1) & ((code == 0.0) | (code == 3.0) | (code == 4.0)))
            | ((lane == 2) & ((code == 1.0) | (code == 3.0) | (code == 5.0)))
            | ((lane == 3) & ((code == 2.0) | (code > 3.5)))
        )
        columns = slice(4 * at, 4 * (at + size))
        positive = jnp.where(kept, jnp.maximum(pre_ref[:, columns].astype(F32), 0.0), 0.0)
        hidden_ref[:, columns] = (positive * positive).astype(BF16)
        slope_ref[:, columns] = (2.0 * positive).astype(BF16)


def first_kernel(place_ref, grad_ref, grad_far, hidden_ref, weight_ref, *refs):
    part_refs, half_ref, weight_out = refs[-6:-2], refs[-2], refs[-1]
    me = place_ref[0]
    for out_ref, token in zip(part_refs, TOKEN_PARTS):
        for n, column in enumerate(COLUMN_BLOCKS):
            at = pl.ds(pl.multiple_of((me ^ (token ^ column)) * 128, 128), 128)
            out_ref[0, :, n * 128 : (n + 1) * 128] = grad_ref[:, at]
            out_ref[1, :, n * 128 : (n + 1) * 128] = grad_far[:, at]
    half_ref[...] = hidden_ref[: half_ref.shape[0]]
    weight_out[...] = weight_ref[...]


def second_kernel(*refs):
    part_refs, hidden_ref, weight_z = refs[:4], refs[4], refs[5]
    near_ref, far_ref, half_ref, hidden_out, weight_out = refs[-5:]
    for n, ref in enumerate(part_refs):
        near_ref[n] = ref[0]
        far_ref[n] = ref[1]
    half_ref[...] = hidden_ref[half_ref.shape[0] :]
    hidden_out[...] = hidden_ref[...]
    weight_out[...] = weight_z[...]


def third_kernel(near_ref, near_x, far_ref, far_x, z0_ref, z1_ref, *refs):
    weight_refs = refs[:4]
    near_out, far_out, hidden_z, weights = refs[-4:]
    near_out[0] = near_ref[...]
    near_out[1] = near_x[...]
    far_out[0] = far_ref[...]
    far_out[1] = far_x[...]
    hidden_z[:64] = z0_ref[...]
    hidden_z[64:] = z1_ref[...]
    for n, ref in enumerate(weight_refs):
        weights[n] = ref[...]


def gather_rows(me, grad_refs, rows_ref):
    near_two, near_rest, far_two, far_rest = grad_refs
    for k in range(4):
        for rx, ref in enumerate((near_two.at[0], near_two.at[1], near_rest.at[1], near_rest.at[0])):
            rows_ref[part_at(me, rx, 0, k), :] = ref[k]
        for rx, ref in enumerate((far_two.at[0], far_rest.at[0], far_rest.at[1], far_two.at[1])):
            rows_ref[part_at(me, rx, 1, k), :] = ref[k]


def part_at(me, rx, rz, k):
    return pl.ds(pl.multiple_of(k * 128 + (me ^ (2 * rx + rz)) * 16, 16), 16)


def steps(width, body):
    for at in range(0, width, STEP):
        body(slice(at, at + STEP))


def output_kernel(place_ref, *refs):
    hidden_refs, (mine_ref, far_ref) = refs[:4], refs[4:6]
    first0, first3, first_send, second0, second1, second_send, rows_ref = refs[6:]
    hidden = jnp.concatenate([ref[...] for ref in hidden_refs], axis=0)
    for n in range(4):
        ref = (mine_ref, far_ref)[n // 2]
        weight = jnp.concatenate([ref[2 * n % 4], ref[2 * n % 4 + 1]], axis=1)
        total = jnp.dot(hidden, weight, preferred_element_type=F32).astype(BF16)
        rows_ref[:, 256 * n : 256 * (n + 1)] = total
    me = place_ref[0]
    for k in range(4):
        for rx, ref in enumerate((first0, first_send.at[0], first_send.at[1], first3)):
            ref[k] = rows_ref[part_at(me, rx, 0, k), :]
        for rx, ref in enumerate((second0, second1, second_send.at[1], second_send.at[0])):
            ref[k] = rows_ref[part_at(me, rx, 1, k), :]


def weight_grad_kernel(scale, place_ref, *refs):
    grad_refs, hidden_refs, (near_ref, away_ref, rows_ref) = refs[:4], refs[4:8], refs[-3:]
    gather_rows(place_ref[0], grad_refs, rows_ref)

    def body(at):
        hidden = jnp.concatenate([ref[:, at] for ref in hidden_refs], axis=0)
        product = lax.dot_general(
            hidden, rows_ref[...], (((0,), (0,)), ((), ())), preferred_element_type=F32
        )
        product = (product * scale).astype(BF16)
        for n in range(4):
            near_ref[n, at, :] = product[:, n * 128 : (n + 1) * 128]
            away_ref[n, at, :] = product[:, (n + 4) * 128 : (n + 5) * 128]

    steps(near_ref.shape[1], body)


def back_kernel(rows_ref, mine_ref, far_ref, *refs):
    near_ref, half0_ref, half1_ref = refs[-3:]
    middle = half0_ref.shape[1]

    def body(at):
        weight = jnp.concatenate([ref[n, at, :] for ref in (mine_ref, far_ref) for n in range(4)], axis=1)
        back = lax.dot_general(
            rows_ref[...], weight, (((1,), (1,)), ((), ())), preferred_element_type=F32
        ).astype(BF16)
        for n in range(2):
            near_ref[n, :, at] = back[256 * n : 256 * n + 128]
            half0_ref[n, :, at] = back[256 * n + 128 : 256 * n + 128 + middle]
            half1_ref[n, :, at] = back[256 * n + 128 + middle : 256 * n + 256]

    steps(mine_ref.shape[1], body)


def added(*arrays):
    total = arrays[0].astype(F32)
    for array in arrays[1:]:
        total = total + array.astype(F32)
    return total


def y_kernel(near_ref, far_ref, half0_ref, *refs):
    first0, first3, first_far, second0, second1, second_far = refs[:6]
    send0_ref, send1_ref, sum_ref, half0_out, first_sum, first_send, second_sum, second_send = refs[6:]
    half0_out[...] = half0_ref[...]
    first_sum[...] = added(first0[...], first_far[0])
    first_send[...] = added(first3[...], first_far[1]).astype(BF16)
    second_sum[...] = added(second0[...], second_far[0])
    second_send[...] = added(second1[...], second_far[1]).astype(BF16)
    middle = send0_ref.shape[1]
    for n in range(2):
        send = added(near_ref[2 * n + 1], far_ref[2 * n + 1]).astype(BF16)
        send0_ref[n] = send[:middle]
        send1_ref[n] = send[middle:]
        sum_ref[n] = added(near_ref[2 * n], far_ref[2 * n])


def z0_kernel(sum_ref, far0_ref, back_ref, back0_ref, first_ref, first_far, second_ref, *refs):
    weight1_ref, back1_ref = refs[:2]
    weight_out, back_out, weight1_out, back1_out, total_ref, send_ref = refs[2:]
    middle = far0_ref.shape[1]
    weight_out[...] = added(sum_ref[1, :middle], far0_ref[1]).astype(BF16)
    back_out[...] = added(back_ref[1, : back0_ref.shape[1]], back0_ref[1]).astype(BF16)
    weight1_out[...] = weight1_ref[...]
    back1_out[...] = back1_ref[...]
    total = added(first_ref[...], first_far[...], second_ref[...]).astype(BF16)
    total_ref[...] = total
    send_ref[0] = total[1]
    send_ref[1] = total[3]


def z1_kernel(sum_ref, far1_ref, back_ref, back1_ref, total_ref, arrived_ref, *refs):
    weight_out, back_out, send_ref = refs[-3:]
    middle = sum_ref.shape[1] - far1_ref.shape[1]
    weight_out[...] = added(sum_ref[1, middle:], far1_ref[1]).astype(BF16)
    middle = back_ref.shape[1] - back1_ref.shape[1]
    back_out[...] = added(back_ref[1, middle:], back1_ref[1]).astype(BF16)
    send_ref[0] = total_ref[2]
    send_ref[1] = arrived_ref[1]


def last_kernel(place_ref, *refs):
    sum_ref, far0, far1, z0, z1, back_ref, back0, back1, backz0, backz1, slope_ref = refs[:11]
    total_ref, arrived_y, arrived_z, weight_out, input_out, output_ref = refs[11:]
    middle = far0.shape[1]
    for at, far, last in ((slice(0, middle), far0, z0), (slice(middle, None), far1, z1)):
        weight_out[at] = added(sum_ref[0, at], far[0], last[...]).astype(BF16)
    middle = back0.shape[1]
    for at, far, last in ((slice(0, middle), back0, backz0), (slice(middle, None), back1, backz1)):
        back = added(back_ref[0, at], far[0], last[...])
        input_out[at] = (slope_ref[at].astype(F32) * back).astype(BF16)
    me = place_ref[0]
    parts = (total_ref.at[0], arrived_y.at[0], arrived_z.at[0], arrived_z.at[1])
    for part_ref, token in zip(parts, TOKEN_PARTS):
        for n, column in enumerate(COLUMN_BLOCKS):
            at = pl.multiple_of((me ^ (token ^ column)) * 128, 128)
            output_ref[:, pl.ds(at, 128)] = part_ref[:, n * 128 : (n + 1) * 128]


def move(kernel, out_shape, *arrays, scratch=(), flops=COST):
    return call(
        kernel,
        out_shape,
        in_specs=[in_smem() if a.dtype == jnp.int32 and a.size == 1 else whole() for a in arrays],
        out_specs=[whole()] * len(out_shape),
        scratch=scratch,
        flops=flops,
        moved=COST,
    )(*arrays)


def on_device(preactivation, keep_codes, down_weight, output_grad):
    rows, width = preactivation.shape
    scale = 1.0 / math.sqrt(rows * lax.axis_size("dp"))
    dp_place, mp_place = place("dp"), place("mp")

    def shape(*sizes):
        return jax.ShapeDtypeStruct(sizes, BF16)

    def wide(*sizes):
        return jax.ShapeDtypeStruct(sizes, F32)

    piece, half, column = shape(rows, width), shape(rows // 2, width), shape(width, 128)
    part, pair = shape(4, 16, 1024), shape(2, 4, 16, 1024)
    early = width * EARLY // rows
    split0, split1 = shape(2, early, 128), shape(2, width - early, 128)
    rows_scratch = [pltpu.VMEM((512, 1024), BF16)]

    grad_far = mp_swap(output_grad, 1)
    codes = keep_codes.T
    hidden, slope = call(
        mask_kernel,
        [piece, piece],
        in_specs=[pl.BlockSpec(memory_space=pl.ANY)] * 2,
        out_specs=[whole()] * 2,
        scratch=[
            pltpu.VMEM(preactivation.shape, BF16),
            pltpu.VMEM(codes.shape, jnp.int32),
            pltpu.SemaphoreType.DMA((2,)),
        ],
        flops=10**11,
    )(preactivation, codes)
    outs = move(
        first_kernel,
        [shape(2, 16, 1024)] * 4 + [half, column],
        dp_place,
        output_grad,
        grad_far,
        hidden,
        down_weight,
    )
    parts, half_out, weight_out = outs[:4], outs[4], outs[5]

    parts = [parts[0]] + [dp_swap(p, k) for p, k in zip(parts[1:], TOKEN_PARTS[1:])]
    weight_z = dp_swap(weight_out, COLS_Z)
    weight_y = dp_swap(weight_out, COLS_Y)
    hidden_z0 = dp_swap(half_out, ROWS_Z)
    near, far, half_out, hidden_out, weight_out = move(
        second_kernel, [part, part, half, piece, column], *parts, hidden, weight_z, hidden_z0, weight_y
    )

    near_x = mp_swap(near, 2)
    far_x = mp_swap(far, 6)
    hidden_z1 = dp_swap(half_out, ROWS_Z)
    hidden_y = dp_swap(hidden_out, ROWS_Y)
    weight_yz = dp_swap(weight_out, COLS_Y)
    near_two, far_two, hidden_z, weights = move(
        third_kernel,
        [pair, pair, piece, shape(4, width, 128)],
        near,
        near_x,
        far,
        far_x,
        hidden_z0,
        hidden_z1,
        down_weight,
        weight_y,
        weight_z,
        weight_yz,
        hidden_y,
    )

    near_rest = mp_swap(near_two, 6)
    far_rest = mp_swap(far_two, 2)
    hidden_yz = dp_swap(hidden_z, ROWS_Y)
    weights_far = dp_swap(weights, CORE)
    grads = [near_two, near_rest, far_two, far_rest]
    hiddens = [hidden, hidden_y, hidden_z, hidden_yz]

    first0, first3, first_send, second0, second1, second_send = move(
        output_kernel,
        [part, part, pair, part, part, pair],
        mp_place,
        *hiddens,
        weights,
        weights_far,
        scratch=rows_scratch,
    )
    first_far = mp_swap(first_send, 2)
    second_far = mp_swap(second_send, 6)
    near, away, grad_rows = move(
        lambda *refs: weight_grad_kernel(scale, *refs),
        [shape(4, width, 128)] * 2 + [shape(512, 1024)],
        mp_place,
        *grads,
        *hiddens,
        first0,
        flops=5 * 10**9,
    )
    away = dp_swap(away, CORE)
    back_near, half0, half1 = move(
        back_kernel,
        [shape(2, rows, width), shape(2, EARLY, width), shape(2, rows - EARLY, width)],
        grad_rows,
        weights,
        weights_far,
        flops=5 * 10**9,
    )

    send0, send1, sums, half0, first, first_send, second, second_send = move(
        y_kernel,
        [split0, split1, wide(2, width, 128), shape(2, EARLY, width)]
        + [wide(4, 16, 1024), part] * 2,
        near,
        away,
        half0,
        first0,
        first3,
        first_far,
        second0,
        second1,
        second_far,
    )
    far0 = dp_swap(send0, COLS_Y)
    back0 = dp_swap(half0, ROWS_Y)
    first_far = mp_swap(first_send, 6)
    second = mp_swap(added(second, mp_swap(second_send, 2)).astype(BF16), 1)

    weight_z0, back_z0, send1, half1, total, total_send = move(
        z0_kernel,
        [
            shape(early, 128),
            shape(EARLY, width),
            split1,
            shape(2, rows - EARLY, width),
            part,
            shape(2, 16, 1024),
        ],
        sums,
        far0,
        back_near,
        back0,
        first,
        first_far,
        second,
        send1,
        half1,
    )
    weight_z0 = dp_swap(weight_z0, COLS_Z)
    back_z0 = dp_swap(back_z0, ROWS_Z)
    far1 = dp_swap(send1, COLS_Y)
    back1 = dp_swap(half1, ROWS_Y)
    arrived_y = dp_swap(total_send, ROWS_Y)

    weight_z1, back_z1, total_send = move(
        z1_kernel,
        [shape(width - early, 128), shape(rows - EARLY, width), shape(2, 16, 1024)],
        sums,
        far1,
        back_near,
        back1,
        total,
        arrived_y,
        weight_z0,
        back_z0,
    )
    weight_z1 = dp_swap(weight_z1, COLS_Z)
    back_z1 = dp_swap(back_z1, ROWS_Z)
    arrived_z = dp_swap(total_send, ROWS_Z)
    weight_grad, input_grad, output = move(
        last_kernel,
        [column, piece, shape(16, 4096)],
        dp_place,
        sums,
        far0,
        far1,
        weight_z0,
        weight_z1,
        back_near,
        back0,
        back1,
        back_z0,
        back_z1,
        slope,
        total,
        arrived_y,
        arrived_z,
    )
    return (output, weight_grad, input_grad)


def solution(mesh):
    in_specs = (P("dp", "mp"), P("dp", "mp"), P("mp", "dp"), P(("dp", "mp"), None))
    out_specs = (P(("dp", "mp"), None), P("mp", "dp"), P("dp", "mp"))
    return jax.shard_map(
        on_device, mesh=mesh, in_specs=in_specs, out_specs=out_specs, check_vma=False
    )
```

time: 391 us -> 129 us (0.33)
  waiting for transfers between devices: 297 us -> 55.3 us
  starting transfers between devices: 0.16 us -> 54.6 us
  blocking collectives: 39.2 us -> 0 us
  matrix products: 30.3 us -> 0 us
  Pallas kernels: 0 us -> 16.4 us
  between operations: 14 us -> 0.81 us
  local copies, waits for them, and re-layouts: 6.8 us -> 1.97 us
    all_gather x3 -> x0, waiting for transfers between devices: 213 us -> none  [the longest x1 85.4 us: on_device(): piece = lax.all_gather(down_weight, 'dp', axis=1, tiled=True)]
    reduce_scatter x1 -> x0, waiting for transfers between devices: 81.8 us -> none  [on_device(): lax.psum_scatter(columns.astype(jnp.bfloat16), 'mp', scatter_dimension=0,...]
    ppermute x0 -> x32, waiting for transfers between devices: none -> 55.3 us  [swap(): return lax.ppermute(array, axis, [(i, i ^ k) for i in range(size)])]
    ppermute x0 -> x32, starting transfers between devices: none -> 54.6 us  [swap(): return lax.ppermute(array, axis, [(i, i ^ k) for i in range(size)])]
    all_to_all x1 -> x0, blocking collectives: 39.2 us -> none  [on_device(): lax.all_to_all(grad_group, 'dp', split_axis=1, concat_axis=0, tiled=True)]
    dot_general x3 -> x0, matrix products: 30.3 us -> none  [the longest x1 11.7 us: on_device(): lax.dot_general(grad_group, piece, (((1,), (1,)), ((), ())), preferred_el...]
    pallas_call x0 -> x11, Pallas kernels: none -> 16.4 us  [the longest x10 14.1 us: move(): call(kernel, out_shape, in_specs=[in_smem() if a.dtype == jnp.int32 and a...]
  transfers between devices with their start and end apart: 4 -> 32, of which waited for: 4 -> 14; matrix products, arithmetic and copies ran while one was open for 10% -> 0% of each run, Pallas kernels for 0% -> 7%
where the time goes in v2:
time: 129 us
  waiting for transfers between devices  55.3 us (43%)
  starting transfers between devices  54.6 us (42%)
  Pallas kernels  16.4 us (13%)
  local copies, waits for them, and re-layouts  1.97 us (2%)
    ppermute x32, waiting for transfers between devices, swap(): return lax.ppermute(array, axis, [(i, i ^ k) for i in range(size)])  55.3 us
    ppermute x32, starting transfers between devices, swap(): return lax.ppermute(array, axis, [(i, i ^ k) for i in range(size)])  54.6 us
    pallas_call x10, Pallas kernels, move(): call(kernel, out_shape, in_specs=[in_smem() if a.dtype == jnp.int32 and a...  14.1 us
  transfers between devices with their start and end apart: 32, of which 14 were waited for; matrix products, arithmetic and copies ran while one was open for 0% of the time, Pallas kernels for 7%

profile of v2, /device:TPU:8, one launch (start us, length us, event | category | flops | bytes accessed | tf_op | source)
XLA Modules:
  0.0 129.1 jit_solution(6923070290847367807)
XLA Ops:
  0.6 7.3 %collective-permute-start = (bf16[16,4096]{1,0:T(8,128)(2,1)}, bf16[16,4096]{1,0:T(8,128)(2,1)S(1)}, u32[]{:S(2)}, u32[]{:S(2)}) collective-permute-start(bf16[16,4096]{1,0:T(8,128)(2,1)} %grad_ref.1), channel_id=1, source_target_pairs={{0,1},{1,0},{2,3},{3,2},{4,5},{5,4},{6,7},{7,6},{8,9},{9,8},{10,11... | collective-permute-start | bytes 393224 | tf_op jit(solution)/shard_map/ppermute | solution.py:25
  9.9 2.2 %shard_map.67 = (bf16[128,1792]{1,0:T(8,128)(2,1)S(1)}, bf16[128,1792]{1,0:T(8,128)(2,1)S(1)}) custom-call(bf16[128,1792]{1,0:T(8,128)(2,1)S(1)} %copy-done.4, s32[448,128]{1,0:T(8,128)S(1)} %bitcast.3), custom_call_target="tpu_custom_call" | custom-call | flops 99999997952 | tf_op jit(solution)/shard_map/pallas_call | solution.py:295
  12.3 1.7 %collective-permute-start.6 = (bf16[1792,128]{1,0:T(8,128)(2,1)S(1)}, bf16[1792,128]{1,0:T(8,128)(2,1)S(1)}, u32[]{:S(2)}, u32[]{:S(2)}) collective-permute-start(bf16[1792,128]{1,0:T(8,128)(2,1)S(1)} %get-tuple-element.57), channel_id=1, source_target_pairs={{0,48},{8,56},{16,32},{24,40},{32,16},{40,24},{48,0},{56,8},{64,11... | collective-permute-start | bytes 1376264 | tf_op jit(solution)/shard_map/ppermute | solution.py:25
  14.0 3.3 %collective-permute-start.4 = (bf16[1792,128]{1,0:T(8,128)(2,1)S(1)}, bf16[1792,128]{1,0:T(8,128)(2,1)S(1)}, u32[]{:S(2)}, u32[]{:S(2)}) collective-permute-start(bf16[1792,128]{1,0:T(8,128)(2,1)S(1)} %get-tuple-element.57), channel_id=1, source_target_pairs={{0,64},{8,72},{16,80},{24,88},{32,96},{40,104},{48,112},{56,120},{... | collective-permute-start | bytes 1376264 | tf_op jit(solution)/shard_map/ppermute | solution.py:25
  18.1 1.9 %collective-permute-start.1 = (bf16[2,16,1024]{2,1,0:T(8,128)(2,1)S(1)}, bf16[2,16,1024]{2,1,0:T(8,128)(2,1)S(1)}, u32[]{:S(2)}, u32[]{:S(2)}) collective-permute-start(bf16[2,16,1024]{2,1,0:T(8,128)(2,1)S(1)} %get-tuple-element.54), channel_id=1, source_target_pairs={{0,16},{8,24},{16,0},{24,8},{32,48},{40,56},{48,32},{56,40},{64,80... | collective-permute-start | bytes 196616 | tf_op jit(solution)/shard_map/ppermute | solution.py:25
  20.0 2.1 %collective-permute-start.2 = (bf16[2,16,1024]{2,1,0:T(8,128)(2,1)S(1)}, bf16[2,16,1024]{2,1,0:T(8,128)(2,1)S(1)}, u32[]{:S(2)}, u32[]{:S(2)}) collective-permute-start(bf16[2,16,1024]{2,1,0:T(8,128)(2,1)S(1)} %get-tuple-element.55), channel_id=1, source_target_pairs={{0,128},{8,136},{16,144},{24,152},{32,160},{40,168},{48,176},{56,1... | collective-permute-start | bytes 196616 | tf_op jit(solution)/shard_map/ppermute | solution.py:25
  22.3 3.4 %collective-permute-start.3 = (bf16[2,16,1024]{2,1,0:T(8,128)(2,1)S(1)}, bf16[2,16,1024]{2,1,0:T(8,128)(2,1)S(1)}, u32[]{:S(2)}, u32[]{:S(2)}) collective-permute-start(bf16[2,16,1024]{2,1,0:T(8,128)(2,1)S(1)} %get-tuple-element.56), channel_id=1, source_target_pairs={{0,144},{8,152},{16,128},{24,136},{32,176},{40,184},{48,160},{56,1... | collective-permute-start | bytes 196616 | tf_op jit(solution)/shard_map/ppermute | solution.py:25
  25.8 5.5 %collective-permute-done.2.refs_2_ = bf16[2,16,1024]{2,1,0:T(8,128)(2,1)S(1)} collective-permute-done((bf16[2,16,1024]{2,1,0:T(8,128)(2,1)S(1)}, bf16[2,16,1024]{2,1,0:T(8,128)(2,1)S(1)}, u32[]{:S(2)}, u32[]{:S(2)}) %collective-permute-start.2) | collective-permute-done | bytes 65568 | tf_op jit(solution)/shard_map/ppermute | solution.py:25
  34.5 1.9 %collective-permute-start.11 = (bf16[128,1792]{1,0:T(8,128)(2,1)S(1)}, bf16[128,1792]{1,0:T(8,128)(2,1)S(1)}, u32[]{:S(2)}, u32[]{:S(2)}) collective-permute-start(bf16[128,1792]{1,0:T(8,128)(2,1)S(1)} %get-tuple-element.63), channel_id=1, source_target_pairs={{0,16},{8,24},{16,0},{24,8},{32,48},{40,56},{48,32},{56,40},{64,80... | collective-permute-start | bytes 1376264 | tf_op jit(solution)/shard_map/ppermute | solution.py:25
  36.4 1.8 %collective-permute-start.9 = (bf16[64,1792]{1,0:T(8,128)(2,1)S(1)}, bf16[64,1792]{1,0:T(8,128)(2,1)S(1)}, u32[]{:S(2)}, u32[]{:S(2)}) collective-permute-start(bf16[64,1792]{1,0:T(8,128)(2,1)S(1)} %get-tuple-element.61), channel_id=1, source_target_pairs={{0,128},{8,136},{16,144},{24,152},{32,160},{40,168},{48,176},{56,1... | collective-permute-start | bytes 688136 | tf_op jit(solution)/shard_map/ppermute | solution.py:25
  39.6 2.1 %collective-permute-start.8 = (bf16[4,16,1024]{2,1,0:T(8,128)(2,1)S(1)}, bf16[4,16,1024]{2,1,0:T(8,128)(2,1)S(1)}, u32[]{:S(2)}, u32[]{:S(2)}) collective-permute-start(bf16[4,16,1024]{2,1,0:T(8,128)(2,1)S(1)} %get-tuple-element.60.far_ref), channel_id=1, source_target_pairs={{0,6},{1,7},{2,4},{3,5},{4,2},{5,3},{6,0},{7,1},{8,14},{9,15},{10,... | collective-permute-start | bytes 393224 | tf_op jit(solution)/shard_map/ppermute | solution.py:25
  43.1 2.7 %collective-permute-done.8.far_x = bf16[4,16,1024]{2,1,0:T(8,128)(2,1)S(1)} collective-permute-done((bf16[4,16,1024]{2,1,0:T(8,128)(2,1)S(1)}, bf16[4,16,1024]{2,1,0:T(8,128)(2,1)S(1)}, u32[]{:S(2)}, u32[]{:S(2)}) %collective-permute-start.8) | collective-permute-done | bytes 131104 | tf_op jit(solution)/shard_map/ppermute | solution.py:25
  45.8 1.7 %collective-permute-done.9.z1_ref = bf16[64,1792]{1,0:T(8,128)(2,1)S(1)} collective-permute-done((bf16[64,1792]{1,0:T(8,128)(2,1)S(1)}, bf16[64,1792]{1,0:T(8,128)(2,1)S(1)}, u32[]{:S(2)}, u32[]{:S(2)}) %collective-permute-start.9) | collective-permute-done | bytes 229408 | tf_op jit(solution)/shard_map/ppermute | solution.py:25
  49.4 2.8 %collective-permute-start.12 = (bf16[2,4,16,1024]{3,2,1,0:T(8,128)(2,1)S(1)}, bf16[2,4,16,1024]{3,2,1,0:T(8,128)(2,1)}, u32[]{:S(2)}, u32[]{:S(2)}) collective-permute-start(bf16[2,4,16,1024]{3,2,1,0:T(8,128)(2,1)S(1)} %get-tuple-element.64.refs_1_), channel_id=1, source_target_pairs={{0,6},{1,7},{2,4},{3,5},{4,2},{5,3},{6,0},{7,1},{8,14},{9,15},{10,... | collective-permute-start | bytes 786440 | tf_op jit(solution)/shard_map/ppermute | solution.py:25
  52.4 9.3 %collective-permute-done.14.refs_3_.refs_8_ = bf16[128,1792]{1,0:T(8,128)(2,1)S(1)} collective-permute-done((bf16[128,1792]{1,0:T(8,128)(2,1)}, bf16[128,1792]{1,0:T(8,128)(2,1)S(1)}, u32[]{:S(2)}, u32[]{:S(2)}) %collective-permute-start.14) | collective-permute-done | bytes 458784 | tf_op jit(solution)/shard_map/ppermute | solution.py:25
  61.7 3.8 %shard_map.71 = (bf16[4,16,1024]{2,1,0:T(8,128)(2,1)S(1)}, bf16[4,16,1024]{2,1,0:T(8,128)(2,1)S(1)}, bf16[2,4,16,1024]{3,2,1,0:T(8,128)(2,1)S(1)}, bf16[4,16,102...) custom-call(s32[1]{0:T(128)} %bitcast.1.place_ref.refs_0_, ...), custom_call_target="tpu_custom_call" | custom-call | flops 1 | bytes 1 | tf_op jit(solution)/shard_map/pallas_call | solution.py:265
  65.5 3.4 %shard_map.72 = (bf16[4,1792,128]{2,1,0:T(8,128)(2,1)S(1)}, bf16[4,1792,128]{2,1,0:T(8,128)(2,1)S(1)}, bf16[512,1024]{1,0:T(8,128)(2,1)S(1)}) custom-call(s32[1]{0:T(128)} %bitcast.1.place_ref.refs_0_, bf16[2,4,16,1024]{3,2,1,0:T(8,128)(2,1)S(1)} %get-tuple-element.64.refs_1_, bf16[2,4,16,1024]{3,2,1,0:T(8,128)(2,1)} %collective-permute-done.12.refs_2_, ...), custom_call_target="tpu_custom_call" | custom-call | flops 5000000000 | bytes 1 | tf_op jit(solution)/shard_map/pallas_call | solution.py:265
  69.0 1.6 %collective-permute-start.17 = (bf16[2,4,16,1024]{3,2,1,0:T(8,128)(2,1)S(1)}, bf16[2,4,16,1024]{3,2,1,0:T(8,128)(2,1)S(1)}, u32[]{:S(2)}, u32[]{:S(2)}) collective-permute-start(bf16[2,4,16,1024]{3,2,1,0:T(8,128)(2,1)S(1)} %get-tuple-element.74), channel_id=1, source_target_pairs={{0,2},{1,3},{2,0},{3,1},{4,6},{5,7},{6,4},{7,5},{8,10},{9,11},{10,... | collective-permute-start | bytes 786440 | tf_op jit(solution)/shard_map/ppermute | solution.py:25
  70.6 2.1 %collective-permute-start.18 = (bf16[2,4,16,1024]{3,2,1,0:T(8,128)(2,1)S(1)}, bf16[2,4,16,1024]{3,2,1,0:T(8,128)(2,1)S(1)}, u32[]{:S(2)}, u32[]{:S(2)}) collective-permute-start(bf16[2,4,16,1024]{3,2,1,0:T(8,128)(2,1)S(1)} %get-tuple-element.77), channel_id=1, source_target_pairs={{0,6},{1,7},{2,4},{3,5},{4,2},{5,3},{6,0},{7,1},{8,14},{9,15},{10,... | collective-permute-start | bytes 786440 | tf_op jit(solution)/shard_map/ppermute | solution.py:25
  72.7 3.6 %shard_map.73 = (bf16[2,128,1792]{2,1,0:T(8,128)(2,1)S(1)}, bf16[2,64,1792]{2,1,0:T(8,128)(2,1)S(1)}, bf16[2,64,1792]{2,1,0:T(8,128)(2,1)S(1)}) custom-call(bf16[512,1024]{1,0:T(8,128)(2,1)S(1)} %get-tuple-element.71.rows_ref, bf16[4,1792,128]{2,1,0:T(8,128)(2,1)S(1)} %get-tuple-element.67.refs_4_.mine_ref, ...), custom_call_target="tpu_custom_call" | custom-call | flops 5000000000 | bytes 1 | tf_op jit(solution)/shard_map/pallas_call | solution.py:265
  77.7 2.4 %collective-permute-done.18.refs_5_ = bf16[2,4,16,1024]{3,2,1,0:T(8,128)(2,1)S(1)} collective-permute-done((bf16[2,4,16,1024]{3,2,1,0:T(8,128)(2,1)S(1)}, bf16[2,4,16,1024]{3,2,1,0:T(8,128)(2,1)S(1)}, u32[]{:S(2)}, u32[]{:S(2)}) %collective-permute-start.18) | collective-permute-done | bytes 262176 | tf_op jit(solution)/shard_map/ppermute | solution.py:25
  80.8 1.6 %collective-permute-start.19 = (bf16[2,896,128]{2,1,0:T(8,128)(2,1)S(1)}, bf16[2,896,128]{2,1,0:T(8,128)(2,1)S(1)}, u32[]{:S(2)}, u32[]{:S(2)}) collective-permute-start(bf16[2,896,128]{2,1,0:T(8,128)(2,1)S(1)} %get-tuple-element.79), channel_id=1, source_target_pairs={{0,48},{8,56},{16,32},{24,40},{32,16},{40,24},{48,0},{56,8},{64,11... | collective-permute-start | bytes 1376264 | tf_op jit(solution)/shard_map/ppermute | solution.py:25
  82.3 1.7 %collective-permute-start.20 = (bf16[2,64,1792]{2,1,0:T(8,128)(2,1)S(1)}, bf16[2,64,1792]{2,1,0:T(8,128)(2,1)S(1)}, u32[]{:S(2)}, u32[]{:S(2)}) collective-permute-start(bf16[2,64,1792]{2,1,0:T(8,128)(2,1)S(1)} %get-tuple-element.81), channel_id=1, source_target_pairs={{0,16},{8,24},{16,0},{24,8},{32,48},{40,56},{48,32},{56,40},{64,80... | collective-permute-start | bytes 1376264 | tf_op jit(solution)/shard_map/ppermute | solution.py:25
  84.0 2.1 %collective-permute-start.21 = (bf16[4,16,1024]{2,1,0:T(8,128)(2,1)S(1)}, bf16[4,16,1024]{2,1,0:T(8,128)(2,1)S(1)}, u32[]{:S(2)}, u32[]{:S(2)}) collective-permute-start(bf16[4,16,1024]{2,1,0:T(8,128)(2,1)S(1)} %get-tuple-element.83), channel_id=1, source_target_pairs={{0,6},{1,7},{2,4},{3,5},{4,2},{5,3},{6,0},{7,1},{8,14},{9,15},{10,... | collective-permute-start | bytes 393224 | tf_op jit(solution)/shard_map/ppermute | solution.py:25
  86.1 4.7 %collective-permute-start.23 = (bf16[4,16,1024]{2,1,0:T(8,128)(2,1)S(1)}, bf16[4,16,1024]{2,1,0:T(8,128)(2,1)S(1)}, u32[]{:S(2)}, u32[]{:S(2)}) collective-permute-start(bf16[4,16,1024]{2,1,0:T(8,128)(2,1)S(1)} %add_convert_fusion), channel_id=1, source_target_pairs={{0,1},{1,0},{2,3},{3,2},{4,5},{5,4},{6,7},{7,6},{8,9},{9,8},{10,11... | collective-permute-start | bytes 393224 | tf_op jit(solution)/shard_map/ppermute | solution.py:25
  90.8 5.6 %collective-permute-done.23.second_ref = bf16[4,16,1024]{2,1,0:T(8,128)(2,1)S(1)} collective-permute-done((bf16[4,16,1024]{2,1,0:T(8,128)(2,1)S(1)}, bf16[4,16,1024]{2,1,0:T(8,128)(2,1)S(1)}, u32[]{:S(2)}, u32[]{:S(2)}) %collective-permute-start.23) | collective-permute-done | bytes 131104 | tf_op jit(solution)/shard_map/ppermute | solution.py:25
  96.7 2.0 %collective-permute-start.26 = (bf16[2,64,1792]{2,1,0:T(8,128)(2,1)S(1)}, bf16[2,64,1792]{2,1,0:T(8,128)(2,1)S(1)}, u32[]{:S(2)}, u32[]{:S(2)}) collective-permute-start(bf16[2,64,1792]{2,1,0:T(8,128)(2,1)S(1)} %get-tuple-element.90), channel_id=1, source_target_pairs={{0,16},{8,24},{16,0},{24,8},{32,48},{40,56},{48,32},{56,40},{64,80... | collective-permute-start | bytes 1376264 | tf_op jit(solution)/shard_map/ppermute | solution.py:25
  98.7 2.7 %collective-permute-start.25 = (bf16[896,128]{1,0:T(8,128)(2,1)S(1)}, bf16[896,128]{1,0:T(8,128)(2,1)S(1)}, u32[]{:S(2)}, u32[]{:S(2)}) collective-permute-start(bf16[896,128]{1,0:T(8,128)(2,1)S(1)} %get-tuple-element.89), channel_id=1, source_target_pairs={{0,64},{8,72},{16,80},{24,88},{32,96},{40,104},{48,112},{56,120},{... | collective-permute-start | bytes 688136 | tf_op jit(solution)/shard_map/ppermute | solution.py:25
  101.7 6.9 %collective-permute-done.27.arrived_ref.refs_12_ = bf16[2,16,1024]{2,1,0:T(8,128)(2,1)S(1)} collective-permute-done((bf16[2,16,1024]{2,1,0:T(8,128)(2,1)S(1)}, bf16[2,16,1024]{2,1,0:T(8,128)(2,1)S(1)}, u32[]{:S(2)}, u32[]{:S(2)}) %collective-permute-start.27) | collective-permute-done | bytes 65568 | tf_op jit(solution)/shard_map/ppermute | solution.py:25
  108.6 4.1 %collective-permute-done.28.refs_1_.refs_8_ = bf16[64,1792]{1,0:T(8,128)(2,1)S(1)} collective-permute-done((bf16[64,1792]{1,0:T(8,128)(2,1)S(1)}, bf16[64,1792]{1,0:T(8,128)(2,1)S(1)}, u32[]{:S(2)}, u32[]{:S(2)}) %collective-permute-start.28) | collective-permute-done | bytes 229408 | tf_op jit(solution)/shard_map/ppermute | solution.py:25
  113.4 2.5 %collective-permute-start.31 = (bf16[2,16,1024]{2,1,0:T(8,128)(2,1)S(1)}, bf16[2,16,1024]{2,1,0:T(8,128)(2,1)S(1)}, u32[]{:S(2)}, u32[]{:S(2)}) collective-permute-start(bf16[2,16,1024]{2,1,0:T(8,128)(2,1)S(1)} %get-tuple-element.97), channel_id=1, source_target_pairs={{0,128},{8,136},{16,144},{24,152},{32,160},{40,168},{48,176},{56,1... | collective-permute-start | bytes 196616 | tf_op jit(solution)/shard_map/ppermute | solution.py:25
  115.9 12.0 %collective-permute-done.31.refs_13_ = bf16[2,16,1024]{2,1,0:T(8,128)(2,1)S(1)} collective-permute-done((bf16[2,16,1024]{2,1,0:T(8,128)(2,1)S(1)}, bf16[2,16,1024]{2,1,0:T(8,128)(2,1)S(1)}, u32[]{:S(2)}, u32[]{:S(2)}) %collective-permute-start.31) | collective-permute-done | bytes 65568 | tf_op jit(solution)/shard_map/ppermute | solution.py:25
  (56 shorter events, 16.1 us)
Async XLA Ops:
  0.6 11.5 %collective-permute-start = (bf16[16,4096]{1,0:T(8,128)(2,1)}, bf16[16,4096]{1,0:T(8,128)(2,1)S(1)}, u32[]{:S(2)}, u32[]{:S(2)}) collective-permute-start(bf16[16,4096]{1,0:T(8,128)(2,1)} %grad_ref.1), channel_id=1, source_target_pairs={{0,1},{1,0},{2,3},{3,2},{4,5},{5,4},{6,7},{7,6},{8,9},{9,8},{10,11... | collective-permute-start | bytes 393224 | tf_op jit(solution)/shard_map/ppermute | solution.py:25
  12.3 19.7 %collective-permute-start.6 = (bf16[1792,128]{1,0:T(8,128)(2,1)S(1)}, bf16[1792,128]{1,0:T(8,128)(2,1)S(1)}, u32[]{:S(2)}, u32[]{:S(2)}) collective-permute-start(bf16[1792,128]{1,0:T(8,128)(2,1)S(1)} %get-tuple-element.57), channel_id=1, source_target_pairs={{0,48},{8,56},{16,32},{24,40},{32,16},{40,24},{48,0},{56,8},{64,11... | collective-permute-start | bytes 1376264 | tf_op jit(solution)/shard_map/ppermute | solution.py:25
  14.0 19.4 %collective-permute-start.4 = (bf16[1792,128]{1,0:T(8,128)(2,1)S(1)}, bf16[1792,128]{1,0:T(8,128)(2,1)S(1)}, u32[]{:S(2)}, u32[]{:S(2)}) collective-permute-start(bf16[1792,128]{1,0:T(8,128)(2,1)S(1)} %get-tuple-element.57), channel_id=1, source_target_pairs={{0,64},{8,72},{16,80},{24,88},{32,96},{40,104},{48,112},{56,120},{... | collective-permute-start | bytes 1376264 | tf_op jit(solution)/shard_map/ppermute | solution.py:25
  17.3 14.7 %collective-permute-start.5 = (bf16[64,1792]{1,0:T(8,128)(2,1)S(1)}, bf16[64,1792]{1,0:T(8,128)(2,1)S(1)}, u32[]{:S(2)}, u32[]{:S(2)}) collective-permute-start(bf16[64,1792]{1,0:T(8,128)(2,1)S(1)} %get-tuple-element.58), channel_id=1, source_target_pairs={{0,128},{8,136},{16,144},{24,152},{32,160},{40,168},{48,176},{56,1... | collective-permute-start | bytes 688136 | tf_op jit(solution)/shard_map/ppermute | solution.py:25
  18.1 4.3 %collective-permute-start.1 = (bf16[2,16,1024]{2,1,0:T(8,128)(2,1)S(1)}, bf16[2,16,1024]{2,1,0:T(8,128)(2,1)S(1)}, u32[]{:S(2)}, u32[]{:S(2)}) collective-permute-start(bf16[2,16,1024]{2,1,0:T(8,128)(2,1)S(1)} %get-tuple-element.54), channel_id=1, source_target_pairs={{0,16},{8,24},{16,0},{24,8},{32,48},{40,56},{48,32},{56,40},{64,80... | collective-permute-start | bytes 196616 | tf_op jit(solution)/shard_map/ppermute | solution.py:25
  20.0 11.3 %collective-permute-start.2 = (bf16[2,16,1024]{2,1,0:T(8,128)(2,1)S(1)}, bf16[2,16,1024]{2,1,0:T(8,128)(2,1)S(1)}, u32[]{:S(2)}, u32[]{:S(2)}) collective-permute-start(bf16[2,16,1024]{2,1,0:T(8,128)(2,1)S(1)} %get-tuple-element.55), channel_id=1, source_target_pairs={{0,128},{8,136},{16,144},{24,152},{32,160},{40,168},{48,176},{56,1... | collective-permute-start | bytes 196616 | tf_op jit(solution)/shard_map/ppermute | solution.py:25
  22.3 9.6 %collective-permute-start.3 = (bf16[2,16,1024]{2,1,0:T(8,128)(2,1)S(1)}, bf16[2,16,1024]{2,1,0:T(8,128)(2,1)S(1)}, u32[]{:S(2)}, u32[]{:S(2)}) collective-permute-start(bf16[2,16,1024]{2,1,0:T(8,128)(2,1)S(1)} %get-tuple-element.56), channel_id=1, source_target_pairs={{0,144},{8,152},{16,128},{24,136},{32,176},{40,184},{48,160},{56,1... | collective-permute-start | bytes 196616 | tf_op jit(solution)/shard_map/ppermute | solution.py:25
  33.5 14.0 %collective-permute-start.10 = (bf16[1792,128]{1,0:T(8,128)(2,1)S(1)}, bf16[1792,128]{1,0:T(8,128)(2,1)S(1)}, u32[]{:S(2)}, u32[]{:S(2)}) collective-permute-start(bf16[1792,128]{1,0:T(8,128)(2,1)S(1)} %get-tuple-element.62), channel_id=1, source_target_pairs={{0,48},{8,56},{16,32},{24,40},{32,16},{40,24},{48,0},{56,8},{64,11... | collective-permute-start | bytes 1376264 | tf_op jit(solution)/shard_map/ppermute | solution.py:25
  34.5 13.0 %collective-permute-start.11 = (bf16[128,1792]{1,0:T(8,128)(2,1)S(1)}, bf16[128,1792]{1,0:T(8,128)(2,1)S(1)}, u32[]{:S(2)}, u32[]{:S(2)}) collective-permute-start(bf16[128,1792]{1,0:T(8,128)(2,1)S(1)} %get-tuple-element.63), channel_id=1, source_target_pairs={{0,16},{8,24},{16,0},{24,8},{32,48},{40,56},{48,32},{56,40},{64,80... | collective-permute-start | bytes 1376264 | tf_op jit(solution)/shard_map/ppermute | solution.py:25
  36.4 11.1 %collective-permute-start.9 = (bf16[64,1792]{1,0:T(8,128)(2,1)S(1)}, bf16[64,1792]{1,0:T(8,128)(2,1)S(1)}, u32[]{:S(2)}, u32[]{:S(2)}) collective-permute-start(bf16[64,1792]{1,0:T(8,128)(2,1)S(1)} %get-tuple-element.61), channel_id=1, source_target_pairs={{0,128},{8,136},{16,144},{24,152},{32,160},{40,168},{48,176},{56,1... | collective-permute-start | bytes 688136 | tf_op jit(solution)/shard_map/ppermute | solution.py:25
  38.1 5.0 %collective-permute-start.7 = (bf16[4,16,1024]{2,1,0:T(8,128)(2,1)S(1)}, bf16[4,16,1024]{2,1,0:T(8,128)(2,1)S(1)}, u32[]{:S(2)}, u32[]{:S(2)}) collective-permute-start(bf16[4,16,1024]{2,1,0:T(8,128)(2,1)S(1)} %get-tuple-element.59.near_ref), channel_id=1, source_target_pairs={{0,2},{1,3},{2,0},{3,1},{4,6},{5,7},{6,4},{7,5},{8,10},{9,11},{10,... | collective-permute-start | bytes 393224 | tf_op jit(solution)/shard_map/ppermute | solution.py:25
  39.6 6.2 %collective-permute-start.8 = (bf16[4,16,1024]{2,1,0:T(8,128)(2,1)S(1)}, bf16[4,16,1024]{2,1,0:T(8,128)(2,1)S(1)}, u32[]{:S(2)}, u32[]{:S(2)}) collective-permute-start(bf16[4,16,1024]{2,1,0:T(8,128)(2,1)S(1)} %get-tuple-element.60.far_ref), channel_id=1, source_target_pairs={{0,6},{1,7},{2,4},{3,5},{4,2},{5,3},{6,0},{7,1},{8,14},{9,15},{10,... | collective-permute-start | bytes 393224 | tf_op jit(solution)/shard_map/ppermute | solution.py:25
  48.5 13.1 %collective-permute-start.15 = (bf16[4,1792,128]{2,1,0:T(8,128)(2,1)S(1)}, bf16[4,1792,128]{2,1,0:T(8,128)(2,1)}, u32[]{:S(2)}, u32[]{:S(2)}) collective-permute-start(bf16[4,1792,128]{2,1,0:T(8,128)(2,1)S(1)} %get-tuple-element.67.refs_4_.mine_ref), channel_id=1, source_target_pairs={{0,8},{8,0},{16,24},{24,16},{32,40},{40,32},{48,56},{56,48},{64,72... | collective-permute-start | bytes 5505032 | tf_op jit(solution)/shard_map/ppermute | solution.py:25
  48.5 13.1 %collective-permute-start.14 = (bf16[128,1792]{1,0:T(8,128)(2,1)}, bf16[128,1792]{1,0:T(8,128)(2,1)S(1)}, u32[]{:S(2)}, u32[]{:S(2)}) collective-permute-start(bf16[128,1792]{1,0:T(8,128)(2,1)} %get-tuple-element.66.refs_2_.refs_7_), channel_id=1, source_target_pairs={{0,16},{8,24},{16,0},{24,8},{32,48},{40,56},{48,32},{56,40},{64,80... | collective-permute-start | bytes 1376264 | tf_op jit(solution)/shard_map/ppermute | solution.py:25
  49.4 16.1 %collective-permute-start.12 = (bf16[2,4,16,1024]{3,2,1,0:T(8,128)(2,1)S(1)}, bf16[2,4,16,1024]{3,2,1,0:T(8,128)(2,1)}, u32[]{:S(2)}, u32[]{:S(2)}) collective-permute-start(bf16[2,4,16,1024]{3,2,1,0:T(8,128)(2,1)S(1)} %get-tuple-element.64.refs_1_), channel_id=1, source_target_pairs={{0,6},{1,7},{2,4},{3,5},{4,2},{5,3},{6,0},{7,1},{8,14},{9,15},{10,... | collective-permute-start | bytes 786440 | tf_op jit(solution)/shard_map/ppermute | solution.py:25
  52.1 13.3 %collective-permute-start.13 = (bf16[2,4,16,1024]{3,2,1,0:T(8,128)(2,1)}, bf16[2,4,16,1024]{3,2,1,0:T(8,128)(2,1)}, u32[]{:S(2)}, u32[]{:S(2)}) collective-permute-start(bf16[2,4,16,1024]{3,2,1,0:T(8,128)(2,1)} %get-tuple-element.65.refs_3_), channel_id=1, source_target_pairs={{0,2},{1,3},{2,0},{3,1},{4,6},{5,7},{6,4},{7,5},{8,10},{9,11},{10,... | collective-permute-start | bytes 786440 | tf_op jit(solution)/shard_map/ppermute | solution.py:25
  68.9 11.3 %collective-permute-start.16 = (bf16[4,1792,128]{2,1,0:T(8,128)(2,1)S(1)}, bf16[4,1792,128]{2,1,0:T(8,128)(2,1)S(1)}, u32[]{:S(2)}, u32[]{:S(2)}) collective-permute-start(bf16[4,1792,128]{2,1,0:T(8,128)(2,1)S(1)} %get-tuple-element.70), channel_id=1, source_target_pairs={{0,8},{8,0},{16,24},{24,16},{32,40},{40,32},{48,56},{56,48},{64,72... | collective-permute-start | bytes 5505032 | tf_op jit(solution)/shard_map/ppermute | solution.py:25
  69.0 8.7 %collective-permute-start.17 = (bf16[2,4,16,1024]{3,2,1,0:T(8,128)(2,1)S(1)}, bf16[2,4,16,1024]{3,2,1,0:T(8,128)(2,1)S(1)}, u32[]{:S(2)}, u32[]{:S(2)}) collective-permute-start(bf16[2,4,16,1024]{3,2,1,0:T(8,128)(2,1)S(1)} %get-tuple-element.74), channel_id=1, source_target_pairs={{0,2},{1,3},{2,0},{3,1},{4,6},{5,7},{6,4},{7,5},{8,10},{9,11},{10,... | collective-permute-start | bytes 786440 | tf_op jit(solution)/shard_map/ppermute | solution.py:25
  70.6 9.6 %collective-permute-start.18 = (bf16[2,4,16,1024]{3,2,1,0:T(8,128)(2,1)S(1)}, bf16[2,4,16,1024]{3,2,1,0:T(8,128)(2,1)S(1)}, u32[]{:S(2)}, u32[]{:S(2)}) collective-permute-start(bf16[2,4,16,1024]{3,2,1,0:T(8,128)(2,1)S(1)} %get-tuple-element.77), channel_id=1, source_target_pairs={{0,6},{1,7},{2,4},{3,5},{4,2},{5,3},{6,0},{7,1},{8,14},{9,15},{10,... | collective-permute-start | bytes 786440 | tf_op jit(solution)/shard_map/ppermute | solution.py:25
  80.7 5.4 %collective-permute-start.22 = (bf16[4,16,1024]{2,1,0:T(8,128)(2,1)S(1)}, bf16[4,16,1024]{2,1,0:T(8,128)(2,1)S(1)}, u32[]{:S(2)}, u32[]{:S(2)}) collective-permute-start(bf16[4,16,1024]{2,1,0:T(8,128)(2,1)S(1)} %get-tuple-element.85), channel_id=1, source_target_pairs={{0,2},{1,3},{2,0},{3,1},{4,6},{5,7},{6,4},{7,5},{8,10},{9,11},{10,... | collective-permute-start | bytes 393224 | tf_op jit(solution)/shard_map/ppermute | solution.py:25
  80.8 15.7 %collective-permute-start.19 = (bf16[2,896,128]{2,1,0:T(8,128)(2,1)S(1)}, bf16[2,896,128]{2,1,0:T(8,128)(2,1)S(1)}, u32[]{:S(2)}, u32[]{:S(2)}) collective-permute-start(bf16[2,896,128]{2,1,0:T(8,128)(2,1)S(1)} %get-tuple-element.79), channel_id=1, source_target_pairs={{0,48},{8,56},{16,32},{24,40},{32,16},{40,24},{48,0},{56,8},{64,11... | collective-permute-start | bytes 1376264 | tf_op jit(solution)/shard_map/ppermute | solution.py:25
  82.3 14.1 %collective-permute-start.20 = (bf16[2,64,1792]{2,1,0:T(8,128)(2,1)S(1)}, bf16[2,64,1792]{2,1,0:T(8,128)(2,1)S(1)}, u32[]{:S(2)}, u32[]{:S(2)}) collective-permute-start(bf16[2,64,1792]{2,1,0:T(8,128)(2,1)S(1)} %get-tuple-element.81), channel_id=1, source_target_pairs={{0,16},{8,24},{16,0},{24,8},{32,48},{40,56},{48,32},{56,40},{64,80... | collective-permute-start | bytes 1376264 | tf_op jit(solution)/shard_map/ppermute | solution.py:25
  84.0 6.8 %collective-permute-start.21 = (bf16[4,16,1024]{2,1,0:T(8,128)(2,1)S(1)}, bf16[4,16,1024]{2,1,0:T(8,128)(2,1)S(1)}, u32[]{:S(2)}, u32[]{:S(2)}) collective-permute-start(bf16[4,16,1024]{2,1,0:T(8,128)(2,1)S(1)} %get-tuple-element.83), channel_id=1, source_target_pairs={{0,6},{1,7},{2,4},{3,5},{4,2},{5,3},{6,0},{7,1},{8,14},{9,15},{10,... | collective-permute-start | bytes 393224 | tf_op jit(solution)/shard_map/ppermute | solution.py:25
  86.1 10.3 %collective-permute-start.23 = (bf16[4,16,1024]{2,1,0:T(8,128)(2,1)S(1)}, bf16[4,16,1024]{2,1,0:T(8,128)(2,1)S(1)}, u32[]{:S(2)}, u32[]{:S(2)}) collective-permute-start(bf16[4,16,1024]{2,1,0:T(8,128)(2,1)S(1)} %add_convert_fusion), channel_id=1, source_target_pairs={{0,1},{1,0},{2,3},{3,2},{4,5},{5,4},{6,7},{7,6},{8,9},{9,8},{10,11... | collective-permute-start | bytes 393224 | tf_op jit(solution)/shard_map/ppermute | solution.py:25
  96.6 16.0 %collective-permute-start.24 = (bf16[2,896,128]{2,1,0:T(8,128)(2,1)S(1)}, bf16[2,896,128]{2,1,0:T(8,128)(2,1)S(1)}, u32[]{:S(2)}, u32[]{:S(2)}) collective-permute-start(bf16[2,896,128]{2,1,0:T(8,128)(2,1)S(1)} %get-tuple-element.88), channel_id=1, source_target_pairs={{0,48},{8,56},{16,32},{24,40},{32,16},{40,24},{48,0},{56,8},{64,11... | collective-permute-start | bytes 1376264 | tf_op jit(solution)/shard_map/ppermute | solution.py:25
  96.7 15.9 %collective-permute-start.26 = (bf16[2,64,1792]{2,1,0:T(8,128)(2,1)S(1)}, bf16[2,64,1792]{2,1,0:T(8,128)(2,1)S(1)}, u32[]{:S(2)}, u32[]{:S(2)}) collective-permute-start(bf16[2,64,1792]{2,1,0:T(8,128)(2,1)S(1)} %get-tuple-element.90), channel_id=1, source_target_pairs={{0,16},{8,24},{16,0},{24,8},{32,48},{40,56},{48,32},{56,40},{64,80... | collective-permute-start | bytes 1376264 | tf_op jit(solution)/shard_map/ppermute | solution.py:25
  98.7 9.9 %collective-permute-start.25 = (bf16[896,128]{1,0:T(8,128)(2,1)S(1)}, bf16[896,128]{1,0:T(8,128)(2,1)S(1)}, u32[]{:S(2)}, u32[]{:S(2)}) collective-permute-start(bf16[896,128]{1,0:T(8,128)(2,1)S(1)} %get-tuple-element.89), channel_id=1, source_target_pairs={{0,64},{8,72},{16,80},{24,88},{32,96},{40,104},{48,112},{56,120},{... | collective-permute-start | bytes 688136 | tf_op jit(solution)/shard_map/ppermute | solution.py:25
  101.4 11.2 %collective-permute-start.28 = (bf16[64,1792]{1,0:T(8,128)(2,1)S(1)}, bf16[64,1792]{1,0:T(8,128)(2,1)S(1)}, u32[]{:S(2)}, u32[]{:S(2)}) collective-permute-start(bf16[64,1792]{1,0:T(8,128)(2,1)S(1)} %get-tuple-element.93), channel_id=1, source_target_pairs={{0,128},{8,136},{16,144},{24,152},{32,160},{40,168},{48,176},{56,1... | collective-permute-start | bytes 688136 | tf_op jit(solution)/shard_map/ppermute | solution.py:25
  101.4 7.1 %collective-permute-start.27 = (bf16[2,16,1024]{2,1,0:T(8,128)(2,1)S(1)}, bf16[2,16,1024]{2,1,0:T(8,128)(2,1)S(1)}, u32[]{:S(2)}, u32[]{:S(2)}) collective-permute-start(bf16[2,16,1024]{2,1,0:T(8,128)(2,1)S(1)} %get-tuple-element.92), channel_id=1, source_target_pairs={{0,16},{8,24},{16,0},{24,8},{32,48},{40,56},{48,32},{56,40},{64,80... | collective-permute-start | bytes 196616 | tf_op jit(solution)/shard_map/ppermute | solution.py:25
  112.7 15.1 %collective-permute-start.29 = (bf16[896,128]{1,0:T(8,128)(2,1)S(1)}, bf16[896,128]{1,0:T(8,128)(2,1)S(1)}, u32[]{:S(2)}, u32[]{:S(2)}) collective-permute-start(bf16[896,128]{1,0:T(8,128)(2,1)S(1)} %get-tuple-element.94), channel_id=1, source_target_pairs={{0,64},{8,72},{16,80},{24,88},{32,96},{40,104},{48,112},{56,120},{... | collective-permute-start | bytes 688136 | tf_op jit(solution)/shard_map/ppermute | solution.py:25
  112.8 15.0 %collective-permute-start.30 = (bf16[64,1792]{1,0:T(8,128)(2,1)S(1)}, bf16[64,1792]{1,0:T(8,128)(2,1)S(1)}, u32[]{:S(2)}, u32[]{:S(2)}) collective-permute-start(bf16[64,1792]{1,0:T(8,128)(2,1)S(1)} %get-tuple-element.95), channel_id=1, source_target_pairs={{0,128},{8,136},{16,144},{24,152},{32,160},{40,168},{48,176},{56,1... | collective-permute-start | bytes 688136 | tf_op jit(solution)/shard_map/ppermute | solution.py:25
  113.4 14.5 %collective-permute-start.31 = (bf16[2,16,1024]{2,1,0:T(8,128)(2,1)S(1)}, bf16[2,16,1024]{2,1,0:T(8,128)(2,1)S(1)}, u32[]{:S(2)}, u32[]{:S(2)}) collective-permute-start(bf16[2,16,1024]{2,1,0:T(8,128)(2,1)S(1)} %get-tuple-element.97), channel_id=1, source_target_pairs={{0,128},{8,136},{16,144},{24,152},{32,160},{40,168},{48,176},{56,1... | collective-permute-start | bytes 196616 | tf_op jit(solution)/shard_map/ppermute | solution.py:25
  (6 other events, 44.1 us)

commit v3 on v2

--- a/solution.py
+++ b/solution.py
@@ -18,7 +18,10 @@
 COLUMN_BLOCKS = COLUMN_PARTS + tuple(k ^ CORE for k in COLUMN_PARTS)
 STEP = 256
 COST = 1
-EARLY = 64
+PACKED = 3 * 384 + 256
+KEPT = 3 * 256 + 128
+CHUNKS = ((0, 512, 0, 0), (512, 1024, 384, 256), (1024, 1536, 768, 512), (1536, 1792, 1152, 768))
+EARLY = 80
 
 
 def swap(array, axis, size, k):
@@ -45,7 +48,7 @@
     return pl.BlockSpec(memory_space=pltpu.VMEM)
 
 
-def call(kernel, out_shape, scratch=(), grid=None, in_specs=None, out_specs=None, flops=0, moved=0, limit=16 * 2**20):
+def call(kernel, out_shape, scratch=(), grid=None, in_specs=None, out_specs=None, flops=0, moved=0, limit=12 * 2**20):
     return pl.pallas_call(
         kernel,
         out_shape=out_shape,
@@ -58,37 +61,95 @@
     )
 
 
-def mask_kernel(pre_in, code_in, hidden_ref, slope_ref, pre_ref, code_ref, sems):
-    copies = [
-        pltpu.make_async_copy(pre_in, pre_ref, sems.at[0]),
-        pltpu.make_async_copy(code_in, code_ref, sems.at[1]),
-    ]
-    for copy in copies:
-        copy.start()
-    for copy in copies:
-        copy.wait()
-    groups = code_ref.shape[0]
-    for at in range(0, groups, 128):
-        size = min(128, groups - at)
-        spread = (
-            lax.broadcasted_iota(jnp.int32, (size, 4 * size), 1) // 4
-            == lax.broadcasted_iota(jnp.int32, (size, 4 * size), 0)
-        ).astype(BF16)
-        codes = code_ref[at : at + size, :].astype(F32).astype(BF16)
-        code = lax.dot_general(
-            codes, spread, (((0,), (0,)), ((), ())), preferred_element_type=F32
-        )
-        lane = lax.broadcasted_iota(jnp.int32, code.shape, 1) % 4
-        kept = (
-            ((lane == 0) & (code < 2.5))
-            | ((lane == 1) & ((code == 0.0) | (code == 3.0) | (code == 4.0)))
-            | ((lane == 2) & ((code == 1.0) | (code == 3.0) | (code == 5.0)))
-            | ((lane == 3) & ((code == 2.0) | (code > 3.5)))
-        )
-        columns = slice(4 * at, 4 * (at + size))
-        positive = jnp.where(kept, jnp.maximum(pre_ref[:, columns].astype(F32), 0.0), 0.0)
-        hidden_ref[:, columns] = (positive * positive).astype(BF16)
-        slope_ref[:, columns] = (2.0 * positive).astype(BF16)
+def spread(rows, width, start=0):
+    of = lax.broadcasted_iota(jnp.int32, (rows, width), 1) // 4 + start
+    return (of == lax.broadcasted_iota(jnp.int32, (rows, width), 0)).astype(BF16)
+
+
+def spreads(width):
+    if width == 512:
+        return spread(128, 512), spread(128, 512)
+    return spread(128, 256), spread(128, 256, 64)
+
+
+def matmul(a, b):
+    return jnp.dot(a, b, preferred_element_type=F32)
+
+
+def matmul_t(a, b):
+    return lax.dot_general(a, b, (((1,), (1,)), ((), ())), preferred_element_type=F32)
+
+
+def kept_places(code):
+    first = (code > 2.5).astype(F32) + (code > 4.5).astype(F32)
+    second = 3.0 - ((code == 1.0) | (code == 3.0)).astype(F32) - 2.0 * (code == 0.0).astype(F32)
+    return first.astype(BF16), second.astype(BF16)
+
+
+def lanes(shape):
+    return (lax.broadcasted_iota(jnp.int32, shape, 1) % 4).astype(F32)
+
+
+def put_kept(ref, at, kept0, kept1, width):
+    to0, to1 = spreads(width)
+    if width == 512:
+        ref[:, at : at + 128] = matmul_t(kept0, to0).astype(BF16)
+        ref[:, at + 128 : at + 256] = matmul_t(kept1, to1).astype(BF16)
+    else:
+        ref[:, at : at + 128] = (matmul_t(kept0, to0) + matmul_t(kept1, to1)).astype(BF16)
+
+
+def mask_kernel(pre_ref, code_ref, hidden_ref, slope_ref, first_ref, packed_ref):
+    for low, high, at, _ in CHUNKS:
+        width = high - low
+        code = code_ref[low // 4 : high // 4, :].astype(F32)
+        first, second = kept_places(code)
+        turn = (((0,), (0,)), ((), ()))
+        to = spread(width // 4, width)
+        first = lax.dot_general(first, to, turn, preferred_element_type=F32)
+        second = lax.dot_general(second, to, turn, preferred_element_type=F32)
+        lane = lanes(first.shape)
+        is_first, is_second = first == lane, second == lane
+        positive = jnp.maximum(pre_ref[:, low:high].astype(F32), 0.0)
+        square = positive * positive
+        kept0 = jnp.where(is_first, square, 0.0)
+        kept1 = jnp.where(is_second, square, 0.0)
+        hidden_ref[:, low:high] = (kept0 + kept1).astype(BF16)
+        slope_ref[:, low:high] = jnp.where(is_first | is_second, 2.0 * positive, 0.0).astype(BF16)
+        first_ref[:, low:high] = jnp.where(is_first, 1.0, 0.0).astype(BF16)
+        put_kept(packed_ref, at, kept0.astype(BF16), kept1.astype(BF16), width)
+        same = lax.broadcasted_iota(jnp.int32, (width // 4, 128), 0)
+        same = (same == lax.broadcasted_iota(jnp.int32, same.shape, 1)).astype(BF16)
+        codes = lax.dot_general(code.astype(BF16), same, turn, preferred_element_type=F32)
+        at = at + (256 if width == 512 else 128)
+        packed_ref[:, at : at + 128] = codes.astype(BF16)
+
+
+def spread_kept(ref, at, width):
+    to0, to1 = spreads(width)
+    values = ref[:, at : at + 128]
+    others = ref[:, at + 128 : at + 256] if width == 512 else values
+    return matmul(values, to0), matmul(others, to1)
+
+
+def unpack_kernel(*refs):
+    count = len(refs) // 4
+    for n in range(count):
+        packed_ref = refs[n]
+        hidden_ref, first_ref, second_ref = refs[count + 3 * n : count + 3 * n + 3]
+        for low, high, at, _ in CHUNKS:
+            width = high - low
+            value0, value1 = spread_kept(packed_ref, at, width)
+            at = at + (256 if width == 512 else 128)
+            first, second = kept_places(packed_ref[:, at : at + 128].astype(F32))
+            to = spreads(width)[0]
+            first, second = matmul(first, to), matmul(second, to)
+            lane = lanes(first.shape)
+            is_first, is_second = first == lane, second == lane
+            hidden = jnp.where(is_first, value0, jnp.where(is_second, value1, 0.0))
+            hidden_ref[:, low:high] = hidden.astype(BF16)
+            first_ref[:, low:high] = jnp.where(is_first, 1.0, 0.0).astype(BF16)
+            second_ref[:, low:high] = jnp.where(is_second, 1.0, 0.0).astype(BF16)
 
 
 def first_kernel(place_ref, grad_ref, grad_far, hidden_ref, weight_ref, *refs):
@@ -180,20 +241,20 @@
 
 
 def back_kernel(rows_ref, mine_ref, far_ref, *refs):
-    near_ref, half0_ref, half1_ref = refs[-3:]
+    masks, (near_ref, z_ref, half0_ref, half1_ref, kept_ref) = refs[:6], refs[6:]
+    for low, high, _, to in CHUNKS:
+        at = slice(low, high)
+        weight = jnp.concatenate([ref[n, at, :] for ref in (mine_ref, far_ref) for n in range(4)], axis=1)
+        back = matmul_t(rows_ref[...], weight).astype(BF16)
+        near_ref[:, at] = back[:128]
+        first = jnp.concatenate([ref[:, at] for ref in masks[::2]], axis=0)
+        second = jnp.concatenate([ref[:, at] for ref in masks[1::2]], axis=0)
+        put_kept(kept_ref, to, back[128:] * first, back[128:] * second, high - low)
     middle = half0_ref.shape[1]
-
-    def body(at):
-        weight = jnp.concatenate([ref[n, at, :] for ref in (mine_ref, far_ref) for n in range(4)], axis=1)
-        back = lax.dot_general(
-            rows_ref[...], weight, (((1,), (1,)), ((), ())), preferred_element_type=F32
-        ).astype(BF16)
-        for n in range(2):
-            near_ref[n, :, at] = back[256 * n : 256 * n + 128]
-            half0_ref[n, :, at] = back[256 * n + 128 : 256 * n + 128 + middle]
-            half1_ref[n, :, at] = back[256 * n + 128 + middle : 256 * n + 256]
-
-    steps(mine_ref.shape[1], body)
+    z_ref[...] = kept_ref[128:256]
+    for n in range(2):
+        half0_ref[n] = kept_ref[256 * n : 256 * n + middle]
+        half1_ref[n] = kept_ref[256 * n + middle : 256 * n + 128]
 
 
 def added(*arrays):
@@ -224,7 +285,7 @@
     weight_out, back_out, weight1_out, back1_out, total_ref, send_ref = refs[2:]
     middle = far0_ref.shape[1]
     weight_out[...] = added(sum_ref[1, :middle], far0_ref[1]).astype(BF16)
-    back_out[...] = added(back_ref[1, : back0_ref.shape[1]], back0_ref[1]).astype(BF16)
+    back_out[...] = added(back_ref[: back0_ref.shape[1]], back0_ref[1]).astype(BF16)
     weight1_out[...] = weight1_ref[...]
     back1_out[...] = back1_ref[...]
     total = added(first_ref[...], first_far[...], second_ref[...]).astype(BF16)
@@ -237,22 +298,27 @@
     weight_out, back_out, send_ref = refs[-3:]
     middle = sum_ref.shape[1] - far1_ref.shape[1]
     weight_out[...] = added(sum_ref[1, middle:], far1_ref[1]).astype(BF16)
-    middle = back_ref.shape[1] - back1_ref.shape[1]
-    back_out[...] = added(back_ref[1, middle:], back1_ref[1]).astype(BF16)
+    middle = back_ref.shape[0] - back1_ref.shape[1]
+    back_out[...] = added(back_ref[middle:], back1_ref[1]).astype(BF16)
     send_ref[0] = total_ref[2]
     send_ref[1] = arrived_ref[1]
 
 
 def last_kernel(place_ref, *refs):
-    sum_ref, far0, far1, z0, z1, back_ref, back0, back1, backz0, backz1, slope_ref = refs[:11]
-    total_ref, arrived_y, arrived_z, weight_out, input_out, output_ref = refs[11:]
+    sum_ref, far0, far1, z0, z1, back_ref, back0, back1, backz0, backz1 = refs[:10]
+    slope_ref, first_ref = refs[10:12]
+    total_ref, arrived_y, arrived_z, weight_out, input_out, output_ref = refs[12:]
     middle = far0.shape[1]
     for at, far, last in ((slice(0, middle), far0, z0), (slice(middle, None), far1, z1)):
         weight_out[at] = added(sum_ref[0, at], far[0], last[...]).astype(BF16)
     middle = back0.shape[1]
-    for at, far, last in ((slice(0, middle), back0, backz0), (slice(middle, None), back1, backz1)):
-        back = added(back_ref[0, at], far[0], last[...])
-        input_out[at] = (slope_ref[at].astype(F32) * back).astype(BF16)
+    for at, far, last in ((slice(0, middle), back0.at[0], backz0), (slice(middle, None), back1.at[0], backz1)):
+        for low, high, _, to in CHUNKS:
+            far_0, far_1 = spread_kept(far, to, high - low)
+            last_0, last_1 = spread_kept(last, to, high - low)
+            arrived = jnp.where(first_ref[at, low:high].astype(F32) > 0.5, far_0 + last_0, far_1 + last_1)
+            back = back_ref[at, low:high].astype(F32) + arrived
+            input_out[at, low:high] = (slope_ref[at, low:high].astype(F32) * back).astype(BF16)
     me = place_ref[0]
     parts = (total_ref.at[0], arrived_y.at[0], arrived_z.at[0], arrived_z.at[1])
     for part_ref, token in zip(parts, TOKEN_PARTS):
@@ -284,33 +350,28 @@
     def wide(*sizes):
         return jax.ShapeDtypeStruct(sizes, F32)
 
-    piece, half, column = shape(rows, width), shape(rows // 2, width), shape(width, 128)
+    piece, column = shape(rows, width), shape(width, 128)
+    packed_shape, half = shape(rows, PACKED), shape(rows // 2, PACKED)
     part, pair = shape(4, 16, 1024), shape(2, 4, 16, 1024)
     early = width * EARLY // rows
     split0, split1 = shape(2, early, 128), shape(2, width - early, 128)
     rows_scratch = [pltpu.VMEM((512, 1024), BF16)]
 
     grad_far = mp_swap(output_grad, 1)
-    codes = keep_codes.T
-    hidden, slope = call(
+    hidden, slope, first_kept, packed = move(
         mask_kernel,
-        [piece, piece],
-        in_specs=[pl.BlockSpec(memory_space=pl.ANY)] * 2,
-        out_specs=[whole()] * 2,
-        scratch=[
-            pltpu.VMEM(preactivation.shape, BF16),
-            pltpu.VMEM(codes.shape, jnp.int32),
-            pltpu.SemaphoreType.DMA((2,)),
-        ],
+        [piece, piece, piece, packed_shape],
+        preactivation,
+        keep_codes.T,
         flops=10**11,
-    )(preactivation, codes)
+    )
     outs = move(
         first_kernel,
         [shape(2, 16, 1024)] * 4 + [half, column],
         dp_place,
         output_grad,
         grad_far,
-        hidden,
+        packed,
         down_weight,
     )
     parts, half_out, weight_out = outs[:4], outs[4], outs[5]
@@ -320,7 +381,7 @@
     weight_y = dp_swap(weight_out, COLS_Y)
     hidden_z0 = dp_swap(half_out, ROWS_Z)
     near, far, half_out, hidden_out, weight_out = move(
-        second_kernel, [part, part, half, piece, column], *parts, hidden, weight_z, hidden_z0, weight_y
+        second_kernel, [part, part, half, packed_shape, column], *parts, packed, weight_z, hidden_z0, weight_y
     )
 
     near_x = mp_swap(near, 2)
@@ -330,7 +391,7 @@
     weight_yz = dp_swap(weight_out, COLS_Y)
     near_two, far_two, hidden_z, weights = move(
         third_kernel,
-        [pair, pair, piece, shape(4, width, 128)],
+        [pair, pair, packed_shape, shape(4, width, 128)],
         near,
         near_x,
         far,
@@ -349,6 +410,12 @@
     hidden_yz = dp_swap(hidden_z, ROWS_Y)
     weights_far = dp_swap(weights, CORE)
     grads = [near_two, near_rest, far_two, far_rest]
+    masked = [piece] * 3
+    hidden_y, first_y, second_y, hidden_z, first_z, second_z = move(
+        unpack_kernel, masked * 2, hidden_y, hidden_z, flops=3 * 10**9
+    )
+    hidden_yz, first_yz, second_yz = move(unpack_kernel, masked, hidden_yz)
+    masks = [first_y, second_y, first_z, second_z, first_yz, second_yz]
     hiddens = [hidden, hidden_y, hidden_z, hidden_yz]
 
     first0, first3, first_send, second0, second1, second_send = move(
@@ -372,18 +439,20 @@
         flops=5 * 10**9,
     )
     away = dp_swap(away, CORE)
-    back_near, half0, half1 = move(
+    back_near, back_z, half0, half1 = move(
         back_kernel,
-        [shape(2, rows, width), shape(2, EARLY, width), shape(2, rows - EARLY, width)],
+        [piece, shape(rows, KEPT), shape(2, EARLY, KEPT), shape(2, rows - EARLY, KEPT)],
         grad_rows,
         weights,
         weights_far,
+        *masks,
+        scratch=[pltpu.VMEM((3 * rows, KEPT), BF16)],
         flops=5 * 10**9,
     )
 
     send0, send1, sums, half0, first, first_send, second, second_send = move(
         y_kernel,
-        [split0, split1, wide(2, width, 128), shape(2, EARLY, width)]
+        [split0, split1, wide(2, width, 128), shape(2, EARLY, KEPT)]
         + [wide(4, 16, 1024), part] * 2,
         near,
         away,
@@ -404,15 +473,15 @@
         z0_kernel,
         [
             shape(early, 128),
-            shape(EARLY, width),
+            shape(EARLY, KEPT),
             split1,
-            shape(2, rows - EARLY, width),
+            shape(2, rows - EARLY, KEPT),
             part,
             shape(2, 16, 1024),
         ],
         sums,
         far0,
-        back_near,
+        back_z,
         back0,
         first,
         first_far,
@@ -428,10 +497,10 @@
 
     weight_z1, back_z1, total_send = move(
         z1_kernel,
-        [shape(width - early, 128), shape(rows - EARLY, width), shape(2, 16, 1024)],
+        [shape(width - early, 128), shape(rows - EARLY, KEPT), shape(2, 16, 1024)],
         sums,
         far1,
-        back_near,
+        back_z,
         back1,
         total,
         arrived_y,
@@ -456,6 +525,7 @@
         back_z0,
         back_z1,
         slope,
+        first_kept,
         total,
         arrived_y,
         arrived_z,

time: 129 us -> 120 us (0.930)
  waiting for transfers between devices: 55.3 us -> 38.7 us
  Pallas kernels: 16.4 us -> 19.5 us
  starting transfers between devices: 54.6 us -> 57 us
  local copies, waits for them, and re-layouts: 1.97 us -> 3.73 us
    ppermute x32, waiting for transfers between devices: 55.3 us -> 38.7 us  [swap(): return lax.ppermute(array, axis, [(i, i ^ k) for i in range(size)])]
    pallas_call x10 -> x13, Pallas kernels: 14.1 us -> 19.5 us  [move(): call(kernel, out_shape, in_specs=[in_smem() if a.dtype == jnp.int32 and a...]
    ppermute x32, starting transfers between devices: 54.6 us -> 57 us  [swap(): return lax.ppermute(array, axis, [(i, i ^ k) for i in range(size)])]
    pallas_call x1 -> x0, Pallas kernels: 2.25 us -> none  [on_device(): call(mask_kernel, [piece, piece], in_specs=[pl.BlockSpec(memory_space=pl....]
    unnamed x12 -> x20, local copies, waits for them, and re-layouts: 1.97 us -> 3.73 us
  transfers between devices with their start and end apart: 32 -> 32, of which waited for: 14 -> 15; matrix products, arithmetic and copies ran while one was open for 0% -> 0% of each run, Pallas kernels for 7% -> 11%
where the time goes in v3:
time: 120 us
  starting transfers between devices  57 us (48%)
  waiting for transfers between devices  38.7 us (32%)
  Pallas kernels  19.5 us (16%)
  local copies, waits for them, and re-layouts  3.73 us (3%)
    ppermute x32, starting transfers between devices, swap(): return lax.ppermute(array, axis, [(i, i ^ k) for i in range(size)])  57 us
    ppermute x32, waiting for transfers between devices, swap(): return lax.ppermute(array, axis, [(i, i ^ k) for i in range(size)])  38.7 us
    pallas_call x13, Pallas kernels, move(): call(kernel, out_shape, in_specs=[in_smem() if a.dtype == jnp.int32 and a...  19.5 us
    unnamed x20, local copies, waits for them, and re-layouts  3.73 us
  transfers between devices with their start and end apart: 32, of which 15 were waited for; matrix products, arithmetic and copies ran while one was open for 0% of the time, Pallas kernels for 11%

profile of v3, /device:TPU:8, one launch (start us, length us, event | category | flops | bytes accessed | tf_op | source)
XLA Modules:
  0.0 119.8 jit_solution(13737266455250234492)
XLA Ops:
  0.6 7.3 %collective-permute-start = (bf16[16,4096]{1,0:T(8,128)(2,1)}, bf16[16,4096]{1,0:T(8,128)(2,1)S(1)}, u32[]{:S(2)}, u32[]{:S(2)}) collective-permute-start(bf16[16,4096]{1,0:T(8,128)(2,1)} %grad_ref.1), channel_id=1, source_target_pairs={{0,1},{1,0},{2,3},{3,2},{4,5},{5,4},{6,7},{7,6},{8,9},{9,8},{10,11... | collective-permute-start | bytes 393224 | tf_op jit(solution)/shard_map/ppermute | solution.py:28
  11.8 1.7 %collective-permute-start.6 = (bf16[1792,128]{1,0:T(8,128)(2,1)S(1)}, bf16[1792,128]{1,0:T(8,128)(2,1)S(1)}, u32[]{:S(2)}, u32[]{:S(2)}) collective-permute-start(bf16[1792,128]{1,0:T(8,128)(2,1)S(1)} %get-tuple-element.69), channel_id=1, source_target_pairs={{0,48},{8,56},{16,32},{24,40},{32,16},{40,24},{48,0},{56,8},{64,11... | collective-permute-start | bytes 1376264 | tf_op jit(solution)/shard_map/ppermute | solution.py:28
  13.5 3.8 %collective-permute-start.4 = (bf16[1792,128]{1,0:T(8,128)(2,1)S(1)}, bf16[1792,128]{1,0:T(8,128)(2,1)S(1)}, u32[]{:S(2)}, u32[]{:S(2)}) collective-permute-start(bf16[1792,128]{1,0:T(8,128)(2,1)S(1)} %get-tuple-element.69), channel_id=1, source_target_pairs={{0,64},{8,72},{16,80},{24,88},{32,96},{40,104},{48,112},{56,120},{... | collective-permute-start | bytes 1376264 | tf_op jit(solution)/shard_map/ppermute | solution.py:28
  18.1 1.9 %collective-permute-start.1 = (bf16[2,16,1024]{2,1,0:T(8,128)(2,1)S(1)}, bf16[2,16,1024]{2,1,0:T(8,128)(2,1)S(1)}, u32[]{:S(2)}, u32[]{:S(2)}) collective-permute-start(bf16[2,16,1024]{2,1,0:T(8,128)(2,1)S(1)} %get-tuple-element.66), channel_id=1, source_target_pairs={{0,16},{8,24},{16,0},{24,8},{32,48},{40,56},{48,32},{56,40},{64,80... | collective-permute-start | bytes 196616 | tf_op jit(solution)/shard_map/ppermute | solution.py:28
  20.0 2.2 %collective-permute-start.2 = (bf16[2,16,1024]{2,1,0:T(8,128)(2,1)S(1)}, bf16[2,16,1024]{2,1,0:T(8,128)(2,1)S(1)}, u32[]{:S(2)}, u32[]{:S(2)}) collective-permute-start(bf16[2,16,1024]{2,1,0:T(8,128)(2,1)S(1)} %get-tuple-element.67), channel_id=1, source_target_pairs={{0,128},{8,136},{16,144},{24,152},{32,160},{40,168},{48,176},{56,1... | collective-permute-start | bytes 196616 | tf_op jit(solution)/shard_map/ppermute | solution.py:28
  22.3 3.5 %collective-permute-start.3 = (bf16[2,16,1024]{2,1,0:T(8,128)(2,1)S(1)}, bf16[2,16,1024]{2,1,0:T(8,128)(2,1)S(1)}, u32[]{:S(2)}, u32[]{:S(2)}) collective-permute-start(bf16[2,16,1024]{2,1,0:T(8,128)(2,1)S(1)} %get-tuple-element.68), channel_id=1, source_target_pairs={{0,144},{8,152},{16,128},{24,136},{32,176},{40,184},{48,160},{56,1... | collective-permute-start | bytes 196616 | tf_op jit(solution)/shard_map/ppermute | solution.py:28
  25.8 3.5 %collective-permute-done.2.refs_2_ = bf16[2,16,1024]{2,1,0:T(8,128)(2,1)S(1)} collective-permute-done((bf16[2,16,1024]{2,1,0:T(8,128)(2,1)S(1)}, bf16[2,16,1024]{2,1,0:T(8,128)(2,1)S(1)}, u32[]{:S(2)}, u32[]{:S(2)}) %collective-permute-start.2) | collective-permute-done | bytes 65568 | tf_op jit(solution)/shard_map/ppermute | solution.py:28
  30.1 1.6 %collective-permute-done.4.refs_5_.refs_2_ = bf16[1792,128]{1,0:T(8,128)(2,1)S(1)} collective-permute-done((bf16[1792,128]{1,0:T(8,128)(2,1)S(1)}, bf16[1792,128]{1,0:T(8,128)(2,1)S(1)}, u32[]{:S(2)}, u32[]{:S(2)}) %collective-permute-start.4) | collective-permute-done | bytes 458784 | tf_op jit(solution)/shard_map/ppermute | solution.py:28
  31.7 1.7 %collective-permute-start.10 = (bf16[1792,128]{1,0:T(8,128)(2,1)S(1)}, bf16[1792,128]{1,0:T(8,128)(2,1)S(1)}, u32[]{:S(2)}, u32[]{:S(2)}) collective-permute-start(bf16[1792,128]{1,0:T(8,128)(2,1)S(1)} %get-tuple-element.74), channel_id=1, source_target_pairs={{0,48},{8,56},{16,32},{24,40},{32,16},{40,24},{48,0},{56,8},{64,11... | collective-permute-start | bytes 1376264 | tf_op jit(solution)/shard_map/ppermute | solution.py:28
  33.4 1.9 %collective-permute-start.11 = (bf16[128,1408]{1,0:T(8,128)(2,1)S(1)}, bf16[128,1408]{1,0:T(8,128)(2,1)S(1)}, u32[]{:S(2)}, u32[]{:S(2)}) collective-permute-start(bf16[128,1408]{1,0:T(8,128)(2,1)S(1)} %get-tuple-element.75), channel_id=1, source_target_pairs={{0,16},{8,24},{16,0},{24,8},{32,48},{40,56},{48,32},{56,40},{64,80... | collective-permute-start | bytes 1081352 | tf_op jit(solution)/shard_map/ppermute | solution.py:28
  38.3 2.1 %collective-permute-start.8 = (bf16[4,16,1024]{2,1,0:T(8,128)(2,1)S(1)}, bf16[4,16,1024]{2,1,0:T(8,128)(2,1)S(1)}, u32[]{:S(2)}, u32[]{:S(2)}) collective-permute-start(bf16[4,16,1024]{2,1,0:T(8,128)(2,1)S(1)} %get-tuple-element.72.far_ref), channel_id=1, source_target_pairs={{0,6},{1,7},{2,4},{3,5},{4,2},{5,3},{6,0},{7,1},{8,14},{9,15},{10,... | collective-permute-start | bytes 393224 | tf_op jit(solution)/shard_map/ppermute | solution.py:28
  41.7 2.7 %collective-permute-done.8.far_x = bf16[4,16,1024]{2,1,0:T(8,128)(2,1)S(1)} collective-permute-done((bf16[4,16,1024]{2,1,0:T(8,128)(2,1)S(1)}, bf16[4,16,1024]{2,1,0:T(8,128)(2,1)S(1)}, u32[]{:S(2)}, u32[]{:S(2)}) %collective-permute-start.8) | collective-permute-done | bytes 131104 | tf_op jit(solution)/shard_map/ppermute | solution.py:28
  46.8 2.1 %collective-permute-start.12 = (bf16[2,4,16,1024]{3,2,1,0:T(8,128)(2,1)S(1)}, bf16[2,4,16,1024]{3,2,1,0:T(8,128)(2,1)S(1)}, u32[]{:S(2)}, u32[]{:S(2)}) collective-permute-start(bf16[2,4,16,1024]{3,2,1,0:T(8,128)(2,1)S(1)} %get-tuple-element.76.refs_1_), channel_id=1, source_target_pairs={{0,6},{1,7},{2,4},{3,5},{4,2},{5,3},{6,0},{7,1},{8,14},{9,15},{10,... | collective-permute-start | bytes 786440 | tf_op jit(solution)/shard_map/ppermute | solution.py:28
  50.0 2.1 %shard_map.71 = (bf16[128,1792]{1,0:T(8,128)(2,1)S(1)}, bf16[128,1792]{1,0:T(8,128)(2,1)S(1)}, bf16[128,1792]{1,0:T(8,128)(2,1)S(1)}, bf16[128,1792]{1,0:T(8,128...) custom-call(bf16[128,1408]{1,0:T(8,128)(2,1)S(1)} %copy-done.4, ...), custom_call_target="tpu_custom_call" | custom-call | flops 3000000000 | bytes 1 | tf_op jit(solution)/shard_map/pallas_call | solution.py:331
  52.1 5.1 %collective-permute-done.14.refs_0_ = bf16[128,1408]{1,0:T(8,128)(2,1)} collective-permute-done((bf16[128,1408]{1,0:T(8,128)(2,1)}, bf16[128,1408]{1,0:T(8,128)(2,1)}, u32[]{:S(2)}, u32[]{:S(2)}) %collective-permute-start.14) | collective-permute-done | bytes 360480 | tf_op jit(solution)/shard_map/ppermute | solution.py:28
  57.3 1.7 %shard_map.72 = (bf16[128,1792]{1,0:T(8,128)(2,1)S(1)}, bf16[128,1792]{1,0:T(8,128)(2,1)S(1)}, bf16[128,1792]{1,0:T(8,128)(2,1)S(1)}) custom-call(bf16[128,1408]{1,0:T(8,128)(2,1)} %collective-permute-done.14.refs_0_), custom_call_target="tpu_custom_call" | custom-call | flops 1 | bytes 1 | tf_op jit(solution)/shard_map/pallas_call | solution.py:331
  59.0 3.7 %shard_map.73 = (bf16[4,16,1024]{2,1,0:T(8,128)(2,1)S(1)}, bf16[4,16,1024]{2,1,0:T(8,128)(2,1)S(1)}, bf16[2,4,16,1024]{3,2,1,0:T(8,128)(2,1)S(1)}, bf16[4,16,102...) custom-call(s32[1]{0:T(128)} %bitcast.1.place_ref.refs_0_, ...), custom_call_target="tpu_custom_call" | custom-call | flops 1 | bytes 1 | tf_op jit(solution)/shard_map/pallas_call | solution.py:331
  62.7 2.2 %shard_map.74 = (bf16[4,1792,128]{2,1,0:T(8,128)(2,1)S(1)}, bf16[4,1792,128]{2,1,0:T(8,128)(2,1)S(1)}, bf16[512,1024]{1,0:T(8,128)(2,1)S(1)}) custom-call(s32[1]{0:T(128)} %bitcast.1.place_ref.refs_0_, bf16[2,4,16,1024]{3,2,1,0:T(8,128)(2,1)S(1)} %get-tuple-element.76.refs_1_, bf16[2,4,16,1024]{3,2,1,0:T(8,128)(2,1)S(1)} %collective-permute-done.12.refs_2_, ...), custom_call_target="tpu_custom_call" | custom-call | flops 5000000000 | bytes 1 | tf_op jit(solution)/shard_map/pallas_call | solution.py:331
  65.1 2.2 %collective-permute-start.18 = (bf16[2,4,16,1024]{3,2,1,0:T(8,128)(2,1)S(1)}, bf16[2,4,16,1024]{3,2,1,0:T(8,128)(2,1)S(1)}, u32[]{:S(2)}, u32[]{:S(2)}) collective-permute-start(bf16[2,4,16,1024]{3,2,1,0:T(8,128)(2,1)S(1)} %get-tuple-element.99), channel_id=1, source_target_pairs={{0,6},{1,7},{2,4},{3,5},{4,2},{5,3},{6,0},{7,1},{8,14},{9,15},{10,... | collective-permute-start | bytes 786440 | tf_op jit(solution)/shard_map/ppermute | solution.py:28
  67.3 5.0 %shard_map.75 = (bf16[128,1792]{1,0:T(8,128)(2,1)S(1)}, bf16[128,896]{1,0:T(8,128)(2,1)S(1)}, bf16[2,80,896]{2,1,0:T(8,128)(2,1)S(1)}, bf16[2,48,896]{2,1,0:T(8,128)(2,1)S(1)}) custom-call(bf16[512,1024]{1,0:T(8,128)(2,1)S(1)} %get-tuple-element.87.rows_ref, bf16[4,1792,128]{2,1,0:T(8,128)(2,1)S(1)} %get-tuple-element.83.refs_4_.mine_ref, ...), custom_call_target="tpu_custom_call" | custom-call | flops 5000000000 | bytes 1 | tf_op jit(solution)/shard_map/pallas_call | solution.py:331
  75.4 1.9 %collective-permute-start.19 = (bf16[2,1120,128]{2,1,0:T(8,128)(2,1)S(1)}, bf16[2,1120,128]{2,1,0:T(8,128)(2,1)S(1)}, u32[]{:S(2)}, u32[]{:S(2)}) collective-permute-start(bf16[2,1120,128]{2,1,0:T(8,128)(2,1)S(1)} %get-tuple-element.101), channel_id=1, source_target_pairs={{0,48},{8,56},{16,32},{24,40},{32,16},{40,24},{48,0},{56,8},{64,11... | collective-permute-start | bytes 1720328 | tf_op jit(solution)/shard_map/ppermute | solution.py:28
  77.9 2.1 %collective-permute-start.21 = (bf16[4,16,1024]{2,1,0:T(8,128)(2,1)S(1)}, bf16[4,16,1024]{2,1,0:T(8,128)(2,1)S(1)}, u32[]{:S(2)}, u32[]{:S(2)}) collective-permute-start(bf16[4,16,1024]{2,1,0:T(8,128)(2,1)S(1)} %get-tuple-element.105), channel_id=1, source_target_pairs={{0,6},{1,7},{2,4},{3,5},{4,2},{5,3},{6,0},{7,1},{8,14},{9,15},{10,... | collective-permute-start | bytes 393224 | tf_op jit(solution)/shard_map/ppermute | solution.py:28
  80.0 1.6 %collective-permute-start.20 = (bf16[2,80,896]{2,1,0:T(8,128)(2,1)S(1)}, bf16[2,80,896]{2,1,0:T(8,128)(2,1)S(1)}, u32[]{:S(2)}, u32[]{:S(2)}) collective-permute-start(bf16[2,80,896]{2,1,0:T(8,128)(2,1)S(1)} %get-tuple-element.103), channel_id=1, source_target_pairs={{0,16},{8,24},{16,0},{24,8},{32,48},{40,56},{48,32},{56,40},{64,80... | collective-permute-start | bytes 860168 | tf_op jit(solution)/shard_map/ppermute | solution.py:28
  82.3 5.4 %collective-permute-start.23 = (bf16[4,16,1024]{2,1,0:T(8,128)(2,1)S(1)}, bf16[4,16,1024]{2,1,0:T(8,128)(2,1)S(1)}, u32[]{:S(2)}, u32[]{:S(2)}) collective-permute-start(bf16[4,16,1024]{2,1,0:T(8,128)(2,1)S(1)} %add_convert_fusion), channel_id=1, source_target_pairs={{0,1},{1,0},{2,3},{3,2},{4,5},{5,4},{6,7},{7,6},{8,9},{9,8},{10,11... | collective-permute-start | bytes 393224 | tf_op jit(solution)/shard_map/ppermute | solution.py:28
  87.8 5.2 %collective-permute-done.23.second_ref = bf16[4,16,1024]{2,1,0:T(8,128)(2,1)S(1)} collective-permute-done((bf16[4,16,1024]{2,1,0:T(8,128)(2,1)S(1)}, bf16[4,16,1024]{2,1,0:T(8,128)(2,1)S(1)}, u32[]{:S(2)}, u32[]{:S(2)}) %collective-permute-start.23) | collective-permute-done | bytes 131104 | tf_op jit(solution)/shard_map/ppermute | solution.py:28
  93.2 4.8 %collective-permute-start.25 = (bf16[1120,128]{1,0:T(8,128)(2,1)S(1)}, bf16[1120,128]{1,0:T(8,128)(2,1)S(1)}, u32[]{:S(2)}, u32[]{:S(2)}) collective-permute-start(bf16[1120,128]{1,0:T(8,128)(2,1)S(1)} %get-tuple-element.111), channel_id=1, source_target_pairs={{0,64},{8,72},{16,80},{24,88},{32,96},{40,104},{48,112},{56,120},{... | collective-permute-start | bytes 860168 | tf_op jit(solution)/shard_map/ppermute | solution.py:28
  98.0 2.5 %collective-permute-start.26 = (bf16[2,48,896]{2,1,0:T(8,128)(2,1)S(1)}, bf16[2,48,896]{2,1,0:T(8,128)(2,1)S(1)}, u32[]{:S(2)}, u32[]{:S(2)}) collective-permute-start(bf16[2,48,896]{2,1,0:T(8,128)(2,1)S(1)} %get-tuple-element.112), channel_id=1, source_target_pairs={{0,16},{8,24},{16,0},{24,8},{32,48},{40,56},{48,32},{56,40},{64,80... | collective-permute-start | bytes 516104 | tf_op jit(solution)/shard_map/ppermute | solution.py:28
  100.5 4.2 %collective-permute-done.27.arrived_ref.refs_13_ = bf16[2,16,1024]{2,1,0:T(8,128)(2,1)S(1)} collective-permute-done((bf16[2,16,1024]{2,1,0:T(8,128)(2,1)S(1)}, bf16[2,16,1024]{2,1,0:T(8,128)(2,1)S(1)}, u32[]{:S(2)}, u32[]{:S(2)}) %collective-permute-start.27) | collective-permute-done | bytes 65568 | tf_op jit(solution)/shard_map/ppermute | solution.py:28
  104.8 3.4 %collective-permute-done.28.refs_1_.refs_8_ = bf16[80,896]{1,0:T(8,128)(2,1)S(1)} collective-permute-done((bf16[80,896]{1,0:T(8,128)(2,1)S(1)}, bf16[80,896]{1,0:T(8,128)(2,1)S(1)}, u32[]{:S(2)}, u32[]{:S(2)}) %collective-permute-start.28) | collective-permute-done | bytes 143392 | tf_op jit(solution)/shard_map/ppermute | solution.py:28
  108.3 2.9 %collective-permute-start.30 = (bf16[48,896]{1,0:T(8,128)(2,1)S(1)}, bf16[48,896]{1,0:T(8,128)(2,1)S(1)}, u32[]{:S(2)}, u32[]{:S(2)}) collective-permute-start(bf16[48,896]{1,0:T(8,128)(2,1)S(1)} %get-tuple-element.118), channel_id=1, source_target_pairs={{0,128},{8,136},{16,144},{24,152},{32,160},{40,168},{48,176},{56,1... | collective-permute-start | bytes 258056 | tf_op jit(solution)/shard_map/ppermute | solution.py:28
  111.4 6.7 %collective-permute-done.31.refs_14_ = bf16[2,16,1024]{2,1,0:T(8,128)(2,1)S(1)} collective-permute-done((bf16[2,16,1024]{2,1,0:T(8,128)(2,1)S(1)}, bf16[2,16,1024]{2,1,0:T(8,128)(2,1)S(1)}, u32[]{:S(2)}, u32[]{:S(2)}) %collective-permute-start.31) | collective-permute-done | bytes 65568 | tf_op jit(solution)/shard_map/ppermute | solution.py:28
  118.1 1.8 %shard_map.79 = (bf16[1792,128]{1,0:T(8,128)(2,1)}, bf16[128,1792]{1,0:T(8,128)(2,1)}, bf16[16,4096]{1,0:T(8,128)(2,1)}) custom-call(s32[1]{0:T(128)} %bitcast.place_ref, f32[2,1792,128]{2,1,0:T(8,128)S(1)} %get-tuple-element.100.sum_ref.refs_0_, bf16[2,1120,128]{2,1,0:T(8,128)(2,1)S(1)} %collective-permute-done.19.far0_ref.refs_1_, ...), custom_call_target="tpu_custom_call" | custom-call | flops 1 | bytes 1 | tf_op jit(solution)/shard_map/pallas_call | solution.py:331
  (66 shorter events, 18.5 us)
Async XLA Ops:
  0.6 11.1 %collective-permute-start = (bf16[16,4096]{1,0:T(8,128)(2,1)}, bf16[16,4096]{1,0:T(8,128)(2,1)S(1)}, u32[]{:S(2)}, u32[]{:S(2)}) collective-permute-start(bf16[16,4096]{1,0:T(8,128)(2,1)} %grad_ref.1), channel_id=1, source_target_pairs={{0,1},{1,0},{2,3},{3,2},{4,5},{5,4},{6,7},{7,6},{8,9},{9,8},{10,11... | collective-permute-start | bytes 393224 | tf_op jit(solution)/shard_map/ppermute | solution.py:28
  11.8 18.2 %collective-permute-start.6 = (bf16[1792,128]{1,0:T(8,128)(2,1)S(1)}, bf16[1792,128]{1,0:T(8,128)(2,1)S(1)}, u32[]{:S(2)}, u32[]{:S(2)}) collective-permute-start(bf16[1792,128]{1,0:T(8,128)(2,1)S(1)} %get-tuple-element.69), channel_id=1, source_target_pairs={{0,48},{8,56},{16,32},{24,40},{32,16},{40,24},{48,0},{56,8},{64,11... | collective-permute-start | bytes 1376264 | tf_op jit(solution)/shard_map/ppermute | solution.py:28
  13.5 18.2 %collective-permute-start.4 = (bf16[1792,128]{1,0:T(8,128)(2,1)S(1)}, bf16[1792,128]{1,0:T(8,128)(2,1)S(1)}, u32[]{:S(2)}, u32[]{:S(2)}) collective-permute-start(bf16[1792,128]{1,0:T(8,128)(2,1)S(1)} %get-tuple-element.69), channel_id=1, source_target_pairs={{0,64},{8,72},{16,80},{24,88},{32,96},{40,104},{48,112},{56,120},{... | collective-permute-start | bytes 1376264 | tf_op jit(solution)/shard_map/ppermute | solution.py:28
  17.3 12.7 %collective-permute-start.5 = (bf16[64,1408]{1,0:T(8,128)(2,1)S(1)}, bf16[64,1408]{1,0:T(8,128)(2,1)S(1)}, u32[]{:S(2)}, u32[]{:S(2)}) collective-permute-start(bf16[64,1408]{1,0:T(8,128)(2,1)S(1)} %get-tuple-element.70), channel_id=1, source_target_pairs={{0,128},{8,136},{16,144},{24,152},{32,160},{40,168},{48,176},{56,1... | collective-permute-start | bytes 540680 | tf_op jit(solution)/shard_map/ppermute | solution.py:28
  18.1 4.3 %collective-permute-start.1 = (bf16[2,16,1024]{2,1,0:T(8,128)(2,1)S(1)}, bf16[2,16,1024]{2,1,0:T(8,128)(2,1)S(1)}, u32[]{:S(2)}, u32[]{:S(2)}) collective-permute-start(bf16[2,16,1024]{2,1,0:T(8,128)(2,1)S(1)} %get-tuple-element.66), channel_id=1, source_target_pairs={{0,16},{8,24},{16,0},{24,8},{32,48},{40,56},{48,32},{56,40},{64,80... | collective-permute-start | bytes 196616 | tf_op jit(solution)/shard_map/ppermute | solution.py:28
  20.0 9.4 %collective-permute-start.2 = (bf16[2,16,1024]{2,1,0:T(8,128)(2,1)S(1)}, bf16[2,16,1024]{2,1,0:T(8,128)(2,1)S(1)}, u32[]{:S(2)}, u32[]{:S(2)}) collective-permute-start(bf16[2,16,1024]{2,1,0:T(8,128)(2,1)S(1)} %get-tuple-element.67), channel_id=1, source_target_pairs={{0,128},{8,136},{16,144},{24,152},{32,160},{40,168},{48,176},{56,1... | collective-permute-start | bytes 196616 | tf_op jit(solution)/shard_map/ppermute | solution.py:28
  22.3 7.7 %collective-permute-start.3 = (bf16[2,16,1024]{2,1,0:T(8,128)(2,1)S(1)}, bf16[2,16,1024]{2,1,0:T(8,128)(2,1)S(1)}, u32[]{:S(2)}, u32[]{:S(2)}) collective-permute-start(bf16[2,16,1024]{2,1,0:T(8,128)(2,1)S(1)} %get-tuple-element.68), channel_id=1, source_target_pairs={{0,144},{8,152},{16,128},{24,136},{32,176},{40,184},{48,160},{56,1... | collective-permute-start | bytes 196616 | tf_op jit(solution)/shard_map/ppermute | solution.py:28
  31.7 12.7 %collective-permute-start.10 = (bf16[1792,128]{1,0:T(8,128)(2,1)S(1)}, bf16[1792,128]{1,0:T(8,128)(2,1)S(1)}, u32[]{:S(2)}, u32[]{:S(2)}) collective-permute-start(bf16[1792,128]{1,0:T(8,128)(2,1)S(1)} %get-tuple-element.74), channel_id=1, source_target_pairs={{0,48},{8,56},{16,32},{24,40},{32,16},{40,24},{48,0},{56,8},{64,11... | collective-permute-start | bytes 1376264 | tf_op jit(solution)/shard_map/ppermute | solution.py:28
  33.4 11.0 %collective-permute-start.11 = (bf16[128,1408]{1,0:T(8,128)(2,1)S(1)}, bf16[128,1408]{1,0:T(8,128)(2,1)S(1)}, u32[]{:S(2)}, u32[]{:S(2)}) collective-permute-start(bf16[128,1408]{1,0:T(8,128)(2,1)S(1)} %get-tuple-element.75), channel_id=1, source_target_pairs={{0,16},{8,24},{16,0},{24,8},{32,48},{40,56},{48,32},{56,40},{64,80... | collective-permute-start | bytes 1081352 | tf_op jit(solution)/shard_map/ppermute | solution.py:28
  35.3 9.2 %collective-permute-start.9 = (bf16[64,1408]{1,0:T(8,128)(2,1)S(1)}, bf16[64,1408]{1,0:T(8,128)(2,1)S(1)}, u32[]{:S(2)}, u32[]{:S(2)}) collective-permute-start(bf16[64,1408]{1,0:T(8,128)(2,1)S(1)} %get-tuple-element.73), channel_id=1, source_target_pairs={{0,128},{8,136},{16,144},{24,152},{32,160},{40,168},{48,176},{56,1... | collective-permute-start | bytes 540680 | tf_op jit(solution)/shard_map/ppermute | solution.py:28
  36.8 5.0 %collective-permute-start.7 = (bf16[4,16,1024]{2,1,0:T(8,128)(2,1)S(1)}, bf16[4,16,1024]{2,1,0:T(8,128)(2,1)S(1)}, u32[]{:S(2)}, u32[]{:S(2)}) collective-permute-start(bf16[4,16,1024]{2,1,0:T(8,128)(2,1)S(1)} %get-tuple-element.71.near_ref), channel_id=1, source_target_pairs={{0,2},{1,3},{2,0},{3,1},{4,6},{5,7},{6,4},{7,5},{8,10},{9,11},{10,... | collective-permute-start | bytes 393224 | tf_op jit(solution)/shard_map/ppermute | solution.py:28
  38.3 6.2 %collective-permute-start.8 = (bf16[4,16,1024]{2,1,0:T(8,128)(2,1)S(1)}, bf16[4,16,1024]{2,1,0:T(8,128)(2,1)S(1)}, u32[]{:S(2)}, u32[]{:S(2)}) collective-permute-start(bf16[4,16,1024]{2,1,0:T(8,128)(2,1)S(1)} %get-tuple-element.72.far_ref), channel_id=1, source_target_pairs={{0,6},{1,7},{2,4},{3,5},{4,2},{5,3},{6,0},{7,1},{8,14},{9,15},{10,... | collective-permute-start | bytes 393224 | tf_op jit(solution)/shard_map/ppermute | solution.py:28
  46.1 12.8 %collective-permute-start.15 = (bf16[4,1792,128]{2,1,0:T(8,128)(2,1)S(1)}, bf16[4,1792,128]{2,1,0:T(8,128)(2,1)}, u32[]{:S(2)}, u32[]{:S(2)}) collective-permute-start(bf16[4,1792,128]{2,1,0:T(8,128)(2,1)S(1)} %get-tuple-element.83.refs_4_.mine_ref), channel_id=1, source_target_pairs={{0,8},{8,0},{16,24},{24,16},{32,40},{40,32},{48,56},{56,48},{64,72... | collective-permute-start | bytes 5505032 | tf_op jit(solution)/shard_map/ppermute | solution.py:28
  46.1 11.1 %collective-permute-start.14 = (bf16[128,1408]{1,0:T(8,128)(2,1)}, bf16[128,1408]{1,0:T(8,128)(2,1)}, u32[]{:S(2)}, u32[]{:S(2)}) collective-permute-start(bf16[128,1408]{1,0:T(8,128)(2,1)} %get-tuple-element.79.refs_1_), channel_id=1, source_target_pairs={{0,16},{8,24},{16,0},{24,8},{32,48},{40,56},{48,32},{56,40},{64,80... | collective-permute-start | bytes 1081352 | tf_op jit(solution)/shard_map/ppermute | solution.py:28
  46.8 15.8 %collective-permute-start.12 = (bf16[2,4,16,1024]{3,2,1,0:T(8,128)(2,1)S(1)}, bf16[2,4,16,1024]{3,2,1,0:T(8,128)(2,1)S(1)}, u32[]{:S(2)}, u32[]{:S(2)}) collective-permute-start(bf16[2,4,16,1024]{3,2,1,0:T(8,128)(2,1)S(1)} %get-tuple-element.76.refs_1_), channel_id=1, source_target_pairs={{0,6},{1,7},{2,4},{3,5},{4,2},{5,3},{6,0},{7,1},{8,14},{9,15},{10,... | collective-permute-start | bytes 786440 | tf_op jit(solution)/shard_map/ppermute | solution.py:28
  48.9 13.7 %collective-permute-start.13 = (bf16[2,4,16,1024]{3,2,1,0:T(8,128)(2,1)}, bf16[2,4,16,1024]{3,2,1,0:T(8,128)(2,1)S(1)}, u32[]{:S(2)}, u32[]{:S(2)}) collective-permute-start(bf16[2,4,16,1024]{3,2,1,0:T(8,128)(2,1)} %copy-done.7), channel_id=1, source_target_pairs={{0,2},{1,3},{2,0},{3,1},{4,6},{5,7},{6,4},{7,5},{8,10},{9,11},{10,... | collective-permute-start | bytes 786440 | tf_op jit(solution)/shard_map/ppermute | solution.py:28
  64.9 10.0 %collective-permute-start.16 = (bf16[4,1792,128]{2,1,0:T(8,128)(2,1)S(1)}, bf16[4,1792,128]{2,1,0:T(8,128)(2,1)S(1)}, u32[]{:S(2)}, u32[]{:S(2)}) collective-permute-start(bf16[4,1792,128]{2,1,0:T(8,128)(2,1)S(1)} %get-tuple-element.86), channel_id=1, source_target_pairs={{0,8},{8,0},{16,24},{24,16},{32,40},{40,32},{48,56},{56,48},{64,72... | collective-permute-start | bytes 5505032 | tf_op jit(solution)/shard_map/ppermute | solution.py:28
  65.0 8.7 %collective-permute-start.17 = (bf16[2,4,16,1024]{3,2,1,0:T(8,128)(2,1)S(1)}, bf16[2,4,16,1024]{3,2,1,0:T(8,128)(2,1)S(1)}, u32[]{:S(2)}, u32[]{:S(2)}) collective-permute-start(bf16[2,4,16,1024]{3,2,1,0:T(8,128)(2,1)S(1)} %get-tuple-element.96), channel_id=1, source_target_pairs={{0,2},{1,3},{2,0},{3,1},{4,6},{5,7},{6,4},{7,5},{8,10},{9,11},{10,... | collective-permute-start | bytes 786440 | tf_op jit(solution)/shard_map/ppermute | solution.py:28
  65.1 9.8 %collective-permute-start.18 = (bf16[2,4,16,1024]{3,2,1,0:T(8,128)(2,1)S(1)}, bf16[2,4,16,1024]{3,2,1,0:T(8,128)(2,1)S(1)}, u32[]{:S(2)}, u32[]{:S(2)}) collective-permute-start(bf16[2,4,16,1024]{3,2,1,0:T(8,128)(2,1)S(1)} %get-tuple-element.99), channel_id=1, source_target_pairs={{0,6},{1,7},{2,4},{3,5},{4,2},{5,3},{6,0},{7,1},{8,14},{9,15},{10,... | collective-permute-start | bytes 786440 | tf_op jit(solution)/shard_map/ppermute | solution.py:28
  75.4 17.5 %collective-permute-start.19 = (bf16[2,1120,128]{2,1,0:T(8,128)(2,1)S(1)}, bf16[2,1120,128]{2,1,0:T(8,128)(2,1)S(1)}, u32[]{:S(2)}, u32[]{:S(2)}) collective-permute-start(bf16[2,1120,128]{2,1,0:T(8,128)(2,1)S(1)} %get-tuple-element.101), channel_id=1, source_target_pairs={{0,48},{8,56},{16,32},{24,40},{32,16},{40,24},{48,0},{56,8},{64,11... | collective-permute-start | bytes 1720328 | tf_op jit(solution)/shard_map/ppermute | solution.py:28
  77.3 5.0 %collective-permute-start.22 = (bf16[4,16,1024]{2,1,0:T(8,128)(2,1)S(1)}, bf16[4,16,1024]{2,1,0:T(8,128)(2,1)S(1)}, u32[]{:S(2)}, u32[]{:S(2)}) collective-permute-start(bf16[4,16,1024]{2,1,0:T(8,128)(2,1)S(1)} %get-tuple-element.107), channel_id=1, source_target_pairs={{0,2},{1,3},{2,0},{3,1},{4,6},{5,7},{6,4},{7,5},{8,10},{9,11},{10,... | collective-permute-start | bytes 393224 | tf_op jit(solution)/shard_map/ppermute | solution.py:28
  77.9 9.9 %collective-permute-start.21 = (bf16[4,16,1024]{2,1,0:T(8,128)(2,1)S(1)}, bf16[4,16,1024]{2,1,0:T(8,128)(2,1)S(1)}, u32[]{:S(2)}, u32[]{:S(2)}) collective-permute-start(bf16[4,16,1024]{2,1,0:T(8,128)(2,1)S(1)} %get-tuple-element.105), channel_id=1, source_target_pairs={{0,6},{1,7},{2,4},{3,5},{4,2},{5,3},{6,0},{7,1},{8,14},{9,15},{10,... | collective-permute-start | bytes 393224 | tf_op jit(solution)/shard_map/ppermute | solution.py:28
  80.0 12.9 %collective-permute-start.20 = (bf16[2,80,896]{2,1,0:T(8,128)(2,1)S(1)}, bf16[2,80,896]{2,1,0:T(8,128)(2,1)S(1)}, u32[]{:S(2)}, u32[]{:S(2)}) collective-permute-start(bf16[2,80,896]{2,1,0:T(8,128)(2,1)S(1)} %get-tuple-element.103), channel_id=1, source_target_pairs={{0,16},{8,24},{16,0},{24,8},{32,48},{40,56},{48,32},{56,40},{64,80... | collective-permute-start | bytes 860168 | tf_op jit(solution)/shard_map/ppermute | solution.py:28
  82.3 10.6 %collective-permute-start.23 = (bf16[4,16,1024]{2,1,0:T(8,128)(2,1)S(1)}, bf16[4,16,1024]{2,1,0:T(8,128)(2,1)S(1)}, u32[]{:S(2)}, u32[]{:S(2)}) collective-permute-start(bf16[4,16,1024]{2,1,0:T(8,128)(2,1)S(1)} %add_convert_fusion), channel_id=1, source_target_pairs={{0,1},{1,0},{2,3},{3,2},{4,5},{5,4},{6,7},{7,6},{8,9},{9,8},{10,11... | collective-permute-start | bytes 393224 | tf_op jit(solution)/shard_map/ppermute | solution.py:28
  93.1 15.1 %collective-permute-start.24 = (bf16[2,672,128]{2,1,0:T(8,128)(2,1)S(1)}, bf16[2,672,128]{2,1,0:T(8,128)(2,1)S(1)}, u32[]{:S(2)}, u32[]{:S(2)}) collective-permute-start(bf16[2,672,128]{2,1,0:T(8,128)(2,1)S(1)} %get-tuple-element.110), channel_id=1, source_target_pairs={{0,48},{8,56},{16,32},{24,40},{32,16},{40,24},{48,0},{56,8},{64,11... | collective-permute-start | bytes 1032200 | tf_op jit(solution)/shard_map/ppermute | solution.py:28
  93.2 15.0 %collective-permute-start.25 = (bf16[1120,128]{1,0:T(8,128)(2,1)S(1)}, bf16[1120,128]{1,0:T(8,128)(2,1)S(1)}, u32[]{:S(2)}, u32[]{:S(2)}) collective-permute-start(bf16[1120,128]{1,0:T(8,128)(2,1)S(1)} %get-tuple-element.111), channel_id=1, source_target_pairs={{0,64},{8,72},{16,80},{24,88},{32,96},{40,104},{48,112},{56,120},{... | collective-permute-start | bytes 860168 | tf_op jit(solution)/shard_map/ppermute | solution.py:28
  98.0 10.2 %collective-permute-start.26 = (bf16[2,48,896]{2,1,0:T(8,128)(2,1)S(1)}, bf16[2,48,896]{2,1,0:T(8,128)(2,1)S(1)}, u32[]{:S(2)}, u32[]{:S(2)}) collective-permute-start(bf16[2,48,896]{2,1,0:T(8,128)(2,1)S(1)} %get-tuple-element.112), channel_id=1, source_target_pairs={{0,16},{8,24},{16,0},{24,8},{32,48},{40,56},{48,32},{56,40},{64,80... | collective-permute-start | bytes 516104 | tf_op jit(solution)/shard_map/ppermute | solution.py:28
  100.5 7.7 %collective-permute-start.28 = (bf16[80,896]{1,0:T(8,128)(2,1)S(1)}, bf16[80,896]{1,0:T(8,128)(2,1)S(1)}, u32[]{:S(2)}, u32[]{:S(2)}) collective-permute-start(bf16[80,896]{1,0:T(8,128)(2,1)S(1)} %get-tuple-element.115), channel_id=1, source_target_pairs={{0,128},{8,136},{16,144},{24,152},{32,160},{40,168},{48,176},{56,1... | collective-permute-start | bytes 430088 | tf_op jit(solution)/shard_map/ppermute | solution.py:28
  100.5 4.3 %collective-permute-start.27 = (bf16[2,16,1024]{2,1,0:T(8,128)(2,1)S(1)}, bf16[2,16,1024]{2,1,0:T(8,128)(2,1)S(1)}, u32[]{:S(2)}, u32[]{:S(2)}) collective-permute-start(bf16[2,16,1024]{2,1,0:T(8,128)(2,1)S(1)} %get-tuple-element.114), channel_id=1, source_target_pairs={{0,16},{8,24},{16,0},{24,8},{32,48},{40,56},{48,32},{56,40},{64,80... | collective-permute-start | bytes 196616 | tf_op jit(solution)/shard_map/ppermute | solution.py:28
  108.2 9.8 %collective-permute-start.29 = (bf16[672,128]{1,0:T(8,128)(2,1)S(1)}, bf16[672,128]{1,0:T(8,128)(2,1)S(1)}, u32[]{:S(2)}, u32[]{:S(2)}) collective-permute-start(bf16[672,128]{1,0:T(8,128)(2,1)S(1)} %get-tuple-element.116), channel_id=1, source_target_pairs={{0,64},{8,72},{16,80},{24,88},{32,96},{40,104},{48,112},{56,120},{... | collective-permute-start | bytes 516104 | tf_op jit(solution)/shard_map/ppermute | solution.py:28
  108.3 9.7 %collective-permute-start.30 = (bf16[48,896]{1,0:T(8,128)(2,1)S(1)}, bf16[48,896]{1,0:T(8,128)(2,1)S(1)}, u32[]{:S(2)}, u32[]{:S(2)}) collective-permute-start(bf16[48,896]{1,0:T(8,128)(2,1)S(1)} %get-tuple-element.118), channel_id=1, source_target_pairs={{0,128},{8,136},{16,144},{24,152},{32,160},{40,168},{48,176},{56,1... | collective-permute-start | bytes 258056 | tf_op jit(solution)/shard_map/ppermute | solution.py:28
  111.3 6.8 %collective-permute-start.31 = (bf16[2,16,1024]{2,1,0:T(8,128)(2,1)S(1)}, bf16[2,16,1024]{2,1,0:T(8,128)(2,1)S(1)}, u32[]{:S(2)}, u32[]{:S(2)}) collective-permute-start(bf16[2,16,1024]{2,1,0:T(8,128)(2,1)S(1)} %get-tuple-element.121), channel_id=1, source_target_pairs={{0,128},{8,136},{16,144},{24,152},{32,160},{40,168},{48,176},{56,1... | collective-permute-start | bytes 196616 | tf_op jit(solution)/shard_map/ppermute | solution.py:28
  (10 other events, 55.5 us)

commit v4 on v3

--- a/solution.py
+++ b/solution.py
@@ -21,7 +21,8 @@
 PACKED = 3 * 384 + 256
 KEPT = 3 * 256 + 128
 CHUNKS = ((0, 512, 0, 0), (512, 1024, 384, 256), (1024, 1536, 768, 512), (1536, 1792, 1152, 768))
-EARLY = 80
+EARLY = 64
+FIRST = 48
 
 
 def swap(array, axis, size, k):
@@ -170,7 +171,7 @@
     for n, ref in enumerate(part_refs):
         near_ref[n] = ref[0]
         far_ref[n] = ref[1]
-    half_ref[...] = hidden_ref[half_ref.shape[0] :]
+    half_ref[...] = hidden_ref[hidden_ref.shape[0] - half_ref.shape[0] :]
     hidden_out[...] = hidden_ref[...]
     weight_out[...] = weight_z[...]
 
@@ -182,8 +183,8 @@
     near_out[1] = near_x[...]
     far_out[0] = far_ref[...]
     far_out[1] = far_x[...]
-    hidden_z[:64] = z0_ref[...]
-    hidden_z[64:] = z1_ref[...]
+    hidden_z[: z0_ref.shape[0]] = z0_ref[...]
+    hidden_z[z0_ref.shape[0] :] = z1_ref[...]
     for n, ref in enumerate(weight_refs):
         weights[n] = ref[...]
 
@@ -208,7 +209,7 @@
 
 def output_kernel(place_ref, *refs):
     hidden_refs, (mine_ref, far_ref) = refs[:4], refs[4:6]
-    first0, first3, first_send, second0, second1, second_send, rows_ref = refs[6:]
+    first0, first3, first_send, second0, second1, second_send, rows_ref = refs[-7:]
     hidden = jnp.concatenate([ref[...] for ref in hidden_refs], axis=0)
     for n in range(4):
         ref = (mine_ref, far_ref)[n // 2]
@@ -241,7 +242,7 @@
 
 
 def back_kernel(rows_ref, mine_ref, far_ref, *refs):
-    masks, (near_ref, z_ref, half0_ref, half1_ref, kept_ref) = refs[:6], refs[6:]
+    masks, (near_ref, z_ref, half0_ref, half1_ref, kept_ref) = refs[:6], refs[-5:]
     for low, high, _, to in CHUNKS:
         at = slice(low, high)
         weight = jnp.concatenate([ref[n, at, :] for ref in (mine_ref, far_ref) for n in range(4)], axis=1)
@@ -264,14 +265,8 @@
     return total
 
 
-def y_kernel(near_ref, far_ref, half0_ref, *refs):
-    first0, first3, first_far, second0, second1, second_far = refs[:6]
-    send0_ref, send1_ref, sum_ref, half0_out, first_sum, first_send, second_sum, second_send = refs[6:]
-    half0_out[...] = half0_ref[...]
-    first_sum[...] = added(first0[...], first_far[0])
-    first_send[...] = added(first3[...], first_far[1]).astype(BF16)
-    second_sum[...] = added(second0[...], second_far[0])
-    second_send[...] = added(second1[...], second_far[1]).astype(BF16)
+def core_kernel(near_ref, far_ref, *refs):
+    send0_ref, send1_ref, sum_ref = refs[-3:]
     middle = send0_ref.shape[1]
     for n in range(2):
         send = added(near_ref[2 * n + 1], far_ref[2 * n + 1]).astype(BF16)
@@ -280,34 +275,39 @@
         sum_ref[n] = added(near_ref[2 * n], far_ref[2 * n])
 
 
-def z0_kernel(sum_ref, far0_ref, back_ref, back0_ref, first_ref, first_far, second_ref, *refs):
+def x_kernel(first0, first3, first_far, second0, second1, second_far, *refs):
+    first_sum, first_send, second_sum, second_send = refs
+    first_sum[...] = added(first0[...], first_far[0])
+    first_send[...] = added(first3[...], first_far[1]).astype(BF16)
+    second_sum[...] = added(second0[...], second_far[0])
+    second_send[...] = added(second1[...], second_far[1]).astype(BF16)
+
+
+def z0_kernel(sum_ref, far0_ref, back_ref, back0_ref, first_ref, first_far, second_ref, second_far, *refs):
     weight1_ref, back1_ref = refs[:2]
-    weight_out, back_out, weight1_out, back1_out, total_ref, send_ref = refs[2:]
-    middle = far0_ref.shape[1]
-    weight_out[...] = added(sum_ref[1, :middle], far0_ref[1]).astype(BF16)
+    weight_out, back_out, weight1_out, back1_out, first_out, second_out = refs[2:]
+    weight_out[...] = added(sum_ref[1, : far0_ref.shape[1]], far0_ref[1]).astype(BF16)
     back_out[...] = added(back_ref[: back0_ref.shape[1]], back0_ref[1]).astype(BF16)
     weight1_out[...] = weight1_ref[...]
     back1_out[...] = back1_ref[...]
-    total = added(first_ref[...], first_far[...], second_ref[...]).astype(BF16)
-    total_ref[...] = total
-    send_ref[0] = total[1]
-    send_ref[1] = total[3]
-
-
-def z1_kernel(sum_ref, far1_ref, back_ref, back1_ref, total_ref, arrived_ref, *refs):
-    weight_out, back_out, send_ref = refs[-3:]
+    first_out[...] = added(first_ref[...], first_far[...])
+    second_out[...] = added(second_ref[...], second_far[...]).astype(BF16)
+
+
+def z1_kernel(sum_ref, far1_ref, back_ref, back1_ref, first_ref, second_ref, *refs):
+    weight_out, back_out, part_refs = refs[-6], refs[-5], refs[-4:]
     middle = sum_ref.shape[1] - far1_ref.shape[1]
     weight_out[...] = added(sum_ref[1, middle:], far1_ref[1]).astype(BF16)
     middle = back_ref.shape[0] - back1_ref.shape[1]
     back_out[...] = added(back_ref[middle:], back1_ref[1]).astype(BF16)
-    send_ref[0] = total_ref[2]
-    send_ref[1] = arrived_ref[1]
+    for n, ref in enumerate(part_refs):
+        ref[...] = added(first_ref[n], second_ref[n]).astype(BF16)
 
 
 def last_kernel(place_ref, *refs):
     sum_ref, far0, far1, z0, z1, back_ref, back0, back1, backz0, backz1 = refs[:10]
     slope_ref, first_ref = refs[10:12]
-    total_ref, arrived_y, arrived_z, weight_out, input_out, output_ref = refs[12:]
+    parts, (weight_out, input_out, output_ref) = refs[12:16], refs[16:]
     middle = far0.shape[1]
     for at, far, last in ((slice(0, middle), far0, z0), (slice(middle, None), far1, z1)):
         weight_out[at] = added(sum_ref[0, at], far[0], last[...]).astype(BF16)
@@ -320,7 +320,6 @@
             back = back_ref[at, low:high].astype(F32) + arrived
             input_out[at, low:high] = (slope_ref[at, low:high].astype(F32) * back).astype(BF16)
     me = place_ref[0]
-    parts = (total_ref.at[0], arrived_y.at[0], arrived_z.at[0], arrived_z.at[1])
     for part_ref, token in zip(parts, TOKEN_PARTS):
         for n, column in enumerate(COLUMN_BLOCKS):
             at = pl.multiple_of((me ^ (token ^ column)) * 128, 128)
@@ -351,7 +350,8 @@
         return jax.ShapeDtypeStruct(sizes, F32)
 
     piece, column = shape(rows, width), shape(width, 128)
-    packed_shape, half = shape(rows, PACKED), shape(rows // 2, PACKED)
+    packed_shape = shape(rows, PACKED)
+    half0_shape, half1_shape = shape(FIRST, PACKED), shape(rows - FIRST, PACKED)
     part, pair = shape(4, 16, 1024), shape(2, 4, 16, 1024)
     early = width * EARLY // rows
     split0, split1 = shape(2, early, 128), shape(2, width - early, 128)
@@ -367,7 +367,7 @@
     )
     outs = move(
         first_kernel,
-        [shape(2, 16, 1024)] * 4 + [half, column],
+        [shape(2, 16, 1024)] * 4 + [half0_shape, column],
         dp_place,
         output_grad,
         grad_far,
@@ -381,7 +381,7 @@
     weight_y = dp_swap(weight_out, COLS_Y)
     hidden_z0 = dp_swap(half_out, ROWS_Z)
     near, far, half_out, hidden_out, weight_out = move(
-        second_kernel, [part, part, half, packed_shape, column], *parts, packed, weight_z, hidden_z0, weight_y
+        second_kernel, [part, part, half1_shape, packed_shape, column], *parts, packed, weight_z, hidden_z0, weight_y
     )
 
     near_x = mp_swap(near, 2)
@@ -418,6 +418,15 @@
     masks = [first_y, second_y, first_z, second_z, first_yz, second_yz]
     hiddens = [hidden, hidden_y, hidden_z, hidden_yz]
 
+    near, away, grad_rows = move(
+        lambda *refs: weight_grad_kernel(scale, *refs),
+        [shape(4, width, 128)] * 2 + [shape(512, 1024)],
+        mp_place,
+        *grads,
+        *hiddens,
+        flops=5 * 10**9,
+    )
+    away = dp_swap(away, CORE)
     first0, first3, first_send, second0, second1, second_send = move(
         output_kernel,
         [part, part, pair, part, part, pair],
@@ -425,20 +434,16 @@
         *hiddens,
         weights,
         weights_far,
+        near,
         scratch=rows_scratch,
+        flops=5 * 10**9,
     )
     first_far = mp_swap(first_send, 2)
     second_far = mp_swap(second_send, 6)
-    near, away, grad_rows = move(
-        lambda *refs: weight_grad_kernel(scale, *refs),
-        [shape(4, width, 128)] * 2 + [shape(512, 1024)],
-        mp_place,
-        *grads,
-        *hiddens,
-        first0,
-        flops=5 * 10**9,
-    )
-    away = dp_swap(away, CORE)
+    send0, send1, sums = move(
+        core_kernel, [split0, split1, wide(2, width, 128)], near, away, first0
+    )
+    far0 = dp_swap(send0, COLS_Y)
     back_near, back_z, half0, half1 = move(
         back_kernel,
         [piece, shape(rows, KEPT), shape(2, EARLY, KEPT), shape(2, rows - EARLY, KEPT)],
@@ -446,17 +451,14 @@
         weights,
         weights_far,
         *masks,
+        send0,
         scratch=[pltpu.VMEM((3 * rows, KEPT), BF16)],
         flops=5 * 10**9,
     )
-
-    send0, send1, sums, half0, first, first_send, second, second_send = move(
-        y_kernel,
-        [split0, split1, wide(2, width, 128), shape(2, EARLY, KEPT)]
-        + [wide(4, 16, 1024), part] * 2,
-        near,
-        away,
-        half0,
+    back0 = dp_swap(half0, ROWS_Y)
+    first, first_send, second, second_send = move(
+        x_kernel,
+        [wide(4, 16, 1024), part] * 2,
         first0,
         first3,
         first_far,
@@ -464,20 +466,18 @@
         second1,
         second_far,
     )
-    far0 = dp_swap(send0, COLS_Y)
-    back0 = dp_swap(half0, ROWS_Y)
     first_far = mp_swap(first_send, 6)
-    second = mp_swap(added(second, mp_swap(second_send, 2)).astype(BF16), 1)
-
-    weight_z0, back_z0, send1, half1, total, total_send = move(
+    second_far = mp_swap(second_send, 2)
+
+    weight_z0, back_z0, send1, half1, first, second = move(
         z0_kernel,
         [
             shape(early, 128),
             shape(EARLY, KEPT),
             split1,
             shape(2, rows - EARLY, KEPT),
+            wide(4, 16, 1024),
             part,
-            shape(2, 16, 1024),
         ],
         sums,
         far0,
@@ -486,6 +486,7 @@
         first,
         first_far,
         second,
+        second_far,
         send1,
         half1,
     )
@@ -493,23 +494,23 @@
     back_z0 = dp_swap(back_z0, ROWS_Z)
     far1 = dp_swap(send1, COLS_Y)
     back1 = dp_swap(half1, ROWS_Y)
-    arrived_y = dp_swap(total_send, ROWS_Y)
-
-    weight_z1, back_z1, total_send = move(
+    second = mp_swap(second, 1)
+
+    outs = move(
         z1_kernel,
-        [shape(width - early, 128), shape(rows - EARLY, KEPT), shape(2, 16, 1024)],
+        [shape(width - early, 128), shape(rows - EARLY, KEPT)] + [shape(16, 1024)] * 4,
         sums,
         far1,
         back_z,
         back1,
-        total,
-        arrived_y,
+        first,
+        second,
         weight_z0,
         back_z0,
     )
-    weight_z1 = dp_swap(weight_z1, COLS_Z)
-    back_z1 = dp_swap(back_z1, ROWS_Z)
-    arrived_z = dp_swap(total_send, ROWS_Z)
+    weight_z1 = dp_swap(outs[0], COLS_Z)
+    back_z1 = dp_swap(outs[1], ROWS_Z)
+    parts = [outs[2]] + [dp_swap(p, k) for p, k in zip(outs[3:], TOKEN_PARTS[1:])]
     weight_grad, input_grad, output = move(
         last_kernel,
         [column, piece, shape(16, 4096)],
@@ -526,9 +527,7 @@
         back_z1,
         slope,
         first_kept,
-        total,
-        arrived_y,
-        arrived_z,
+        *parts,
     )
     return (output, weight_grad, input_grad)
 

time: 120 us -> 113 us (0.942)
  Pallas kernels: 19.5 us -> 13.6 us
  waiting for transfers between devices: 38.7 us -> 34.7 us
  starting transfers between devices: 57 us -> 60.1 us
    pallas_call x13 -> x14, Pallas kernels: 19.5 us -> 13.6 us  [move(): call(kernel, out_shape, in_specs=[in_smem() if a.dtype == jnp.int32 and a...]
    ppermute x32 -> x33, waiting for transfers between devices: 38.7 us -> 34.7 us  [swap(): return lax.ppermute(array, axis, [(i, i ^ k) for i in range(size)])]
    ppermute x32 -> x33, starting transfers between devices: 57 us -> 60.1 us  [swap(): return lax.ppermute(array, axis, [(i, i ^ k) for i in range(size)])]
    unnamed x20 -> x12, local copies, waits for them, and re-layouts: 3.73 us -> 3.22 us
  transfers between devices with their start and end apart: 32 -> 33, of which waited for: 15 -> 17; matrix products, arithmetic and copies ran while one was open for 0% -> 0% of each run, Pallas kernels for 11% -> 10%
where the time goes in v4:
time: 113 us; the launch traced here: 112 us
  starting transfers between devices  60.1 us (53%)
  waiting for transfers between devices  34.7 us (31%)
  Pallas kernels  13.6 us (12%)
  local copies, waits for them, and re-layouts  3.22 us (3%)
    ppermute x33, starting transfers between devices, swap(): return lax.ppermute(array, axis, [(i, i ^ k) for i in range(size)])  60.1 us
    ppermute x33, waiting for transfers between devices, swap(): return lax.ppermute(array, axis, [(i, i ^ k) for i in range(size)])  34.7 us
    pallas_call x14, Pallas kernels, move(): call(kernel, out_shape, in_specs=[in_smem() if a.dtype == jnp.int32 and a...  13.6 us
    unnamed x12, local copies, waits for them, and re-layouts  3.22 us
  transfers between devices with their start and end apart: 33, of which 17 were waited for; matrix products, arithmetic and copies ran while one was open for 0% of the time, Pallas kernels for 10%

profile of v4, /device:TPU:8, one launch (start us, length us, event | category | flops | bytes accessed | tf_op | source)
XLA Modules:
  0.0 112.4 jit_solution(7817782206523982782)
XLA Ops:
  0.6 7.3 %collective-permute-start = (bf16[16,4096]{1,0:T(8,128)(2,1)}, bf16[16,4096]{1,0:T(8,128)(2,1)S(1)}, u32[]{:S(2)}, u32[]{:S(2)}) collective-permute-start(bf16[16,4096]{1,0:T(8,128)(2,1)} %grad_ref.1), channel_id=1, source_target_pairs={{0,1},{1,0},{2,3},{3,2},{4,5},{5,4},{6,7},{7,6},{8,9},{9,8},{10,11... | collective-permute-start | bytes 393224 | tf_op jit(solution)/shard_map/ppermute | solution.py:29
  11.8 1.7 %collective-permute-start.6 = (bf16[1792,128]{1,0:T(8,128)(2,1)S(1)}, bf16[1792,128]{1,0:T(8,128)(2,1)S(1)}, u32[]{:S(2)}, u32[]{:S(2)}) collective-permute-start(bf16[1792,128]{1,0:T(8,128)(2,1)S(1)} %get-tuple-element.71), channel_id=1, source_target_pairs={{0,48},{8,56},{16,32},{24,40},{32,16},{40,24},{48,0},{56,8},{64,11... | collective-permute-start | bytes 1376264 | tf_op jit(solution)/shard_map/ppermute | solution.py:29
  13.5 3.8 %collective-permute-start.4 = (bf16[1792,128]{1,0:T(8,128)(2,1)S(1)}, bf16[1792,128]{1,0:T(8,128)(2,1)S(1)}, u32[]{:S(2)}, u32[]{:S(2)}) collective-permute-start(bf16[1792,128]{1,0:T(8,128)(2,1)S(1)} %get-tuple-element.71), channel_id=1, source_target_pairs={{0,64},{8,72},{16,80},{24,88},{32,96},{40,104},{48,112},{56,120},{... | collective-permute-start | bytes 1376264 | tf_op jit(solution)/shard_map/ppermute | solution.py:29
  18.1 1.9 %collective-permute-start.1 = (bf16[2,16,1024]{2,1,0:T(8,128)(2,1)S(1)}, bf16[2,16,1024]{2,1,0:T(8,128)(2,1)S(1)}, u32[]{:S(2)}, u32[]{:S(2)}) collective-permute-start(bf16[2,16,1024]{2,1,0:T(8,128)(2,1)S(1)} %get-tuple-element.68), channel_id=1, source_target_pairs={{0,16},{8,24},{16,0},{24,8},{32,48},{40,56},{48,32},{56,40},{64,80... | collective-permute-start | bytes 196616 | tf_op jit(solution)/shard_map/ppermute | solution.py:29
  20.0 2.2 %collective-permute-start.2 = (bf16[2,16,1024]{2,1,0:T(8,128)(2,1)S(1)}, bf16[2,16,1024]{2,1,0:T(8,128)(2,1)S(1)}, u32[]{:S(2)}, u32[]{:S(2)}) collective-permute-start(bf16[2,16,1024]{2,1,0:T(8,128)(2,1)S(1)} %get-tuple-element.69), channel_id=1, source_target_pairs={{0,128},{8,136},{16,144},{24,152},{32,160},{40,168},{48,176},{56,1... | collective-permute-start | bytes 196616 | tf_op jit(solution)/shard_map/ppermute | solution.py:29
  22.3 3.5 %collective-permute-start.3 = (bf16[2,16,1024]{2,1,0:T(8,128)(2,1)S(1)}, bf16[2,16,1024]{2,1,0:T(8,128)(2,1)S(1)}, u32[]{:S(2)}, u32[]{:S(2)}) collective-permute-start(bf16[2,16,1024]{2,1,0:T(8,128)(2,1)S(1)} %get-tuple-element.70), channel_id=1, source_target_pairs={{0,144},{8,152},{16,128},{24,136},{32,176},{40,184},{48,160},{56,1... | collective-permute-start | bytes 196616 | tf_op jit(solution)/shard_map/ppermute | solution.py:29
  25.8 2.5 %collective-permute-done.2.refs_2_ = bf16[2,16,1024]{2,1,0:T(8,128)(2,1)S(1)} collective-permute-done((bf16[2,16,1024]{2,1,0:T(8,128)(2,1)S(1)}, bf16[2,16,1024]{2,1,0:T(8,128)(2,1)S(1)}, u32[]{:S(2)}, u32[]{:S(2)}) %collective-permute-start.2) | collective-permute-done | bytes 65568 | tf_op jit(solution)/shard_map/ppermute | solution.py:29
  29.1 1.6 %collective-permute-done.4.refs_5_.refs_2_ = bf16[1792,128]{1,0:T(8,128)(2,1)S(1)} collective-permute-done((bf16[1792,128]{1,0:T(8,128)(2,1)S(1)}, bf16[1792,128]{1,0:T(8,128)(2,1)S(1)}, u32[]{:S(2)}, u32[]{:S(2)}) %collective-permute-start.4) | collective-permute-done | bytes 458784 | tf_op jit(solution)/shard_map/ppermute | solution.py:29
  30.8 1.7 %collective-permute-start.10 = (bf16[1792,128]{1,0:T(8,128)(2,1)S(1)}, bf16[1792,128]{1,0:T(8,128)(2,1)S(1)}, u32[]{:S(2)}, u32[]{:S(2)}) collective-permute-start(bf16[1792,128]{1,0:T(8,128)(2,1)S(1)} %get-tuple-element.76), channel_id=1, source_target_pairs={{0,48},{8,56},{16,32},{24,40},{32,16},{40,24},{48,0},{56,8},{64,11... | collective-permute-start | bytes 1376264 | tf_op jit(solution)/shard_map/ppermute | solution.py:29
  32.4 1.9 %collective-permute-start.11 = (bf16[128,1408]{1,0:T(8,128)(2,1)S(1)}, bf16[128,1408]{1,0:T(8,128)(2,1)S(1)}, u32[]{:S(2)}, u32[]{:S(2)}) collective-permute-start(bf16[128,1408]{1,0:T(8,128)(2,1)S(1)} %get-tuple-element.77), channel_id=1, source_target_pairs={{0,16},{8,24},{16,0},{24,8},{32,48},{40,56},{48,32},{56,40},{64,80... | collective-permute-start | bytes 1081352 | tf_op jit(solution)/shard_map/ppermute | solution.py:29
  37.2 2.1 %collective-permute-start.8 = (bf16[4,16,1024]{2,1,0:T(8,128)(2,1)S(1)}, bf16[4,16,1024]{2,1,0:T(8,128)(2,1)S(1)}, u32[]{:S(2)}, u32[]{:S(2)}) collective-permute-start(bf16[4,16,1024]{2,1,0:T(8,128)(2,1)S(1)} %get-tuple-element.74.far_ref), channel_id=1, source_target_pairs={{0,6},{1,7},{2,4},{3,5},{4,2},{5,3},{6,0},{7,1},{8,14},{9,15},{10,... | collective-permute-start | bytes 393224 | tf_op jit(solution)/shard_map/ppermute | solution.py:29
  40.7 2.7 %collective-permute-done.8.far_x = bf16[4,16,1024]{2,1,0:T(8,128)(2,1)S(1)} collective-permute-done((bf16[4,16,1024]{2,1,0:T(8,128)(2,1)S(1)}, bf16[4,16,1024]{2,1,0:T(8,128)(2,1)S(1)}, u32[]{:S(2)}, u32[]{:S(2)}) %collective-permute-start.8) | collective-permute-done | bytes 131104 | tf_op jit(solution)/shard_map/ppermute | solution.py:29
  43.4 1.9 %collective-permute-done.9.z1_ref = bf16[80,1408]{1,0:T(8,128)(2,1)S(1)} collective-permute-done((bf16[80,1408]{1,0:T(8,128)(2,1)S(1)}, bf16[80,1408]{1,0:T(8,128)(2,1)S(1)}, u32[]{:S(2)}, u32[]{:S(2)}) %collective-permute-start.9) | collective-permute-done | bytes 225312 | tf_op jit(solution)/shard_map/ppermute | solution.py:29
  47.6 2.8 %collective-permute-start.12 = (bf16[2,4,16,1024]{3,2,1,0:T(8,128)(2,1)S(1)}, bf16[2,4,16,1024]{3,2,1,0:T(8,128)(2,1)S(1)}, u32[]{:S(2)}, u32[]{:S(2)}) collective-permute-start(bf16[2,4,16,1024]{3,2,1,0:T(8,128)(2,1)S(1)} %get-tuple-element.78.refs_1_), channel_id=1, source_target_pairs={{0,6},{1,7},{2,4},{3,5},{4,2},{5,3},{6,0},{7,1},{8,14},{9,15},{10,... | collective-permute-start | bytes 786440 | tf_op jit(solution)/shard_map/ppermute | solution.py:29
  51.8 2.3 %collective-permute-done.14.refs_0_ = bf16[128,1408]{1,0:T(8,128)(2,1)S(1)} collective-permute-done((bf16[128,1408]{1,0:T(8,128)(2,1)S(1)}, bf16[128,1408]{1,0:T(8,128)(2,1)S(1)}, u32[]{:S(2)}, u32[]{:S(2)}) %collective-permute-start.14) | collective-permute-done | bytes 360480 | tf_op jit(solution)/shard_map/ppermute | solution.py:29
  55.2 1.5 %collective-permute-done.13.refs_4_ = bf16[2,4,16,1024]{3,2,1,0:T(8,128)(2,1)S(1)} collective-permute-done((bf16[2,4,16,1024]{3,2,1,0:T(8,128)(2,1)S(1)}, bf16[2,4,16,1024]{3,2,1,0:T(8,128)(2,1)S(1)}, u32[]{:S(2)}, u32[]{:S(2)}) %collective-permute-start.13) | collective-permute-done | bytes 262176 | tf_op jit(solution)/shard_map/ppermute | solution.py:29
  56.8 2.1 %shard_map.73 = (bf16[4,1792,128]{2,1,0:T(8,128)(2,1)S(1)}, bf16[4,1792,128]{2,1,0:T(8,128)(2,1)S(1)}, bf16[512,1024]{1,0:T(8,128)(2,1)S(1)}) custom-call(s32[1]{0:T(128)} %bitcast.1.refs_0_.place_ref, bf16[2,4,16,1024]{3,2,1,0:T(8,128)(2,1)S(1)} %get-tuple-element.78.refs_1_, bf16[2,4,16,1024]{3,2,1,0:T(8,128)(2,1)S(1)} %collective-permute-done.12.refs_2_, ...), custom_call_target="tpu_custom_call" | custom-call | flops 5000000000 | bytes 1 | tf_op jit(solution)/shard_map/pallas_call | solution.py:330
  59.0 2.1 %shard_map.74 = (bf16[4,16,1024]{2,1,0:T(8,128)(2,1)S(1)}, bf16[4,16,1024]{2,1,0:T(8,128)(2,1)S(1)}, bf16[2,4,16,1024]{3,2,1,0:T(8,128)(2,1)S(1)}, bf16[4,16,102...) custom-call(s32[1]{0:T(128)} %bitcast.1.refs_0_.place_ref, ...), custom_call_target="tpu_custom_call" | custom-call | flops 5000000000 | bytes 1 | tf_op jit(solution)/shard_map/pallas_call | solution.py:330
  63.3 1.6 %collective-permute-start.17 = (bf16[2,896,128]{2,1,0:T(8,128)(2,1)S(1)}, bf16[2,896,128]{2,1,0:T(8,128)(2,1)S(1)}, u32[]{:S(2)}, u32[]{:S(2)}) collective-permute-start(bf16[2,896,128]{2,1,0:T(8,128)(2,1)S(1)} %get-tuple-element.90.refs_6_), channel_id=1, source_target_pairs={{0,48},{8,56},{16,32},{24,40},{32,16},{40,24},{48,0},{56,8},{64,11... | collective-permute-start | bytes 1376264 | tf_op jit(solution)/shard_map/ppermute | solution.py:29
  64.9 3.5 %shard_map.76 = (bf16[128,1792]{1,0:T(8,128)(2,1)S(1)}, bf16[128,896]{1,0:T(8,128)(2,1)S(1)}, bf16[2,64,896]{2,1,0:T(8,128)(2,1)S(1)}, bf16[2,64,896]{2,1,0:T(8,128)(2,1)S(1)}) custom-call(bf16[512,1024]{1,0:T(8,128)(2,1)S(1)} %get-tuple-element.91.rows_ref, bf16[4,1792,128]{2,1,0:T(8,128)(2,1)S(1)} %copy-done.3, ...), custom_call_target="tpu_custom_call" | custom-call | flops 5000000000 | bytes 1 | tf_op jit(solution)/shard_map/pallas_call | solution.py:330
  68.4 1.6 %collective-permute-start.18 = (bf16[2,64,896]{2,1,0:T(8,128)(2,1)S(1)}, bf16[2,64,896]{2,1,0:T(8,128)(2,1)S(1)}, u32[]{:S(2)}, u32[]{:S(2)}) collective-permute-start(bf16[2,64,896]{2,1,0:T(8,128)(2,1)S(1)} %get-tuple-element.99), channel_id=1, source_target_pairs={{0,16},{8,24},{16,0},{24,8},{32,48},{40,56},{48,32},{56,40},{64,80... | collective-permute-start | bytes 688136 | tf_op jit(solution)/shard_map/ppermute | solution.py:29
  72.8 4.9 %collective-permute-done.21.first_far = bf16[4,16,1024]{2,1,0:T(8,128)(2,1)S(1)} collective-permute-done((bf16[4,16,1024]{2,1,0:T(8,128)(2,1)S(1)}, bf16[4,16,1024]{2,1,0:T(8,128)(2,1)S(1)}, u32[]{:S(2)}, u32[]{:S(2)}) %collective-permute-start.21) | collective-permute-done | bytes 131104 | tf_op jit(solution)/shard_map/ppermute | solution.py:29
  77.9 1.6 %collective-permute-start.23 = (bf16[2,896,128]{2,1,0:T(8,128)(2,1)S(1)}, bf16[2,896,128]{2,1,0:T(8,128)(2,1)S(1)}, u32[]{:S(2)}, u32[]{:S(2)}) collective-permute-start(bf16[2,896,128]{2,1,0:T(8,128)(2,1)S(1)} %get-tuple-element.111), channel_id=1, source_target_pairs={{0,48},{8,56},{16,32},{24,40},{32,16},{40,24},{48,0},{56,8},{64,11... | collective-permute-start | bytes 1376264 | tf_op jit(solution)/shard_map/ppermute | solution.py:29
  79.5 1.9 %collective-permute-start.24 = (bf16[896,128]{1,0:T(8,128)(2,1)S(1)}, bf16[896,128]{1,0:T(8,128)(2,1)S(1)}, u32[]{:S(2)}, u32[]{:S(2)}) collective-permute-start(bf16[896,128]{1,0:T(8,128)(2,1)S(1)} %get-tuple-element.112), channel_id=1, source_target_pairs={{0,64},{8,72},{16,80},{24,88},{32,96},{40,104},{48,112},{56,120},{... | collective-permute-start | bytes 688136 | tf_op jit(solution)/shard_map/ppermute | solution.py:29
  82.2 4.8 %collective-permute-start.26 = (bf16[4,16,1024]{2,1,0:T(8,128)(2,1)S(1)}, bf16[4,16,1024]{2,1,0:T(8,128)(2,1)S(1)}, u32[]{:S(2)}, u32[]{:S(2)}) collective-permute-start(bf16[4,16,1024]{2,1,0:T(8,128)(2,1)S(1)} %get-tuple-element.115), channel_id=1, source_target_pairs={{0,1},{1,0},{2,3},{3,2},{4,5},{5,4},{6,7},{7,6},{8,9},{9,8},{10,11... | collective-permute-start | bytes 393224 | tf_op jit(solution)/shard_map/ppermute | solution.py:29
  87.0 3.4 %collective-permute-start.27 = (bf16[64,896]{1,0:T(8,128)(2,1)S(1)}, bf16[64,896]{1,0:T(8,128)(2,1)S(1)}, u32[]{:S(2)}, u32[]{:S(2)}) collective-permute-start(bf16[64,896]{1,0:T(8,128)(2,1)S(1)} %get-tuple-element.116), channel_id=1, source_target_pairs={{0,128},{8,136},{16,144},{24,152},{32,160},{40,168},{48,176},{56,1... | collective-permute-start | bytes 344072 | tf_op jit(solution)/shard_map/ppermute | solution.py:29
  90.4 7.6 %collective-permute-done.27.refs_1_.refs_8_ = bf16[64,896]{1,0:T(8,128)(2,1)S(1)} collective-permute-done((bf16[64,896]{1,0:T(8,128)(2,1)S(1)}, bf16[64,896]{1,0:T(8,128)(2,1)S(1)}, u32[]{:S(2)}, u32[]{:S(2)}) %collective-permute-start.27) | collective-permute-done | bytes 114720 | tf_op jit(solution)/shard_map/ppermute | solution.py:29
  98.2 3.1 %collective-permute-start.29 = (bf16[64,896]{1,0:T(8,128)(2,1)S(1)}, bf16[64,896]{1,0:T(8,128)(2,1)S(1)}, u32[]{:S(2)}, u32[]{:S(2)}) collective-permute-start(bf16[64,896]{1,0:T(8,128)(2,1)S(1)} %get-tuple-element.119), channel_id=1, source_target_pairs={{0,128},{8,136},{16,144},{24,152},{32,160},{40,168},{48,176},{56,1... | collective-permute-start | bytes 344072 | tf_op jit(solution)/shard_map/ppermute | solution.py:29
  102.8 2.9 %collective-permute-start.32 = (bf16[16,1024]{1,0:T(8,128)(2,1)S(1)}, bf16[16,1024]{1,0:T(8,128)(2,1)S(1)}, u32[]{:S(2)}, u32[]{:S(2)}) collective-permute-start(bf16[16,1024]{1,0:T(8,128)(2,1)S(1)} %get-tuple-element.125), channel_id=1, source_target_pairs={{0,144},{8,152},{16,128},{24,136},{32,176},{40,184},{48,160},{56,1... | collective-permute-start | bytes 98312 | tf_op jit(solution)/shard_map/ppermute | solution.py:29
  105.7 1.7 %collective-permute-done.31.refs_14_ = bf16[16,1024]{1,0:T(8,128)(2,1)S(1)} collective-permute-done((bf16[16,1024]{1,0:T(8,128)(2,1)S(1)}, bf16[16,1024]{1,0:T(8,128)(2,1)S(1)}, u32[]{:S(2)}, u32[]{:S(2)}) %collective-permute-start.31) | collective-permute-done | bytes 32800 | tf_op jit(solution)/shard_map/ppermute | solution.py:29
  107.4 3.2 %collective-permute-done.32.refs_15_ = bf16[16,1024]{1,0:T(8,128)(2,1)S(1)} collective-permute-done((bf16[16,1024]{1,0:T(8,128)(2,1)S(1)}, bf16[16,1024]{1,0:T(8,128)(2,1)S(1)}, u32[]{:S(2)}, u32[]{:S(2)}) %collective-permute-start.32) | collective-permute-done | bytes 32800 | tf_op jit(solution)/shard_map/ppermute | solution.py:29
  110.7 1.7 %shard_map.80 = (bf16[1792,128]{1,0:T(8,128)(2,1)}, bf16[128,1792]{1,0:T(8,128)(2,1)}, bf16[16,4096]{1,0:T(8,128)(2,1)}) custom-call(s32[1]{0:T(128)} %bitcast.place_ref, f32[2,1792,128]{2,1,0:T(8,128)S(1)} %get-tuple-element.89.sum_ref.refs_0_, bf16[2,896,128]{2,1,0:T(8,128)(2,1)S(1)} %collective-permute-done.17.far0_ref.refs_1_, ...), custom_call_target="tpu_custom_call" | custom-call | flops 1 | bytes 1 | tf_op jit(solution)/shard_map/pallas_call | solution.py:330
  (60 shorter events, 22.5 us)
Async XLA Ops:
  0.6 11.1 %collective-permute-start = (bf16[16,4096]{1,0:T(8,128)(2,1)}, bf16[16,4096]{1,0:T(8,128)(2,1)S(1)}, u32[]{:S(2)}, u32[]{:S(2)}) collective-permute-start(bf16[16,4096]{1,0:T(8,128)(2,1)} %grad_ref.1), channel_id=1, source_target_pairs={{0,1},{1,0},{2,3},{3,2},{4,5},{5,4},{6,7},{7,6},{8,9},{9,8},{10,11... | collective-permute-start | bytes 393224 | tf_op jit(solution)/shard_map/ppermute | solution.py:29
  11.8 17.2 %collective-permute-start.6 = (bf16[1792,128]{1,0:T(8,128)(2,1)S(1)}, bf16[1792,128]{1,0:T(8,128)(2,1)S(1)}, u32[]{:S(2)}, u32[]{:S(2)}) collective-permute-start(bf16[1792,128]{1,0:T(8,128)(2,1)S(1)} %get-tuple-element.71), channel_id=1, source_target_pairs={{0,48},{8,56},{16,32},{24,40},{32,16},{40,24},{48,0},{56,8},{64,11... | collective-permute-start | bytes 1376264 | tf_op jit(solution)/shard_map/ppermute | solution.py:29
  13.5 17.2 %collective-permute-start.4 = (bf16[1792,128]{1,0:T(8,128)(2,1)S(1)}, bf16[1792,128]{1,0:T(8,128)(2,1)S(1)}, u32[]{:S(2)}, u32[]{:S(2)}) collective-permute-start(bf16[1792,128]{1,0:T(8,128)(2,1)S(1)} %get-tuple-element.71), channel_id=1, source_target_pairs={{0,64},{8,72},{16,80},{24,88},{32,96},{40,104},{48,112},{56,120},{... | collective-permute-start | bytes 1376264 | tf_op jit(solution)/shard_map/ppermute | solution.py:29
  17.3 11.7 %collective-permute-start.5 = (bf16[48,1408]{1,0:T(8,128)(2,1)S(1)}, bf16[48,1408]{1,0:T(8,128)(2,1)S(1)}, u32[]{:S(2)}, u32[]{:S(2)}) collective-permute-start(bf16[48,1408]{1,0:T(8,128)(2,1)S(1)} %get-tuple-element.72), channel_id=1, source_target_pairs={{0,128},{8,136},{16,144},{24,152},{32,160},{40,168},{48,176},{56,1... | collective-permute-start | bytes 405512 | tf_op jit(solution)/shard_map/ppermute | solution.py:29
  18.1 4.3 %collective-permute-start.1 = (bf16[2,16,1024]{2,1,0:T(8,128)(2,1)S(1)}, bf16[2,16,1024]{2,1,0:T(8,128)(2,1)S(1)}, u32[]{:S(2)}, u32[]{:S(2)}) collective-permute-start(bf16[2,16,1024]{2,1,0:T(8,128)(2,1)S(1)} %get-tuple-element.68), channel_id=1, source_target_pairs={{0,16},{8,24},{16,0},{24,8},{32,48},{40,56},{48,32},{56,40},{64,80... | collective-permute-start | bytes 196616 | tf_op jit(solution)/shard_map/ppermute | solution.py:29
  20.0 8.4 %collective-permute-start.2 = (bf16[2,16,1024]{2,1,0:T(8,128)(2,1)S(1)}, bf16[2,16,1024]{2,1,0:T(8,128)(2,1)S(1)}, u32[]{:S(2)}, u32[]{:S(2)}) collective-permute-start(bf16[2,16,1024]{2,1,0:T(8,128)(2,1)S(1)} %get-tuple-element.69), channel_id=1, source_target_pairs={{0,128},{8,136},{16,144},{24,152},{32,160},{40,168},{48,176},{56,1... | collective-permute-start | bytes 196616 | tf_op jit(solution)/shard_map/ppermute | solution.py:29
  22.3 6.7 %collective-permute-start.3 = (bf16[2,16,1024]{2,1,0:T(8,128)(2,1)S(1)}, bf16[2,16,1024]{2,1,0:T(8,128)(2,1)S(1)}, u32[]{:S(2)}, u32[]{:S(2)}) collective-permute-start(bf16[2,16,1024]{2,1,0:T(8,128)(2,1)S(1)} %get-tuple-element.70), channel_id=1, source_target_pairs={{0,144},{8,152},{16,128},{24,136},{32,176},{40,184},{48,160},{56,1... | collective-permute-start | bytes 196616 | tf_op jit(solution)/shard_map/ppermute | solution.py:29
  30.8 14.5 %collective-permute-start.10 = (bf16[1792,128]{1,0:T(8,128)(2,1)S(1)}, bf16[1792,128]{1,0:T(8,128)(2,1)S(1)}, u32[]{:S(2)}, u32[]{:S(2)}) collective-permute-start(bf16[1792,128]{1,0:T(8,128)(2,1)S(1)} %get-tuple-element.76), channel_id=1, source_target_pairs={{0,48},{8,56},{16,32},{24,40},{32,16},{40,24},{48,0},{56,8},{64,11... | collective-permute-start | bytes 1376264 | tf_op jit(solution)/shard_map/ppermute | solution.py:29
  32.4 12.8 %collective-permute-start.11 = (bf16[128,1408]{1,0:T(8,128)(2,1)S(1)}, bf16[128,1408]{1,0:T(8,128)(2,1)S(1)}, u32[]{:S(2)}, u32[]{:S(2)}) collective-permute-start(bf16[128,1408]{1,0:T(8,128)(2,1)S(1)} %get-tuple-element.77), channel_id=1, source_target_pairs={{0,16},{8,24},{16,0},{24,8},{32,48},{40,56},{48,32},{56,40},{64,80... | collective-permute-start | bytes 1081352 | tf_op jit(solution)/shard_map/ppermute | solution.py:29
  34.3 10.9 %collective-permute-start.9 = (bf16[80,1408]{1,0:T(8,128)(2,1)S(1)}, bf16[80,1408]{1,0:T(8,128)(2,1)S(1)}, u32[]{:S(2)}, u32[]{:S(2)}) collective-permute-start(bf16[80,1408]{1,0:T(8,128)(2,1)S(1)} %get-tuple-element.75), channel_id=1, source_target_pairs={{0,128},{8,136},{16,144},{24,152},{32,160},{40,168},{48,176},{56,1... | collective-permute-start | bytes 675848 | tf_op jit(solution)/shard_map/ppermute | solution.py:29
  35.7 5.0 %collective-permute-start.7 = (bf16[4,16,1024]{2,1,0:T(8,128)(2,1)S(1)}, bf16[4,16,1024]{2,1,0:T(8,128)(2,1)S(1)}, u32[]{:S(2)}, u32[]{:S(2)}) collective-permute-start(bf16[4,16,1024]{2,1,0:T(8,128)(2,1)S(1)} %get-tuple-element.73.near_ref), channel_id=1, source_target_pairs={{0,2},{1,3},{2,0},{3,1},{4,6},{5,7},{6,4},{7,5},{8,10},{9,11},{10,... | collective-permute-start | bytes 393224 | tf_op jit(solution)/shard_map/ppermute | solution.py:29
  37.2 6.2 %collective-permute-start.8 = (bf16[4,16,1024]{2,1,0:T(8,128)(2,1)S(1)}, bf16[4,16,1024]{2,1,0:T(8,128)(2,1)S(1)}, u32[]{:S(2)}, u32[]{:S(2)}) collective-permute-start(bf16[4,16,1024]{2,1,0:T(8,128)(2,1)S(1)} %get-tuple-element.74.far_ref), channel_id=1, source_target_pairs={{0,6},{1,7},{2,4},{3,5},{4,2},{5,3},{6,0},{7,1},{8,14},{9,15},{10,... | collective-permute-start | bytes 393224 | tf_op jit(solution)/shard_map/ppermute | solution.py:29
  46.7 7.4 %collective-permute-start.14 = (bf16[128,1408]{1,0:T(8,128)(2,1)S(1)}, bf16[128,1408]{1,0:T(8,128)(2,1)S(1)}, u32[]{:S(2)}, u32[]{:S(2)}) collective-permute-start(bf16[128,1408]{1,0:T(8,128)(2,1)S(1)} %get-tuple-element.81.refs_1_), channel_id=1, source_target_pairs={{0,16},{8,24},{16,0},{24,8},{32,48},{40,56},{48,32},{56,40},{64,80... | collective-permute-start | bytes 1081352 | tf_op jit(solution)/shard_map/ppermute | solution.py:29
  47.6 7.6 %collective-permute-start.12 = (bf16[2,4,16,1024]{3,2,1,0:T(8,128)(2,1)S(1)}, bf16[2,4,16,1024]{3,2,1,0:T(8,128)(2,1)S(1)}, u32[]{:S(2)}, u32[]{:S(2)}) collective-permute-start(bf16[2,4,16,1024]{3,2,1,0:T(8,128)(2,1)S(1)} %get-tuple-element.78.refs_1_), channel_id=1, source_target_pairs={{0,6},{1,7},{2,4},{3,5},{4,2},{5,3},{6,0},{7,1},{8,14},{9,15},{10,... | collective-permute-start | bytes 786440 | tf_op jit(solution)/shard_map/ppermute | solution.py:29
  50.4 6.4 %collective-permute-start.13 = (bf16[2,4,16,1024]{3,2,1,0:T(8,128)(2,1)S(1)}, bf16[2,4,16,1024]{3,2,1,0:T(8,128)(2,1)S(1)}, u32[]{:S(2)}, u32[]{:S(2)}) collective-permute-start(bf16[2,4,16,1024]{3,2,1,0:T(8,128)(2,1)S(1)} %get-tuple-element.79.refs_3_), channel_id=1, source_target_pairs={{0,2},{1,3},{2,0},{3,1},{4,6},{5,7},{6,4},{7,5},{8,10},{9,11},{10,... | collective-permute-start | bytes 786440 | tf_op jit(solution)/shard_map/ppermute | solution.py:29
  50.6 8.4 %collective-permute-start.16 = (bf16[4,1792,128]{2,1,0:T(8,128)(2,1)}, bf16[4,1792,128]{2,1,0:T(8,128)(2,1)S(1)}, u32[]{:S(2)}, u32[]{:S(2)}) collective-permute-start(bf16[4,1792,128]{2,1,0:T(8,128)(2,1)} %copy-done.2), channel_id=1, source_target_pairs={{0,8},{8,0},{16,24},{24,16},{32,40},{40,32},{48,56},{56,48},{64,72... | collective-permute-start | bytes 5505032 | tf_op jit(solution)/shard_map/ppermute | solution.py:29
  61.2 8.9 %collective-permute-start.19 = (bf16[2,4,16,1024]{3,2,1,0:T(8,128)(2,1)S(1)}, bf16[2,4,16,1024]{3,2,1,0:T(8,128)(2,1)S(1)}, u32[]{:S(2)}, u32[]{:S(2)}) collective-permute-start(bf16[2,4,16,1024]{3,2,1,0:T(8,128)(2,1)S(1)} %get-tuple-element.101), channel_id=1, source_target_pairs={{0,2},{1,3},{2,0},{3,1},{4,6},{5,7},{6,4},{7,5},{8,10},{9,11},{10,... | collective-permute-start | bytes 786440 | tf_op jit(solution)/shard_map/ppermute | solution.py:29
  61.5 9.8 %collective-permute-start.20 = (bf16[2,4,16,1024]{3,2,1,0:T(8,128)(2,1)S(1)}, bf16[2,4,16,1024]{3,2,1,0:T(8,128)(2,1)S(1)}, u32[]{:S(2)}, u32[]{:S(2)}) collective-permute-start(bf16[2,4,16,1024]{3,2,1,0:T(8,128)(2,1)S(1)} %get-tuple-element.104), channel_id=1, source_target_pairs={{0,6},{1,7},{2,4},{3,5},{4,2},{5,3},{6,0},{7,1},{8,14},{9,15},{10,... | collective-permute-start | bytes 786440 | tf_op jit(solution)/shard_map/ppermute | solution.py:29
  63.3 14.4 %collective-permute-start.17 = (bf16[2,896,128]{2,1,0:T(8,128)(2,1)S(1)}, bf16[2,896,128]{2,1,0:T(8,128)(2,1)S(1)}, u32[]{:S(2)}, u32[]{:S(2)}) collective-permute-start(bf16[2,896,128]{2,1,0:T(8,128)(2,1)S(1)} %get-tuple-element.90.refs_6_), channel_id=1, source_target_pairs={{0,48},{8,56},{16,32},{24,40},{32,16},{40,24},{48,0},{56,8},{64,11... | collective-permute-start | bytes 1376264 | tf_op jit(solution)/shard_map/ppermute | solution.py:29
  68.4 9.3 %collective-permute-start.18 = (bf16[2,64,896]{2,1,0:T(8,128)(2,1)S(1)}, bf16[2,64,896]{2,1,0:T(8,128)(2,1)S(1)}, u32[]{:S(2)}, u32[]{:S(2)}) collective-permute-start(bf16[2,64,896]{2,1,0:T(8,128)(2,1)S(1)} %get-tuple-element.99), channel_id=1, source_target_pairs={{0,16},{8,24},{16,0},{24,8},{32,48},{40,56},{48,32},{56,40},{64,80... | collective-permute-start | bytes 688136 | tf_op jit(solution)/shard_map/ppermute | solution.py:29
  71.4 6.3 %collective-permute-start.21 = (bf16[4,16,1024]{2,1,0:T(8,128)(2,1)S(1)}, bf16[4,16,1024]{2,1,0:T(8,128)(2,1)S(1)}, u32[]{:S(2)}, u32[]{:S(2)}) collective-permute-start(bf16[4,16,1024]{2,1,0:T(8,128)(2,1)S(1)} %get-tuple-element.106), channel_id=1, source_target_pairs={{0,6},{1,7},{2,4},{3,5},{4,2},{5,3},{6,0},{7,1},{8,14},{9,15},{10,... | collective-permute-start | bytes 393224 | tf_op jit(solution)/shard_map/ppermute | solution.py:29
  72.8 5.0 %collective-permute-start.22 = (bf16[4,16,1024]{2,1,0:T(8,128)(2,1)S(1)}, bf16[4,16,1024]{2,1,0:T(8,128)(2,1)S(1)}, u32[]{:S(2)}, u32[]{:S(2)}) collective-permute-start(bf16[4,16,1024]{2,1,0:T(8,128)(2,1)S(1)} %get-tuple-element.108), channel_id=1, source_target_pairs={{0,2},{1,3},{2,0},{3,1},{4,6},{5,7},{6,4},{7,5},{8,10},{9,11},{10,... | collective-permute-start | bytes 393224 | tf_op jit(solution)/shard_map/ppermute | solution.py:29
  77.9 20.1 %collective-permute-start.23 = (bf16[2,896,128]{2,1,0:T(8,128)(2,1)S(1)}, bf16[2,896,128]{2,1,0:T(8,128)(2,1)S(1)}, u32[]{:S(2)}, u32[]{:S(2)}) collective-permute-start(bf16[2,896,128]{2,1,0:T(8,128)(2,1)S(1)} %get-tuple-element.111), channel_id=1, source_target_pairs={{0,48},{8,56},{16,32},{24,40},{32,16},{40,24},{48,0},{56,8},{64,11... | collective-permute-start | bytes 1376264 | tf_op jit(solution)/shard_map/ppermute | solution.py:29
  79.5 18.5 %collective-permute-start.24 = (bf16[896,128]{1,0:T(8,128)(2,1)S(1)}, bf16[896,128]{1,0:T(8,128)(2,1)S(1)}, u32[]{:S(2)}, u32[]{:S(2)}) collective-permute-start(bf16[896,128]{1,0:T(8,128)(2,1)S(1)} %get-tuple-element.112), channel_id=1, source_target_pairs={{0,64},{8,72},{16,80},{24,88},{32,96},{40,104},{48,112},{56,120},{... | collective-permute-start | bytes 688136 | tf_op jit(solution)/shard_map/ppermute | solution.py:29
  81.3 16.6 %collective-permute-start.25 = (bf16[2,64,896]{2,1,0:T(8,128)(2,1)S(1)}, bf16[2,64,896]{2,1,0:T(8,128)(2,1)S(1)}, u32[]{:S(2)}, u32[]{:S(2)}) collective-permute-start(bf16[2,64,896]{2,1,0:T(8,128)(2,1)S(1)} %get-tuple-element.113), channel_id=1, source_target_pairs={{0,16},{8,24},{16,0},{24,8},{32,48},{40,56},{48,32},{56,40},{64,80... | collective-permute-start | bytes 688136 | tf_op jit(solution)/shard_map/ppermute | solution.py:29
  82.2 15.7 %collective-permute-start.26 = (bf16[4,16,1024]{2,1,0:T(8,128)(2,1)S(1)}, bf16[4,16,1024]{2,1,0:T(8,128)(2,1)S(1)}, u32[]{:S(2)}, u32[]{:S(2)}) collective-permute-start(bf16[4,16,1024]{2,1,0:T(8,128)(2,1)S(1)} %get-tuple-element.115), channel_id=1, source_target_pairs={{0,1},{1,0},{2,3},{3,2},{4,5},{5,4},{6,7},{7,6},{8,9},{9,8},{10,11... | collective-permute-start | bytes 393224 | tf_op jit(solution)/shard_map/ppermute | solution.py:29
  87.0 11.0 %collective-permute-start.27 = (bf16[64,896]{1,0:T(8,128)(2,1)S(1)}, bf16[64,896]{1,0:T(8,128)(2,1)S(1)}, u32[]{:S(2)}, u32[]{:S(2)}) collective-permute-start(bf16[64,896]{1,0:T(8,128)(2,1)S(1)} %get-tuple-element.116), channel_id=1, source_target_pairs={{0,128},{8,136},{16,144},{24,152},{32,160},{40,168},{48,176},{56,1... | collective-permute-start | bytes 344072 | tf_op jit(solution)/shard_map/ppermute | solution.py:29
  98.1 12.6 %collective-permute-start.28 = (bf16[896,128]{1,0:T(8,128)(2,1)S(1)}, bf16[896,128]{1,0:T(8,128)(2,1)S(1)}, u32[]{:S(2)}, u32[]{:S(2)}) collective-permute-start(bf16[896,128]{1,0:T(8,128)(2,1)S(1)} %get-tuple-element.117), channel_id=1, source_target_pairs={{0,64},{8,72},{16,80},{24,88},{32,96},{40,104},{48,112},{56,120},{... | collective-permute-start | bytes 688136 | tf_op jit(solution)/shard_map/ppermute | solution.py:29
  98.2 12.4 %collective-permute-start.29 = (bf16[64,896]{1,0:T(8,128)(2,1)S(1)}, bf16[64,896]{1,0:T(8,128)(2,1)S(1)}, u32[]{:S(2)}, u32[]{:S(2)}) collective-permute-start(bf16[64,896]{1,0:T(8,128)(2,1)S(1)} %get-tuple-element.119), channel_id=1, source_target_pairs={{0,128},{8,136},{16,144},{24,152},{32,160},{40,168},{48,176},{56,1... | collective-permute-start | bytes 344072 | tf_op jit(solution)/shard_map/ppermute | solution.py:29
  101.3 4.4 %collective-permute-start.30 = (bf16[16,1024]{1,0:T(8,128)(2,1)S(1)}, bf16[16,1024]{1,0:T(8,128)(2,1)S(1)}, u32[]{:S(2)}, u32[]{:S(2)}) collective-permute-start(bf16[16,1024]{1,0:T(8,128)(2,1)S(1)} %get-tuple-element.123), channel_id=1, source_target_pairs={{0,16},{8,24},{16,0},{24,8},{32,48},{40,56},{48,32},{56,40},{64,80... | collective-permute-start | bytes 98312 | tf_op jit(solution)/shard_map/ppermute | solution.py:29
  102.3 5.1 %collective-permute-start.31 = (bf16[16,1024]{1,0:T(8,128)(2,1)S(1)}, bf16[16,1024]{1,0:T(8,128)(2,1)S(1)}, u32[]{:S(2)}, u32[]{:S(2)}) collective-permute-start(bf16[16,1024]{1,0:T(8,128)(2,1)S(1)} %get-tuple-element.124), channel_id=1, source_target_pairs={{0,128},{8,136},{16,144},{24,152},{32,160},{40,168},{48,176},{56,1... | collective-permute-start | bytes 98312 | tf_op jit(solution)/shard_map/ppermute | solution.py:29
  102.8 7.8 %collective-permute-start.32 = (bf16[16,1024]{1,0:T(8,128)(2,1)S(1)}, bf16[16,1024]{1,0:T(8,128)(2,1)S(1)}, u32[]{:S(2)}, u32[]{:S(2)}) collective-permute-start(bf16[16,1024]{1,0:T(8,128)(2,1)S(1)} %get-tuple-element.125), channel_id=1, source_target_pairs={{0,144},{8,152},{16,128},{24,136},{32,176},{40,184},{48,160},{56,1... | collective-permute-start | bytes 98312 | tf_op jit(solution)/shard_map/ppermute | solution.py:29
  (7 other events, 13.2 us)

commit v5 on v4

--- a/solution.py
+++ b/solution.py
@@ -178,7 +178,7 @@
 
 def third_kernel(near_ref, near_x, far_ref, far_x, z0_ref, z1_ref, *refs):
     weight_refs = refs[:4]
-    near_out, far_out, hidden_z, weights = refs[-4:]
+    near_out, far_out, hidden_z, weights, weights_send = refs[-5:]
     near_out[0] = near_ref[...]
     near_out[1] = near_x[...]
     far_out[0] = far_ref[...]
@@ -187,6 +187,7 @@
     hidden_z[z0_ref.shape[0] :] = z1_ref[...]
     for n, ref in enumerate(weight_refs):
         weights[n] = ref[...]
+        weights_send[n] = ref[...]
 
 
 def gather_rows(me, grad_refs, rows_ref):
@@ -389,9 +390,9 @@
     hidden_z1 = dp_swap(half_out, ROWS_Z)
     hidden_y = dp_swap(hidden_out, ROWS_Y)
     weight_yz = dp_swap(weight_out, COLS_Y)
-    near_two, far_two, hidden_z, weights = move(
+    near_two, far_two, hidden_z, weights, weights_send = move(
         third_kernel,
-        [pair, pair, packed_shape, shape(4, width, 128)],
+        [pair, pair, packed_shape] + [shape(4, width, 128)] * 2,
         near,
         near_x,
         far,
@@ -408,7 +409,7 @@
     near_rest = mp_swap(near_two, 6)
     far_rest = mp_swap(far_two, 2)
     hidden_yz = dp_swap(hidden_z, ROWS_Y)
-    weights_far = dp_swap(weights, CORE)
+    weights_far = dp_swap(weights_send, CORE)
     grads = [near_two, near_rest, far_two, far_rest]
     masked = [piece] * 3
     hidden_y, first_y, second_y, hidden_z, first_z, second_z = move(

time: 113 us -> 114 us (level)
  local copies, waits for them, and re-layouts: 3.22 us -> 4.46 us
    unnamed x12 -> x14, local copies, waits for them, and re-layouts: 3.22 us -> 4.46 us
where the time goes in v5:
time: 114 us
  starting transfers between devices  60.1 us (53%)
  waiting for transfers between devices  34.7 us (30%)
  Pallas kernels  13.9 us (12%)
  local copies, waits for them, and re-layouts  4.46 us (4%)
    ppermute x33, starting transfers between devices, swap(): return lax.ppermute(array, axis, [(i, i ^ k) for i in range(size)])  60.1 us
    ppermute x33, waiting for transfers between devices, swap(): return lax.ppermute(array, axis, [(i, i ^ k) for i in range(size)])  34.7 us
    pallas_call x14, Pallas kernels, move(): call(kernel, out_shape, in_specs=[in_smem() if a.dtype == jnp.int32 and a...  13.9 us
    unnamed x14, local copies, waits for them, and re-layouts  4.46 us
  transfers between devices with their start and end apart: 33, of which 17 were waited for; matrix products, arithmetic and copies ran while one was open for 0% of the time, Pallas kernels for 10%

profile of v5, /device:TPU:8, one launch (start us, length us, event | category | flops | bytes accessed | tf_op | source)
XLA Modules:
  0.0 114.0 jit_solution(12552170720780990141)
XLA Ops:
  0.6 7.3 %collective-permute-start = (bf16[16,4096]{1,0:T(8,128)(2,1)}, bf16[16,4096]{1,0:T(8,128)(2,1)S(1)}, u32[]{:S(2)}, u32[]{:S(2)}) collective-permute-start(bf16[16,4096]{1,0:T(8,128)(2,1)} %grad_ref.1), channel_id=1, source_target_pairs={{0,1},{1,0},{2,3},{3,2},{4,5},{5,4},{6,7},{7,6},{8,9},{9,8},{10,11... | collective-permute-start | bytes 393224 | tf_op jit(solution)/shard_map/ppermute | solution.py:29
  11.8 1.7 %collective-permute-start.6 = (bf16[1792,128]{1,0:T(8,128)(2,1)S(1)}, bf16[1792,128]{1,0:T(8,128)(2,1)S(1)}, u32[]{:S(2)}, u32[]{:S(2)}) collective-permute-start(bf16[1792,128]{1,0:T(8,128)(2,1)S(1)} %get-tuple-element.72), channel_id=1, source_target_pairs={{0,48},{8,56},{16,32},{24,40},{32,16},{40,24},{48,0},{56,8},{64,11... | collective-permute-start | bytes 1376264 | tf_op jit(solution)/shard_map/ppermute | solution.py:29
  13.5 3.8 %collective-permute-start.4 = (bf16[1792,128]{1,0:T(8,128)(2,1)S(1)}, bf16[1792,128]{1,0:T(8,128)(2,1)S(1)}, u32[]{:S(2)}, u32[]{:S(2)}) collective-permute-start(bf16[1792,128]{1,0:T(8,128)(2,1)S(1)} %get-tuple-element.72), channel_id=1, source_target_pairs={{0,64},{8,72},{16,80},{24,88},{32,96},{40,104},{48,112},{56,120},{... | collective-permute-start | bytes 1376264 | tf_op jit(solution)/shard_map/ppermute | solution.py:29
  18.1 1.9 %collective-permute-start.1 = (bf16[2,16,1024]{2,1,0:T(8,128)(2,1)S(1)}, bf16[2,16,1024]{2,1,0:T(8,128)(2,1)S(1)}, u32[]{:S(2)}, u32[]{:S(2)}) collective-permute-start(bf16[2,16,1024]{2,1,0:T(8,128)(2,1)S(1)} %get-tuple-element.69), channel_id=1, source_target_pairs={{0,16},{8,24},{16,0},{24,8},{32,48},{40,56},{48,32},{56,40},{64,80... | collective-permute-start | bytes 196616 | tf_op jit(solution)/shard_map/ppermute | solution.py:29
  20.0 2.2 %collective-permute-start.2 = (bf16[2,16,1024]{2,1,0:T(8,128)(2,1)S(1)}, bf16[2,16,1024]{2,1,0:T(8,128)(2,1)S(1)}, u32[]{:S(2)}, u32[]{:S(2)}) collective-permute-start(bf16[2,16,1024]{2,1,0:T(8,128)(2,1)S(1)} %get-tuple-element.70), channel_id=1, source_target_pairs={{0,128},{8,136},{16,144},{24,152},{32,160},{40,168},{48,176},{56,1... | collective-permute-start | bytes 196616 | tf_op jit(solution)/shard_map/ppermute | solution.py:29
  22.3 3.5 %collective-permute-start.3 = (bf16[2,16,1024]{2,1,0:T(8,128)(2,1)S(1)}, bf16[2,16,1024]{2,1,0:T(8,128)(2,1)S(1)}, u32[]{:S(2)}, u32[]{:S(2)}) collective-permute-start(bf16[2,16,1024]{2,1,0:T(8,128)(2,1)S(1)} %get-tuple-element.71), channel_id=1, source_target_pairs={{0,144},{8,152},{16,128},{24,136},{32,176},{40,184},{48,160},{56,1... | collective-permute-start | bytes 196616 | tf_op jit(solution)/shard_map/ppermute | solution.py:29
  25.8 2.5 %collective-permute-done.2.refs_2_ = bf16[2,16,1024]{2,1,0:T(8,128)(2,1)S(1)} collective-permute-done((bf16[2,16,1024]{2,1,0:T(8,128)(2,1)S(1)}, bf16[2,16,1024]{2,1,0:T(8,128)(2,1)S(1)}, u32[]{:S(2)}, u32[]{:S(2)}) %collective-permute-start.2) | collective-permute-done | bytes 65568 | tf_op jit(solution)/shard_map/ppermute | solution.py:29
  29.1 1.6 %collective-permute-done.4.refs_5_.refs_2_ = bf16[1792,128]{1,0:T(8,128)(2,1)S(1)} collective-permute-done((bf16[1792,128]{1,0:T(8,128)(2,1)S(1)}, bf16[1792,128]{1,0:T(8,128)(2,1)S(1)}, u32[]{:S(2)}, u32[]{:S(2)}) %collective-permute-start.4) | collective-permute-done | bytes 458784 | tf_op jit(solution)/shard_map/ppermute | solution.py:29
  30.8 1.7 %collective-permute-start.10 = (bf16[1792,128]{1,0:T(8,128)(2,1)S(1)}, bf16[1792,128]{1,0:T(8,128)(2,1)S(1)}, u32[]{:S(2)}, u32[]{:S(2)}) collective-permute-start(bf16[1792,128]{1,0:T(8,128)(2,1)S(1)} %get-tuple-element.77), channel_id=1, source_target_pairs={{0,48},{8,56},{16,32},{24,40},{32,16},{40,24},{48,0},{56,8},{64,11... | collective-permute-start | bytes 1376264 | tf_op jit(solution)/shard_map/ppermute | solution.py:29
  32.4 1.9 %collective-permute-start.11 = (bf16[128,1408]{1,0:T(8,128)(2,1)S(1)}, bf16[128,1408]{1,0:T(8,128)(2,1)S(1)}, u32[]{:S(2)}, u32[]{:S(2)}) collective-permute-start(bf16[128,1408]{1,0:T(8,128)(2,1)S(1)} %get-tuple-element.78), channel_id=1, source_target_pairs={{0,16},{8,24},{16,0},{24,8},{32,48},{40,56},{48,32},{56,40},{64,80... | collective-permute-start | bytes 1081352 | tf_op jit(solution)/shard_map/ppermute | solution.py:29
  37.2 2.1 %collective-permute-start.8 = (bf16[4,16,1024]{2,1,0:T(8,128)(2,1)S(1)}, bf16[4,16,1024]{2,1,0:T(8,128)(2,1)S(1)}, u32[]{:S(2)}, u32[]{:S(2)}) collective-permute-start(bf16[4,16,1024]{2,1,0:T(8,128)(2,1)S(1)} %get-tuple-element.75.far_ref), channel_id=1, source_target_pairs={{0,6},{1,7},{2,4},{3,5},{4,2},{5,3},{6,0},{7,1},{8,14},{9,15},{10,... | collective-permute-start | bytes 393224 | tf_op jit(solution)/shard_map/ppermute | solution.py:29
  40.7 2.7 %collective-permute-done.8.far_x = bf16[4,16,1024]{2,1,0:T(8,128)(2,1)S(1)} collective-permute-done((bf16[4,16,1024]{2,1,0:T(8,128)(2,1)S(1)}, bf16[4,16,1024]{2,1,0:T(8,128)(2,1)S(1)}, u32[]{:S(2)}, u32[]{:S(2)}) %collective-permute-start.8) | collective-permute-done | bytes 131104 | tf_op jit(solution)/shard_map/ppermute | solution.py:29
  43.4 1.9 %collective-permute-done.9.z1_ref = bf16[80,1408]{1,0:T(8,128)(2,1)S(1)} collective-permute-done((bf16[80,1408]{1,0:T(8,128)(2,1)S(1)}, bf16[80,1408]{1,0:T(8,128)(2,1)S(1)}, u32[]{:S(2)}, u32[]{:S(2)}) %collective-permute-start.9) | collective-permute-done | bytes 225312 | tf_op jit(solution)/shard_map/ppermute | solution.py:29
  49.2 2.8 %collective-permute-start.12 = (bf16[2,4,16,1024]{3,2,1,0:T(8,128)(2,1)S(1)}, bf16[2,4,16,1024]{3,2,1,0:T(8,128)(2,1)S(1)}, u32[]{:S(2)}, u32[]{:S(2)}) collective-permute-start(bf16[2,4,16,1024]{3,2,1,0:T(8,128)(2,1)S(1)} %get-tuple-element.79.refs_1_), channel_id=1, source_target_pairs={{0,6},{1,7},{2,4},{3,5},{4,2},{5,3},{6,0},{7,1},{8,14},{9,15},{10,... | collective-permute-start | bytes 786440 | tf_op jit(solution)/shard_map/ppermute | solution.py:29
  53.4 2.3 %collective-permute-done.14.refs_0_ = bf16[128,1408]{1,0:T(8,128)(2,1)S(1)} collective-permute-done((bf16[128,1408]{1,0:T(8,128)(2,1)S(1)}, bf16[128,1408]{1,0:T(8,128)(2,1)S(1)}, u32[]{:S(2)}, u32[]{:S(2)}) %collective-permute-start.14) | collective-permute-done | bytes 360480 | tf_op jit(solution)/shard_map/ppermute | solution.py:29
  56.8 1.5 %collective-permute-done.13.refs_4_ = bf16[2,4,16,1024]{3,2,1,0:T(8,128)(2,1)S(1)} collective-permute-done((bf16[2,4,16,1024]{3,2,1,0:T(8,128)(2,1)S(1)}, bf16[2,4,16,1024]{3,2,1,0:T(8,128)(2,1)S(1)}, u32[]{:S(2)}, u32[]{:S(2)}) %collective-permute-start.13) | collective-permute-done | bytes 262176 | tf_op jit(solution)/shard_map/ppermute | solution.py:29
  58.4 2.1 %shard_map.73 = (bf16[4,1792,128]{2,1,0:T(8,128)(2,1)S(1)}, bf16[4,1792,128]{2,1,0:T(8,128)(2,1)S(1)}, bf16[512,1024]{1,0:T(8,128)(2,1)S(1)}) custom-call(s32[1]{0:T(128)} %bitcast.1.refs_0_.place_ref, bf16[2,4,16,1024]{3,2,1,0:T(8,128)(2,1)S(1)} %get-tuple-element.79.refs_1_, bf16[2,4,16,1024]{3,2,1,0:T(8,128)(2,1)S(1)} %collective-permute-done.12.refs_2_, ...), custom_call_target="tpu_custom_call" | custom-call | flops 5000000000 | bytes 1 | tf_op jit(solution)/shard_map/pallas_call | solution.py:331
  60.6 2.1 %shard_map.74 = (bf16[4,16,1024]{2,1,0:T(8,128)(2,1)S(1)}, bf16[4,16,1024]{2,1,0:T(8,128)(2,1)S(1)}, bf16[2,4,16,1024]{3,2,1,0:T(8,128)(2,1)S(1)}, bf16[4,16,102...) custom-call(s32[1]{0:T(128)} %bitcast.1.refs_0_.place_ref, ...), custom_call_target="tpu_custom_call" | custom-call | flops 5000000000 | bytes 1 | tf_op jit(solution)/shard_map/pallas_call | solution.py:331
  64.9 1.6 %collective-permute-start.17 = (bf16[2,896,128]{2,1,0:T(8,128)(2,1)S(1)}, bf16[2,896,128]{2,1,0:T(8,128)(2,1)S(1)}, u32[]{:S(2)}, u32[]{:S(2)}) collective-permute-start(bf16[2,896,128]{2,1,0:T(8,128)(2,1)S(1)} %get-tuple-element.92.refs_6_), channel_id=1, source_target_pairs={{0,48},{8,56},{16,32},{24,40},{32,16},{40,24},{48,0},{56,8},{64,11... | collective-permute-start | bytes 1376264 | tf_op jit(solution)/shard_map/ppermute | solution.py:29
  66.5 3.5 %shard_map.76 = (bf16[128,1792]{1,0:T(8,128)(2,1)S(1)}, bf16[128,896]{1,0:T(8,128)(2,1)S(1)}, bf16[2,64,896]{2,1,0:T(8,128)(2,1)S(1)}, bf16[2,64,896]{2,1,0:T(8,128)(2,1)S(1)}) custom-call(bf16[512,1024]{1,0:T(8,128)(2,1)S(1)} %get-tuple-element.93.rows_ref, bf16[4,1792,128]{2,1,0:T(8,128)(2,1)S(1)} %copy-done.3, ...), custom_call_target="tpu_custom_call" | custom-call | flops 5000000000 | bytes 1 | tf_op jit(solution)/shard_map/pallas_call | solution.py:331
  70.0 1.6 %collective-permute-start.18 = (bf16[2,64,896]{2,1,0:T(8,128)(2,1)S(1)}, bf16[2,64,896]{2,1,0:T(8,128)(2,1)S(1)}, u32[]{:S(2)}, u32[]{:S(2)}) collective-permute-start(bf16[2,64,896]{2,1,0:T(8,128)(2,1)S(1)} %get-tuple-element.101), channel_id=1, source_target_pairs={{0,16},{8,24},{16,0},{24,8},{32,48},{40,56},{48,32},{56,40},{64,80... | collective-permute-start | bytes 688136 | tf_op jit(solution)/shard_map/ppermute | solution.py:29
  74.4 4.9 %collective-permute-done.21.first_far = bf16[4,16,1024]{2,1,0:T(8,128)(2,1)S(1)} collective-permute-done((bf16[4,16,1024]{2,1,0:T(8,128)(2,1)S(1)}, bf16[4,16,1024]{2,1,0:T(8,128)(2,1)S(1)}, u32[]{:S(2)}, u32[]{:S(2)}) %collective-permute-start.21) | collective-permute-done | bytes 131104 | tf_op jit(solution)/shard_map/ppermute | solution.py:29
  79.5 1.6 %collective-permute-start.23 = (bf16[2,896,128]{2,1,0:T(8,128)(2,1)S(1)}, bf16[2,896,128]{2,1,0:T(8,128)(2,1)S(1)}, u32[]{:S(2)}, u32[]{:S(2)}) collective-permute-start(bf16[2,896,128]{2,1,0:T(8,128)(2,1)S(1)} %get-tuple-element.113), channel_id=1, source_target_pairs={{0,48},{8,56},{16,32},{24,40},{32,16},{40,24},{48,0},{56,8},{64,11... | collective-permute-start | bytes 1376264 | tf_op jit(solution)/shard_map/ppermute | solution.py:29
  81.1 1.9 %collective-permute-start.24 = (bf16[896,128]{1,0:T(8,128)(2,1)S(1)}, bf16[896,128]{1,0:T(8,128)(2,1)S(1)}, u32[]{:S(2)}, u32[]{:S(2)}) collective-permute-start(bf16[896,128]{1,0:T(8,128)(2,1)S(1)} %get-tuple-element.114), channel_id=1, source_target_pairs={{0,64},{8,72},{16,80},{24,88},{32,96},{40,104},{48,112},{56,120},{... | collective-permute-start | bytes 688136 | tf_op jit(solution)/shard_map/ppermute | solution.py:29
  83.8 4.8 %collective-permute-start.26 = (bf16[4,16,1024]{2,1,0:T(8,128)(2,1)S(1)}, bf16[4,16,1024]{2,1,0:T(8,128)(2,1)S(1)}, u32[]{:S(2)}, u32[]{:S(2)}) collective-permute-start(bf16[4,16,1024]{2,1,0:T(8,128)(2,1)S(1)} %get-tuple-element.117), channel_id=1, source_target_pairs={{0,1},{1,0},{2,3},{3,2},{4,5},{5,4},{6,7},{7,6},{8,9},{9,8},{10,11... | collective-permute-start | bytes 393224 | tf_op jit(solution)/shard_map/ppermute | solution.py:29
  88.6 3.4 %collective-permute-start.27 = (bf16[64,896]{1,0:T(8,128)(2,1)S(1)}, bf16[64,896]{1,0:T(8,128)(2,1)S(1)}, u32[]{:S(2)}, u32[]{:S(2)}) collective-permute-start(bf16[64,896]{1,0:T(8,128)(2,1)S(1)} %get-tuple-element.118), channel_id=1, source_target_pairs={{0,128},{8,136},{16,144},{24,152},{32,160},{40,168},{48,176},{56,1... | collective-permute-start | bytes 344072 | tf_op jit(solution)/shard_map/ppermute | solution.py:29
  92.0 7.6 %collective-permute-done.27.refs_1_.refs_8_ = bf16[64,896]{1,0:T(8,128)(2,1)S(1)} collective-permute-done((bf16[64,896]{1,0:T(8,128)(2,1)S(1)}, bf16[64,896]{1,0:T(8,128)(2,1)S(1)}, u32[]{:S(2)}, u32[]{:S(2)}) %collective-permute-start.27) | collective-permute-done | bytes 114720 | tf_op jit(solution)/shard_map/ppermute | solution.py:29
  99.8 3.1 %collective-permute-start.29 = (bf16[64,896]{1,0:T(8,128)(2,1)S(1)}, bf16[64,896]{1,0:T(8,128)(2,1)S(1)}, u32[]{:S(2)}, u32[]{:S(2)}) collective-permute-start(bf16[64,896]{1,0:T(8,128)(2,1)S(1)} %get-tuple-element.121), channel_id=1, source_target_pairs={{0,128},{8,136},{16,144},{24,152},{32,160},{40,168},{48,176},{56,1... | collective-permute-start | bytes 344072 | tf_op jit(solution)/shard_map/ppermute | solution.py:29
  104.4 2.9 %collective-permute-start.32 = (bf16[16,1024]{1,0:T(8,128)(2,1)S(1)}, bf16[16,1024]{1,0:T(8,128)(2,1)S(1)}, u32[]{:S(2)}, u32[]{:S(2)}) collective-permute-start(bf16[16,1024]{1,0:T(8,128)(2,1)S(1)} %get-tuple-element.127), channel_id=1, source_target_pairs={{0,144},{8,152},{16,128},{24,136},{32,176},{40,184},{48,160},{56,1... | collective-permute-start | bytes 98312 | tf_op jit(solution)/shard_map/ppermute | solution.py:29
  107.3 1.7 %collective-permute-done.31.refs_14_ = bf16[16,1024]{1,0:T(8,128)(2,1)S(1)} collective-permute-done((bf16[16,1024]{1,0:T(8,128)(2,1)S(1)}, bf16[16,1024]{1,0:T(8,128)(2,1)S(1)}, u32[]{:S(2)}, u32[]{:S(2)}) %collective-permute-start.31) | collective-permute-done | bytes 32800 | tf_op jit(solution)/shard_map/ppermute | solution.py:29
  109.0 3.3 %collective-permute-done.32.refs_15_ = bf16[16,1024]{1,0:T(8,128)(2,1)S(1)} collective-permute-done((bf16[16,1024]{1,0:T(8,128)(2,1)S(1)}, bf16[16,1024]{1,0:T(8,128)(2,1)S(1)}, u32[]{:S(2)}, u32[]{:S(2)}) %collective-permute-start.32) | collective-permute-done | bytes 32800 | tf_op jit(solution)/shard_map/ppermute | solution.py:29
  112.3 1.7 %shard_map.80 = (bf16[1792,128]{1,0:T(8,128)(2,1)}, bf16[128,1792]{1,0:T(8,128)(2,1)}, bf16[16,4096]{1,0:T(8,128)(2,1)}) custom-call(s32[1]{0:T(128)} %bitcast.place_ref, f32[2,1792,128]{2,1,0:T(8,128)S(1)} %get-tuple-element.91.sum_ref.refs_0_, bf16[2,896,128]{2,1,0:T(8,128)(2,1)S(1)} %collective-permute-done.17.far0_ref.refs_1_, ...), custom_call_target="tpu_custom_call" | custom-call | flops 1 | bytes 1 | tf_op jit(solution)/shard_map/pallas_call | solution.py:331
  (62 shorter events, 24.1 us)
Async XLA Ops:
  0.6 11.1 %collective-permute-start = (bf16[16,4096]{1,0:T(8,128)(2,1)}, bf16[16,4096]{1,0:T(8,128)(2,1)S(1)}, u32[]{:S(2)}, u32[]{:S(2)}) collective-permute-start(bf16[16,4096]{1,0:T(8,128)(2,1)} %grad_ref.1), channel_id=1, source_target_pairs={{0,1},{1,0},{2,3},{3,2},{4,5},{5,4},{6,7},{7,6},{8,9},{9,8},{10,11... | collective-permute-start | bytes 393224 | tf_op jit(solution)/shard_map/ppermute | solution.py:29
  11.8 17.2 %collective-permute-start.6 = (bf16[1792,128]{1,0:T(8,128)(2,1)S(1)}, bf16[1792,128]{1,0:T(8,128)(2,1)S(1)}, u32[]{:S(2)}, u32[]{:S(2)}) collective-permute-start(bf16[1792,128]{1,0:T(8,128)(2,1)S(1)} %get-tuple-element.72), channel_id=1, source_target_pairs={{0,48},{8,56},{16,32},{24,40},{32,16},{40,24},{48,0},{56,8},{64,11... | collective-permute-start | bytes 1376264 | tf_op jit(solution)/shard_map/ppermute | solution.py:29
  13.5 17.2 %collective-permute-start.4 = (bf16[1792,128]{1,0:T(8,128)(2,1)S(1)}, bf16[1792,128]{1,0:T(8,128)(2,1)S(1)}, u32[]{:S(2)}, u32[]{:S(2)}) collective-permute-start(bf16[1792,128]{1,0:T(8,128)(2,1)S(1)} %get-tuple-element.72), channel_id=1, source_target_pairs={{0,64},{8,72},{16,80},{24,88},{32,96},{40,104},{48,112},{56,120},{... | collective-permute-start | bytes 1376264 | tf_op jit(solution)/shard_map/ppermute | solution.py:29
  17.3 11.7 %collective-permute-start.5 = (bf16[48,1408]{1,0:T(8,128)(2,1)S(1)}, bf16[48,1408]{1,0:T(8,128)(2,1)S(1)}, u32[]{:S(2)}, u32[]{:S(2)}) collective-permute-start(bf16[48,1408]{1,0:T(8,128)(2,1)S(1)} %get-tuple-element.73), channel_id=1, source_target_pairs={{0,128},{8,136},{16,144},{24,152},{32,160},{40,168},{48,176},{56,1... | collective-permute-start | bytes 405512 | tf_op jit(solution)/shard_map/ppermute | solution.py:29
  18.1 4.3 %collective-permute-start.1 = (bf16[2,16,1024]{2,1,0:T(8,128)(2,1)S(1)}, bf16[2,16,1024]{2,1,0:T(8,128)(2,1)S(1)}, u32[]{:S(2)}, u32[]{:S(2)}) collective-permute-start(bf16[2,16,1024]{2,1,0:T(8,128)(2,1)S(1)} %get-tuple-element.69), channel_id=1, source_target_pairs={{0,16},{8,24},{16,0},{24,8},{32,48},{40,56},{48,32},{56,40},{64,80... | collective-permute-start | bytes 196616 | tf_op jit(solution)/shard_map/ppermute | solution.py:29
  20.0 8.4 %collective-permute-start.2 = (bf16[2,16,1024]{2,1,0:T(8,128)(2,1)S(1)}, bf16[2,16,1024]{2,1,0:T(8,128)(2,1)S(1)}, u32[]{:S(2)}, u32[]{:S(2)}) collective-permute-start(bf16[2,16,1024]{2,1,0:T(8,128)(2,1)S(1)} %get-tuple-element.70), channel_id=1, source_target_pairs={{0,128},{8,136},{16,144},{24,152},{32,160},{40,168},{48,176},{56,1... | collective-permute-start | bytes 196616 | tf_op jit(solution)/shard_map/ppermute | solution.py:29
  22.3 6.7 %collective-permute-start.3 = (bf16[2,16,1024]{2,1,0:T(8,128)(2,1)S(1)}, bf16[2,16,1024]{2,1,0:T(8,128)(2,1)S(1)}, u32[]{:S(2)}, u32[]{:S(2)}) collective-permute-start(bf16[2,16,1024]{2,1,0:T(8,128)(2,1)S(1)} %get-tuple-element.71), channel_id=1, source_target_pairs={{0,144},{8,152},{16,128},{24,136},{32,176},{40,184},{48,160},{56,1... | collective-permute-start | bytes 196616 | tf_op jit(solution)/shard_map/ppermute | solution.py:29
  30.8 14.5 %collective-permute-start.10 = (bf16[1792,128]{1,0:T(8,128)(2,1)S(1)}, bf16[1792,128]{1,0:T(8,128)(2,1)S(1)}, u32[]{:S(2)}, u32[]{:S(2)}) collective-permute-start(bf16[1792,128]{1,0:T(8,128)(2,1)S(1)} %get-tuple-element.77), channel_id=1, source_target_pairs={{0,48},{8,56},{16,32},{24,40},{32,16},{40,24},{48,0},{56,8},{64,11... | collective-permute-start | bytes 1376264 | tf_op jit(solution)/shard_map/ppermute | solution.py:29
  32.4 12.8 %collective-permute-start.11 = (bf16[128,1408]{1,0:T(8,128)(2,1)S(1)}, bf16[128,1408]{1,0:T(8,128)(2,1)S(1)}, u32[]{:S(2)}, u32[]{:S(2)}) collective-permute-start(bf16[128,1408]{1,0:T(8,128)(2,1)S(1)} %get-tuple-element.78), channel_id=1, source_target_pairs={{0,16},{8,24},{16,0},{24,8},{32,48},{40,56},{48,32},{56,40},{64,80... | collective-permute-start | bytes 1081352 | tf_op jit(solution)/shard_map/ppermute | solution.py:29
  34.3 10.9 %collective-permute-start.9 = (bf16[80,1408]{1,0:T(8,128)(2,1)S(1)}, bf16[80,1408]{1,0:T(8,128)(2,1)S(1)}, u32[]{:S(2)}, u32[]{:S(2)}) collective-permute-start(bf16[80,1408]{1,0:T(8,128)(2,1)S(1)} %get-tuple-element.76), channel_id=1, source_target_pairs={{0,128},{8,136},{16,144},{24,152},{32,160},{40,168},{48,176},{56,1... | collective-permute-start | bytes 675848 | tf_op jit(solution)/shard_map/ppermute | solution.py:29
  35.7 5.0 %collective-permute-start.7 = (bf16[4,16,1024]{2,1,0:T(8,128)(2,1)S(1)}, bf16[4,16,1024]{2,1,0:T(8,128)(2,1)S(1)}, u32[]{:S(2)}, u32[]{:S(2)}) collective-permute-start(bf16[4,16,1024]{2,1,0:T(8,128)(2,1)S(1)} %get-tuple-element.74.near_ref), channel_id=1, source_target_pairs={{0,2},{1,3},{2,0},{3,1},{4,6},{5,7},{6,4},{7,5},{8,10},{9,11},{10,... | collective-permute-start | bytes 393224 | tf_op jit(solution)/shard_map/ppermute | solution.py:29
  37.2 6.2 %collective-permute-start.8 = (bf16[4,16,1024]{2,1,0:T(8,128)(2,1)S(1)}, bf16[4,16,1024]{2,1,0:T(8,128)(2,1)S(1)}, u32[]{:S(2)}, u32[]{:S(2)}) collective-permute-start(bf16[4,16,1024]{2,1,0:T(8,128)(2,1)S(1)} %get-tuple-element.75.far_ref), channel_id=1, source_target_pairs={{0,6},{1,7},{2,4},{3,5},{4,2},{5,3},{6,0},{7,1},{8,14},{9,15},{10,... | collective-permute-start | bytes 393224 | tf_op jit(solution)/shard_map/ppermute | solution.py:29
  48.3 7.4 %collective-permute-start.14 = (bf16[128,1408]{1,0:T(8,128)(2,1)S(1)}, bf16[128,1408]{1,0:T(8,128)(2,1)S(1)}, u32[]{:S(2)}, u32[]{:S(2)}) collective-permute-start(bf16[128,1408]{1,0:T(8,128)(2,1)S(1)} %get-tuple-element.82.refs_1_), channel_id=1, source_target_pairs={{0,16},{8,24},{16,0},{24,8},{32,48},{40,56},{48,32},{56,40},{64,80... | collective-permute-start | bytes 1081352 | tf_op jit(solution)/shard_map/ppermute | solution.py:29
  49.2 7.6 %collective-permute-start.12 = (bf16[2,4,16,1024]{3,2,1,0:T(8,128)(2,1)S(1)}, bf16[2,4,16,1024]{3,2,1,0:T(8,128)(2,1)S(1)}, u32[]{:S(2)}, u32[]{:S(2)}) collective-permute-start(bf16[2,4,16,1024]{3,2,1,0:T(8,128)(2,1)S(1)} %get-tuple-element.79.refs_1_), channel_id=1, source_target_pairs={{0,6},{1,7},{2,4},{3,5},{4,2},{5,3},{6,0},{7,1},{8,14},{9,15},{10,... | collective-permute-start | bytes 786440 | tf_op jit(solution)/shard_map/ppermute | solution.py:29
  52.0 6.4 %collective-permute-start.13 = (bf16[2,4,16,1024]{3,2,1,0:T(8,128)(2,1)S(1)}, bf16[2,4,16,1024]{3,2,1,0:T(8,128)(2,1)S(1)}, u32[]{:S(2)}, u32[]{:S(2)}) collective-permute-start(bf16[2,4,16,1024]{3,2,1,0:T(8,128)(2,1)S(1)} %get-tuple-element.80.refs_3_), channel_id=1, source_target_pairs={{0,2},{1,3},{2,0},{3,1},{4,6},{5,7},{6,4},{7,5},{8,10},{9,11},{10,... | collective-permute-start | bytes 786440 | tf_op jit(solution)/shard_map/ppermute | solution.py:29
  52.2 8.4 %collective-permute-start.16 = (bf16[4,1792,128]{2,1,0:T(8,128)(2,1)}, bf16[4,1792,128]{2,1,0:T(8,128)(2,1)S(1)}, u32[]{:S(2)}, u32[]{:S(2)}) collective-permute-start(bf16[4,1792,128]{2,1,0:T(8,128)(2,1)} %copy-done.4), channel_id=1, source_target_pairs={{0,8},{8,0},{16,24},{24,16},{32,40},{40,32},{48,56},{56,48},{64,72... | collective-permute-start | bytes 5505032 | tf_op jit(solution)/shard_map/ppermute | solution.py:29
  62.8 8.9 %collective-permute-start.19 = (bf16[2,4,16,1024]{3,2,1,0:T(8,128)(2,1)S(1)}, bf16[2,4,16,1024]{3,2,1,0:T(8,128)(2,1)S(1)}, u32[]{:S(2)}, u32[]{:S(2)}) collective-permute-start(bf16[2,4,16,1024]{3,2,1,0:T(8,128)(2,1)S(1)} %get-tuple-element.103), channel_id=1, source_target_pairs={{0,2},{1,3},{2,0},{3,1},{4,6},{5,7},{6,4},{7,5},{8,10},{9,11},{10,... | collective-permute-start | bytes 786440 | tf_op jit(solution)/shard_map/ppermute | solution.py:29
  63.1 9.8 %collective-permute-start.20 = (bf16[2,4,16,1024]{3,2,1,0:T(8,128)(2,1)S(1)}, bf16[2,4,16,1024]{3,2,1,0:T(8,128)(2,1)S(1)}, u32[]{:S(2)}, u32[]{:S(2)}) collective-permute-start(bf16[2,4,16,1024]{3,2,1,0:T(8,128)(2,1)S(1)} %get-tuple-element.106), channel_id=1, source_target_pairs={{0,6},{1,7},{2,4},{3,5},{4,2},{5,3},{6,0},{7,1},{8,14},{9,15},{10,... | collective-permute-start | bytes 786440 | tf_op jit(solution)/shard_map/ppermute | solution.py:29
  64.9 14.4 %collective-permute-start.17 = (bf16[2,896,128]{2,1,0:T(8,128)(2,1)S(1)}, bf16[2,896,128]{2,1,0:T(8,128)(2,1)S(1)}, u32[]{:S(2)}, u32[]{:S(2)}) collective-permute-start(bf16[2,896,128]{2,1,0:T(8,128)(2,1)S(1)} %get-tuple-element.92.refs_6_), channel_id=1, source_target_pairs={{0,48},{8,56},{16,32},{24,40},{32,16},{40,24},{48,0},{56,8},{64,11... | collective-permute-start | bytes 1376264 | tf_op jit(solution)/shard_map/ppermute | solution.py:29
  70.0 9.3 %collective-permute-start.18 = (bf16[2,64,896]{2,1,0:T(8,128)(2,1)S(1)}, bf16[2,64,896]{2,1,0:T(8,128)(2,1)S(1)}, u32[]{:S(2)}, u32[]{:S(2)}) collective-permute-start(bf16[2,64,896]{2,1,0:T(8,128)(2,1)S(1)} %get-tuple-element.101), channel_id=1, source_target_pairs={{0,16},{8,24},{16,0},{24,8},{32,48},{40,56},{48,32},{56,40},{64,80... | collective-permute-start | bytes 688136 | tf_op jit(solution)/shard_map/ppermute | solution.py:29
  73.0 6.3 %collective-permute-start.21 = (bf16[4,16,1024]{2,1,0:T(8,128)(2,1)S(1)}, bf16[4,16,1024]{2,1,0:T(8,128)(2,1)S(1)}, u32[]{:S(2)}, u32[]{:S(2)}) collective-permute-start(bf16[4,16,1024]{2,1,0:T(8,128)(2,1)S(1)} %get-tuple-element.108), channel_id=1, source_target_pairs={{0,6},{1,7},{2,4},{3,5},{4,2},{5,3},{6,0},{7,1},{8,14},{9,15},{10,... | collective-permute-start | bytes 393224 | tf_op jit(solution)/shard_map/ppermute | solution.py:29
  74.4 5.0 %collective-permute-start.22 = (bf16[4,16,1024]{2,1,0:T(8,128)(2,1)S(1)}, bf16[4,16,1024]{2,1,0:T(8,128)(2,1)S(1)}, u32[]{:S(2)}, u32[]{:S(2)}) collective-permute-start(bf16[4,16,1024]{2,1,0:T(8,128)(2,1)S(1)} %get-tuple-element.110), channel_id=1, source_target_pairs={{0,2},{1,3},{2,0},{3,1},{4,6},{5,7},{6,4},{7,5},{8,10},{9,11},{10,... | collective-permute-start | bytes 393224 | tf_op jit(solution)/shard_map/ppermute | solution.py:29
  79.5 20.1 %collective-permute-start.23 = (bf16[2,896,128]{2,1,0:T(8,128)(2,1)S(1)}, bf16[2,896,128]{2,1,0:T(8,128)(2,1)S(1)}, u32[]{:S(2)}, u32[]{:S(2)}) collective-permute-start(bf16[2,896,128]{2,1,0:T(8,128)(2,1)S(1)} %get-tuple-element.113), channel_id=1, source_target_pairs={{0,48},{8,56},{16,32},{24,40},{32,16},{40,24},{48,0},{56,8},{64,11... | collective-permute-start | bytes 1376264 | tf_op jit(solution)/shard_map/ppermute | solution.py:29
  81.1 18.5 %collective-permute-start.24 = (bf16[896,128]{1,0:T(8,128)(2,1)S(1)}, bf16[896,128]{1,0:T(8,128)(2,1)S(1)}, u32[]{:S(2)}, u32[]{:S(2)}) collective-permute-start(bf16[896,128]{1,0:T(8,128)(2,1)S(1)} %get-tuple-element.114), channel_id=1, source_target_pairs={{0,64},{8,72},{16,80},{24,88},{32,96},{40,104},{48,112},{56,120},{... | collective-permute-start | bytes 688136 | tf_op jit(solution)/shard_map/ppermute | solution.py:29
  82.9 16.6 %collective-permute-start.25 = (bf16[2,64,896]{2,1,0:T(8,128)(2,1)S(1)}, bf16[2,64,896]{2,1,0:T(8,128)(2,1)S(1)}, u32[]{:S(2)}, u32[]{:S(2)}) collective-permute-start(bf16[2,64,896]{2,1,0:T(8,128)(2,1)S(1)} %get-tuple-element.115), channel_id=1, source_target_pairs={{0,16},{8,24},{16,0},{24,8},{32,48},{40,56},{48,32},{56,40},{64,80... | collective-permute-start | bytes 688136 | tf_op jit(solution)/shard_map/ppermute | solution.py:29
  83.8 15.7 %collective-permute-start.26 = (bf16[4,16,1024]{2,1,0:T(8,128)(2,1)S(1)}, bf16[4,16,1024]{2,1,0:T(8,128)(2,1)S(1)}, u32[]{:S(2)}, u32[]{:S(2)}) collective-permute-start(bf16[4,16,1024]{2,1,0:T(8,128)(2,1)S(1)} %get-tuple-element.117), channel_id=1, source_target_pairs={{0,1},{1,0},{2,3},{3,2},{4,5},{5,4},{6,7},{7,6},{8,9},{9,8},{10,11... | collective-permute-start | bytes 393224 | tf_op jit(solution)/shard_map/ppermute | solution.py:29
  88.6 11.0 %collective-permute-start.27 = (bf16[64,896]{1,0:T(8,128)(2,1)S(1)}, bf16[64,896]{1,0:T(8,128)(2,1)S(1)}, u32[]{:S(2)}, u32[]{:S(2)}) collective-permute-start(bf16[64,896]{1,0:T(8,128)(2,1)S(1)} %get-tuple-element.118), channel_id=1, source_target_pairs={{0,128},{8,136},{16,144},{24,152},{32,160},{40,168},{48,176},{56,1... | collective-permute-start | bytes 344072 | tf_op jit(solution)/shard_map/ppermute | solution.py:29
  99.7 12.6 %collective-permute-start.28 = (bf16[896,128]{1,0:T(8,128)(2,1)S(1)}, bf16[896,128]{1,0:T(8,128)(2,1)S(1)}, u32[]{:S(2)}, u32[]{:S(2)}) collective-permute-start(bf16[896,128]{1,0:T(8,128)(2,1)S(1)} %get-tuple-element.119), channel_id=1, source_target_pairs={{0,64},{8,72},{16,80},{24,88},{32,96},{40,104},{48,112},{56,120},{... | collective-permute-start | bytes 688136 | tf_op jit(solution)/shard_map/ppermute | solution.py:29
  99.8 12.5 %collective-permute-start.29 = (bf16[64,896]{1,0:T(8,128)(2,1)S(1)}, bf16[64,896]{1,0:T(8,128)(2,1)S(1)}, u32[]{:S(2)}, u32[]{:S(2)}) collective-permute-start(bf16[64,896]{1,0:T(8,128)(2,1)S(1)} %get-tuple-element.121), channel_id=1, source_target_pairs={{0,128},{8,136},{16,144},{24,152},{32,160},{40,168},{48,176},{56,1... | collective-permute-start | bytes 344072 | tf_op jit(solution)/shard_map/ppermute | solution.py:29
  102.9 4.4 %collective-permute-start.30 = (bf16[16,1024]{1,0:T(8,128)(2,1)S(1)}, bf16[16,1024]{1,0:T(8,128)(2,1)S(1)}, u32[]{:S(2)}, u32[]{:S(2)}) collective-permute-start(bf16[16,1024]{1,0:T(8,128)(2,1)S(1)} %get-tuple-element.125), channel_id=1, source_target_pairs={{0,16},{8,24},{16,0},{24,8},{32,48},{40,56},{48,32},{56,40},{64,80... | collective-permute-start | bytes 98312 | tf_op jit(solution)/shard_map/ppermute | solution.py:29
  103.9 5.1 %collective-permute-start.31 = (bf16[16,1024]{1,0:T(8,128)(2,1)S(1)}, bf16[16,1024]{1,0:T(8,128)(2,1)S(1)}, u32[]{:S(2)}, u32[]{:S(2)}) collective-permute-start(bf16[16,1024]{1,0:T(8,128)(2,1)S(1)} %get-tuple-element.126), channel_id=1, source_target_pairs={{0,128},{8,136},{16,144},{24,152},{32,160},{40,168},{48,176},{56,1... | collective-permute-start | bytes 98312 | tf_op jit(solution)/shard_map/ppermute | solution.py:29
  104.4 7.8 %collective-permute-start.32 = (bf16[16,1024]{1,0:T(8,128)(2,1)S(1)}, bf16[16,1024]{1,0:T(8,128)(2,1)S(1)}, u32[]{:S(2)}, u32[]{:S(2)}) collective-permute-start(bf16[16,1024]{1,0:T(8,128)(2,1)S(1)} %get-tuple-element.127), channel_id=1, source_target_pairs={{0,144},{8,152},{16,128},{24,136},{32,176},{40,184},{48,160},{56,1... | collective-permute-start | bytes 98312 | tf_op jit(solution)/shard_map/ppermute | solution.py:29
  (8 other events, 14.5 us)

commit v6 on v4

--- a/solution.py
+++ b/solution.py
@@ -22,7 +22,7 @@
 KEPT = 3 * 256 + 128
 CHUNKS = ((0, 512, 0, 0), (512, 1024, 384, 256), (1024, 1536, 768, 512), (1536, 1792, 1152, 768))
 EARLY = 64
-FIRST = 48
+FIRST = 64
 
 
 def swap(array, axis, size, k):

time: 113 us -> 113 us (level)
  waiting for transfers between devices: 34.7 us -> 33.4 us
    ppermute x33, waiting for transfers between devices: 34.7 us -> 33.4 us  [swap(): return lax.ppermute(array, axis, [(i, i ^ k) for i in range(size)])]
  transfers between devices with their start and end apart: 33 -> 33, of which waited for: 17 -> 16; matrix products, arithmetic and copies ran while one was open for 0% -> 0% of each run, Pallas kernels for 10% -> 10%
where the time goes in v6:
time: 113 us; the launch traced here: 112 us
  starting transfers between devices  61.2 us (54%)
  waiting for transfers between devices  33.4 us (30%)
  Pallas kernels  13.6 us (12%)
  local copies, waits for them, and re-layouts  3.22 us (3%)
    ppermute x33, starting transfers between devices, swap(): return lax.ppermute(array, axis, [(i, i ^ k) for i in range(size)])  61.2 us
    ppermute x33, waiting for transfers between devices, swap(): return lax.ppermute(array, axis, [(i, i ^ k) for i in range(size)])  33.4 us
    pallas_call x14, Pallas kernels, move(): call(kernel, out_shape, in_specs=[in_smem() if a.dtype == jnp.int32 and a...  13.6 us
    unnamed x12, local copies, waits for them, and re-layouts  3.22 us
  transfers between devices with their start and end apart: 33, of which 16 were waited for; matrix products, arithmetic and copies ran while one was open for 0% of the time, Pallas kernels for 10%

profile of v6, /device:TPU:8, one launch (start us, length us, event | category | flops | bytes accessed | tf_op | source)
XLA Modules:
  0.0 112.2 jit_solution(11211363612115374350)
XLA Ops:
  0.6 7.3 %collective-permute-start = (bf16[16,4096]{1,0:T(8,128)(2,1)}, bf16[16,4096]{1,0:T(8,128)(2,1)S(1)}, u32[]{:S(2)}, u32[]{:S(2)}) collective-permute-start(bf16[16,4096]{1,0:T(8,128)(2,1)} %grad_ref.1), channel_id=1, source_target_pairs={{0,1},{1,0},{2,3},{3,2},{4,5},{5,4},{6,7},{7,6},{8,9},{9,8},{10,11... | collective-permute-start | bytes 393224 | tf_op jit(solution)/shard_map/ppermute | solution.py:29
  11.8 1.7 %collective-permute-start.6 = (bf16[1792,128]{1,0:T(8,128)(2,1)S(1)}, bf16[1792,128]{1,0:T(8,128)(2,1)S(1)}, u32[]{:S(2)}, u32[]{:S(2)}) collective-permute-start(bf16[1792,128]{1,0:T(8,128)(2,1)S(1)} %get-tuple-element.71), channel_id=1, source_target_pairs={{0,48},{8,56},{16,32},{24,40},{32,16},{40,24},{48,0},{56,8},{64,11... | collective-permute-start | bytes 1376264 | tf_op jit(solution)/shard_map/ppermute | solution.py:29
  13.5 3.8 %collective-permute-start.4 = (bf16[1792,128]{1,0:T(8,128)(2,1)S(1)}, bf16[1792,128]{1,0:T(8,128)(2,1)S(1)}, u32[]{:S(2)}, u32[]{:S(2)}) collective-permute-start(bf16[1792,128]{1,0:T(8,128)(2,1)S(1)} %get-tuple-element.71), channel_id=1, source_target_pairs={{0,64},{8,72},{16,80},{24,88},{32,96},{40,104},{48,112},{56,120},{... | collective-permute-start | bytes 1376264 | tf_op jit(solution)/shard_map/ppermute | solution.py:29
  18.1 1.9 %collective-permute-start.1 = (bf16[2,16,1024]{2,1,0:T(8,128)(2,1)S(1)}, bf16[2,16,1024]{2,1,0:T(8,128)(2,1)S(1)}, u32[]{:S(2)}, u32[]{:S(2)}) collective-permute-start(bf16[2,16,1024]{2,1,0:T(8,128)(2,1)S(1)} %get-tuple-element.68), channel_id=1, source_target_pairs={{0,16},{8,24},{16,0},{24,8},{32,48},{40,56},{48,32},{56,40},{64,80... | collective-permute-start | bytes 196616 | tf_op jit(solution)/shard_map/ppermute | solution.py:29
  20.0 2.2 %collective-permute-start.2 = (bf16[2,16,1024]{2,1,0:T(8,128)(2,1)S(1)}, bf16[2,16,1024]{2,1,0:T(8,128)(2,1)S(1)}, u32[]{:S(2)}, u32[]{:S(2)}) collective-permute-start(bf16[2,16,1024]{2,1,0:T(8,128)(2,1)S(1)} %get-tuple-element.69), channel_id=1, source_target_pairs={{0,128},{8,136},{16,144},{24,152},{32,160},{40,168},{48,176},{56,1... | collective-permute-start | bytes 196616 | tf_op jit(solution)/shard_map/ppermute | solution.py:29
  22.3 3.5 %collective-permute-start.3 = (bf16[2,16,1024]{2,1,0:T(8,128)(2,1)S(1)}, bf16[2,16,1024]{2,1,0:T(8,128)(2,1)S(1)}, u32[]{:S(2)}, u32[]{:S(2)}) collective-permute-start(bf16[2,16,1024]{2,1,0:T(8,128)(2,1)S(1)} %get-tuple-element.70), channel_id=1, source_target_pairs={{0,144},{8,152},{16,128},{24,136},{32,176},{40,184},{48,160},{56,1... | collective-permute-start | bytes 196616 | tf_op jit(solution)/shard_map/ppermute | solution.py:29
  25.8 3.5 %collective-permute-done.2.refs_2_ = bf16[2,16,1024]{2,1,0:T(8,128)(2,1)S(1)} collective-permute-done((bf16[2,16,1024]{2,1,0:T(8,128)(2,1)S(1)}, bf16[2,16,1024]{2,1,0:T(8,128)(2,1)S(1)}, u32[]{:S(2)}, u32[]{:S(2)}) %collective-permute-start.2) | collective-permute-done | bytes 65568 | tf_op jit(solution)/shard_map/ppermute | solution.py:29
  30.1 1.6 %collective-permute-done.4.refs_5_.refs_2_ = bf16[1792,128]{1,0:T(8,128)(2,1)S(1)} collective-permute-done((bf16[1792,128]{1,0:T(8,128)(2,1)S(1)}, bf16[1792,128]{1,0:T(8,128)(2,1)S(1)}, u32[]{:S(2)}, u32[]{:S(2)}) %collective-permute-start.4) | collective-permute-done | bytes 458784 | tf_op jit(solution)/shard_map/ppermute | solution.py:29
  31.7 1.7 %collective-permute-start.10 = (bf16[1792,128]{1,0:T(8,128)(2,1)S(1)}, bf16[1792,128]{1,0:T(8,128)(2,1)S(1)}, u32[]{:S(2)}, u32[]{:S(2)}) collective-permute-start(bf16[1792,128]{1,0:T(8,128)(2,1)S(1)} %get-tuple-element.76), channel_id=1, source_target_pairs={{0,48},{8,56},{16,32},{24,40},{32,16},{40,24},{48,0},{56,8},{64,11... | collective-permute-start | bytes 1376264 | tf_op jit(solution)/shard_map/ppermute | solution.py:29
  33.4 1.9 %collective-permute-start.11 = (bf16[128,1408]{1,0:T(8,128)(2,1)S(1)}, bf16[128,1408]{1,0:T(8,128)(2,1)S(1)}, u32[]{:S(2)}, u32[]{:S(2)}) collective-permute-start(bf16[128,1408]{1,0:T(8,128)(2,1)S(1)} %get-tuple-element.77), channel_id=1, source_target_pairs={{0,16},{8,24},{16,0},{24,8},{32,48},{40,56},{48,32},{56,40},{64,80... | collective-permute-start | bytes 1081352 | tf_op jit(solution)/shard_map/ppermute | solution.py:29
  36.8 1.5 %collective-permute-start.7 = (bf16[4,16,1024]{2,1,0:T(8,128)(2,1)S(1)}, bf16[4,16,1024]{2,1,0:T(8,128)(2,1)S(1)}, u32[]{:S(2)}, u32[]{:S(2)}) collective-permute-start(bf16[4,16,1024]{2,1,0:T(8,128)(2,1)S(1)} %get-tuple-element.73.near_ref), channel_id=1, source_target_pairs={{0,2},{1,3},{2,0},{3,1},{4,6},{5,7},{6,4},{7,5},{8,10},{9,11},{10,... | collective-permute-start | bytes 393224 | tf_op jit(solution)/shard_map/ppermute | solution.py:29
  38.3 2.1 %collective-permute-start.8 = (bf16[4,16,1024]{2,1,0:T(8,128)(2,1)S(1)}, bf16[4,16,1024]{2,1,0:T(8,128)(2,1)S(1)}, u32[]{:S(2)}, u32[]{:S(2)}) collective-permute-start(bf16[4,16,1024]{2,1,0:T(8,128)(2,1)S(1)} %get-tuple-element.74.far_ref), channel_id=1, source_target_pairs={{0,6},{1,7},{2,4},{3,5},{4,2},{5,3},{6,0},{7,1},{8,14},{9,15},{10,... | collective-permute-start | bytes 393224 | tf_op jit(solution)/shard_map/ppermute | solution.py:29
  41.7 2.7 %collective-permute-done.8.far_x = bf16[4,16,1024]{2,1,0:T(8,128)(2,1)S(1)} collective-permute-done((bf16[4,16,1024]{2,1,0:T(8,128)(2,1)S(1)}, bf16[4,16,1024]{2,1,0:T(8,128)(2,1)S(1)}, u32[]{:S(2)}, u32[]{:S(2)}) %collective-permute-start.8) | collective-permute-done | bytes 131104 | tf_op jit(solution)/shard_map/ppermute | solution.py:29
  46.6 2.1 %collective-permute-start.12 = (bf16[2,4,16,1024]{3,2,1,0:T(8,128)(2,1)S(1)}, bf16[2,4,16,1024]{3,2,1,0:T(8,128)(2,1)S(1)}, u32[]{:S(2)}, u32[]{:S(2)}) collective-permute-start(bf16[2,4,16,1024]{3,2,1,0:T(8,128)(2,1)S(1)} %get-tuple-element.78.refs_1_), channel_id=1, source_target_pairs={{0,6},{1,7},{2,4},{3,5},{4,2},{5,3},{6,0},{7,1},{8,14},{9,15},{10,... | collective-permute-start | bytes 786440 | tf_op jit(solution)/shard_map/ppermute | solution.py:29
  49.9 3.4 %collective-permute-done.14.refs_0_ = bf16[128,1408]{1,0:T(8,128)(2,1)S(1)} collective-permute-done((bf16[128,1408]{1,0:T(8,128)(2,1)S(1)}, bf16[128,1408]{1,0:T(8,128)(2,1)S(1)}, u32[]{:S(2)}, u32[]{:S(2)}) %collective-permute-start.14) | collective-permute-done | bytes 360480 | tf_op jit(solution)/shard_map/ppermute | solution.py:29
  55.1 2.1 %shard_map.73 = (bf16[4,1792,128]{2,1,0:T(8,128)(2,1)S(1)}, bf16[4,1792,128]{2,1,0:T(8,128)(2,1)S(1)}, bf16[512,1024]{1,0:T(8,128)(2,1)S(1)}) custom-call(s32[1]{0:T(128)} %bitcast.1.refs_0_.place_ref, bf16[2,4,16,1024]{3,2,1,0:T(8,128)(2,1)S(1)} %get-tuple-element.78.refs_1_, bf16[2,4,16,1024]{3,2,1,0:T(8,128)(2,1)S(1)} %collective-permute-done.12.refs_2_, ...), custom_call_target="tpu_custom_call" | custom-call | flops 5000000000 | bytes 1 | tf_op jit(solution)/shard_map/pallas_call | solution.py:330
  57.3 2.1 %shard_map.74 = (bf16[4,16,1024]{2,1,0:T(8,128)(2,1)S(1)}, bf16[4,16,1024]{2,1,0:T(8,128)(2,1)S(1)}, bf16[2,4,16,1024]{3,2,1,0:T(8,128)(2,1)S(1)}, bf16[4,16,102...) custom-call(s32[1]{0:T(128)} %bitcast.1.refs_0_.place_ref, ...), custom_call_target="tpu_custom_call" | custom-call | flops 5000000000 | bytes 1 | tf_op jit(solution)/shard_map/pallas_call | solution.py:330
  61.5 2.3 %collective-permute-start.17 = (bf16[2,896,128]{2,1,0:T(8,128)(2,1)S(1)}, bf16[2,896,128]{2,1,0:T(8,128)(2,1)S(1)}, u32[]{:S(2)}, u32[]{:S(2)}) collective-permute-start(bf16[2,896,128]{2,1,0:T(8,128)(2,1)S(1)} %get-tuple-element.90.refs_6_), channel_id=1, source_target_pairs={{0,48},{8,56},{16,32},{24,40},{32,16},{40,24},{48,0},{56,8},{64,11... | collective-permute-start | bytes 1376264 | tf_op jit(solution)/shard_map/ppermute | solution.py:29
  63.7 3.5 %shard_map.76 = (bf16[128,1792]{1,0:T(8,128)(2,1)S(1)}, bf16[128,896]{1,0:T(8,128)(2,1)S(1)}, bf16[2,64,896]{2,1,0:T(8,128)(2,1)S(1)}, bf16[2,64,896]{2,1,0:T(8,128)(2,1)S(1)}) custom-call(bf16[512,1024]{1,0:T(8,128)(2,1)S(1)} %get-tuple-element.91.rows_ref, bf16[4,1792,128]{2,1,0:T(8,128)(2,1)S(1)} %copy-done.3, ...), custom_call_target="tpu_custom_call" | custom-call | flops 5000000000 | bytes 1 | tf_op jit(solution)/shard_map/pallas_call | solution.py:330
  67.2 2.1 %collective-permute-start.18 = (bf16[2,64,896]{2,1,0:T(8,128)(2,1)S(1)}, bf16[2,64,896]{2,1,0:T(8,128)(2,1)S(1)}, u32[]{:S(2)}, u32[]{:S(2)}) collective-permute-start(bf16[2,64,896]{2,1,0:T(8,128)(2,1)S(1)} %get-tuple-element.99), channel_id=1, source_target_pairs={{0,16},{8,24},{16,0},{24,8},{32,48},{40,56},{48,32},{56,40},{64,80... | collective-permute-start | bytes 688136 | tf_op jit(solution)/shard_map/ppermute | solution.py:29
  71.7 4.4 %collective-permute-done.21.first_far = bf16[4,16,1024]{2,1,0:T(8,128)(2,1)S(1)} collective-permute-done((bf16[4,16,1024]{2,1,0:T(8,128)(2,1)S(1)}, bf16[4,16,1024]{2,1,0:T(8,128)(2,1)S(1)}, u32[]{:S(2)}, u32[]{:S(2)}) %collective-permute-start.21) | collective-permute-done | bytes 131104 | tf_op jit(solution)/shard_map/ppermute | solution.py:29
  76.2 2.2 %collective-permute-start.23 = (bf16[2,896,128]{2,1,0:T(8,128)(2,1)S(1)}, bf16[2,896,128]{2,1,0:T(8,128)(2,1)S(1)}, u32[]{:S(2)}, u32[]{:S(2)}) collective-permute-start(bf16[2,896,128]{2,1,0:T(8,128)(2,1)S(1)} %get-tuple-element.111), channel_id=1, source_target_pairs={{0,48},{8,56},{16,32},{24,40},{32,16},{40,24},{48,0},{56,8},{64,11... | collective-permute-start | bytes 1376264 | tf_op jit(solution)/shard_map/ppermute | solution.py:29
  78.4 2.9 %collective-permute-start.24 = (bf16[896,128]{1,0:T(8,128)(2,1)S(1)}, bf16[896,128]{1,0:T(8,128)(2,1)S(1)}, u32[]{:S(2)}, u32[]{:S(2)}) collective-permute-start(bf16[896,128]{1,0:T(8,128)(2,1)S(1)} %get-tuple-element.112), channel_id=1, source_target_pairs={{0,64},{8,72},{16,80},{24,88},{32,96},{40,104},{48,112},{56,120},{... | collective-permute-start | bytes 688136 | tf_op jit(solution)/shard_map/ppermute | solution.py:29
  81.3 1.6 %collective-permute-start.25 = (bf16[2,64,896]{2,1,0:T(8,128)(2,1)S(1)}, bf16[2,64,896]{2,1,0:T(8,128)(2,1)S(1)}, u32[]{:S(2)}, u32[]{:S(2)}) collective-permute-start(bf16[2,64,896]{2,1,0:T(8,128)(2,1)S(1)} %get-tuple-element.113), channel_id=1, source_target_pairs={{0,16},{8,24},{16,0},{24,8},{32,48},{40,56},{48,32},{56,40},{64,80... | collective-permute-start | bytes 688136 | tf_op jit(solution)/shard_map/ppermute | solution.py:29
  82.9 5.0 %collective-permute-start.26 = (bf16[4,16,1024]{2,1,0:T(8,128)(2,1)S(1)}, bf16[4,16,1024]{2,1,0:T(8,128)(2,1)S(1)}, u32[]{:S(2)}, u32[]{:S(2)}) collective-permute-start(bf16[4,16,1024]{2,1,0:T(8,128)(2,1)S(1)} %get-tuple-element.115), channel_id=1, source_target_pairs={{0,1},{1,0},{2,3},{3,2},{4,5},{5,4},{6,7},{7,6},{8,9},{9,8},{10,11... | collective-permute-start | bytes 393224 | tf_op jit(solution)/shard_map/ppermute | solution.py:29
  87.8 2.1 %collective-permute-start.27 = (bf16[64,896]{1,0:T(8,128)(2,1)S(1)}, bf16[64,896]{1,0:T(8,128)(2,1)S(1)}, u32[]{:S(2)}, u32[]{:S(2)}) collective-permute-start(bf16[64,896]{1,0:T(8,128)(2,1)S(1)} %get-tuple-element.116), channel_id=1, source_target_pairs={{0,128},{8,136},{16,144},{24,152},{32,160},{40,168},{48,176},{56,1... | collective-permute-start | bytes 344072 | tf_op jit(solution)/shard_map/ppermute | solution.py:29
  89.9 8.1 %collective-permute-done.27.refs_1_.refs_8_ = bf16[64,896]{1,0:T(8,128)(2,1)S(1)} collective-permute-done((bf16[64,896]{1,0:T(8,128)(2,1)S(1)}, bf16[64,896]{1,0:T(8,128)(2,1)S(1)}, u32[]{:S(2)}, u32[]{:S(2)}) %collective-permute-start.27) | collective-permute-done | bytes 114720 | tf_op jit(solution)/shard_map/ppermute | solution.py:29
  98.3 2.7 %collective-permute-start.29 = (bf16[64,896]{1,0:T(8,128)(2,1)S(1)}, bf16[64,896]{1,0:T(8,128)(2,1)S(1)}, u32[]{:S(2)}, u32[]{:S(2)}) collective-permute-start(bf16[64,896]{1,0:T(8,128)(2,1)S(1)} %get-tuple-element.119), channel_id=1, source_target_pairs={{0,128},{8,136},{16,144},{24,152},{32,160},{40,168},{48,176},{56,1... | collective-permute-start | bytes 344072 | tf_op jit(solution)/shard_map/ppermute | solution.py:29
  102.7 2.7 %collective-permute-start.32 = (bf16[16,1024]{1,0:T(8,128)(2,1)S(1)}, bf16[16,1024]{1,0:T(8,128)(2,1)S(1)}, u32[]{:S(2)}, u32[]{:S(2)}) collective-permute-start(bf16[16,1024]{1,0:T(8,128)(2,1)S(1)} %get-tuple-element.125), channel_id=1, source_target_pairs={{0,144},{8,152},{16,128},{24,136},{32,176},{40,184},{48,160},{56,1... | collective-permute-start | bytes 98312 | tf_op jit(solution)/shard_map/ppermute | solution.py:29
  105.4 2.1 %collective-permute-done.31.refs_14_ = bf16[16,1024]{1,0:T(8,128)(2,1)S(1)} collective-permute-done((bf16[16,1024]{1,0:T(8,128)(2,1)S(1)}, bf16[16,1024]{1,0:T(8,128)(2,1)S(1)}, u32[]{:S(2)}, u32[]{:S(2)}) %collective-permute-start.31) | collective-permute-done | bytes 32800 | tf_op jit(solution)/shard_map/ppermute | solution.py:29
  107.5 3.0 %collective-permute-done.32.refs_15_ = bf16[16,1024]{1,0:T(8,128)(2,1)S(1)} collective-permute-done((bf16[16,1024]{1,0:T(8,128)(2,1)S(1)}, bf16[16,1024]{1,0:T(8,128)(2,1)S(1)}, u32[]{:S(2)}, u32[]{:S(2)}) %collective-permute-start.32) | collective-permute-done | bytes 32800 | tf_op jit(solution)/shard_map/ppermute | solution.py:29
  110.5 1.7 %shard_map.80 = (bf16[1792,128]{1,0:T(8,128)(2,1)}, bf16[128,1792]{1,0:T(8,128)(2,1)}, bf16[16,4096]{1,0:T(8,128)(2,1)}) custom-call(s32[1]{0:T(128)} %bitcast.place_ref, f32[2,1792,128]{2,1,0:T(8,128)S(1)} %get-tuple-element.89.sum_ref.refs_0_, bf16[2,896,128]{2,1,0:T(8,128)(2,1)S(1)} %collective-permute-done.17.far0_ref.refs_1_, ...), custom_call_target="tpu_custom_call" | custom-call | flops 1 | bytes 1 | tf_op jit(solution)/shard_map/pallas_call | solution.py:330
  (60 shorter events, 20.0 us)
Async XLA Ops:
  0.6 11.1 %collective-permute-start = (bf16[16,4096]{1,0:T(8,128)(2,1)}, bf16[16,4096]{1,0:T(8,128)(2,1)S(1)}, u32[]{:S(2)}, u32[]{:S(2)}) collective-permute-start(bf16[16,4096]{1,0:T(8,128)(2,1)} %grad_ref.1), channel_id=1, source_target_pairs={{0,1},{1,0},{2,3},{3,2},{4,5},{5,4},{6,7},{7,6},{8,9},{9,8},{10,11... | collective-permute-start | bytes 393224 | tf_op jit(solution)/shard_map/ppermute | solution.py:29
  11.8 18.2 %collective-permute-start.6 = (bf16[1792,128]{1,0:T(8,128)(2,1)S(1)}, bf16[1792,128]{1,0:T(8,128)(2,1)S(1)}, u32[]{:S(2)}, u32[]{:S(2)}) collective-permute-start(bf16[1792,128]{1,0:T(8,128)(2,1)S(1)} %get-tuple-element.71), channel_id=1, source_target_pairs={{0,48},{8,56},{16,32},{24,40},{32,16},{40,24},{48,0},{56,8},{64,11... | collective-permute-start | bytes 1376264 | tf_op jit(solution)/shard_map/ppermute | solution.py:29
  13.5 18.2 %collective-permute-start.4 = (bf16[1792,128]{1,0:T(8,128)(2,1)S(1)}, bf16[1792,128]{1,0:T(8,128)(2,1)S(1)}, u32[]{:S(2)}, u32[]{:S(2)}) collective-permute-start(bf16[1792,128]{1,0:T(8,128)(2,1)S(1)} %get-tuple-element.71), channel_id=1, source_target_pairs={{0,64},{8,72},{16,80},{24,88},{32,96},{40,104},{48,112},{56,120},{... | collective-permute-start | bytes 1376264 | tf_op jit(solution)/shard_map/ppermute | solution.py:29
  17.3 12.7 %collective-permute-start.5 = (bf16[64,1408]{1,0:T(8,128)(2,1)S(1)}, bf16[64,1408]{1,0:T(8,128)(2,1)S(1)}, u32[]{:S(2)}, u32[]{:S(2)}) collective-permute-start(bf16[64,1408]{1,0:T(8,128)(2,1)S(1)} %get-tuple-element.72), channel_id=1, source_target_pairs={{0,128},{8,136},{16,144},{24,152},{32,160},{40,168},{48,176},{56,1... | collective-permute-start | bytes 540680 | tf_op jit(solution)/shard_map/ppermute | solution.py:29
  18.1 4.3 %collective-permute-start.1 = (bf16[2,16,1024]{2,1,0:T(8,128)(2,1)S(1)}, bf16[2,16,1024]{2,1,0:T(8,128)(2,1)S(1)}, u32[]{:S(2)}, u32[]{:S(2)}) collective-permute-start(bf16[2,16,1024]{2,1,0:T(8,128)(2,1)S(1)} %get-tuple-element.68), channel_id=1, source_target_pairs={{0,16},{8,24},{16,0},{24,8},{32,48},{40,56},{48,32},{56,40},{64,80... | collective-permute-start | bytes 196616 | tf_op jit(solution)/shard_map/ppermute | solution.py:29
  20.0 9.4 %collective-permute-start.2 = (bf16[2,16,1024]{2,1,0:T(8,128)(2,1)S(1)}, bf16[2,16,1024]{2,1,0:T(8,128)(2,1)S(1)}, u32[]{:S(2)}, u32[]{:S(2)}) collective-permute-start(bf16[2,16,1024]{2,1,0:T(8,128)(2,1)S(1)} %get-tuple-element.69), channel_id=1, source_target_pairs={{0,128},{8,136},{16,144},{24,152},{32,160},{40,168},{48,176},{56,1... | collective-permute-start | bytes 196616 | tf_op jit(solution)/shard_map/ppermute | solution.py:29
  22.3 7.7 %collective-permute-start.3 = (bf16[2,16,1024]{2,1,0:T(8,128)(2,1)S(1)}, bf16[2,16,1024]{2,1,0:T(8,128)(2,1)S(1)}, u32[]{:S(2)}, u32[]{:S(2)}) collective-permute-start(bf16[2,16,1024]{2,1,0:T(8,128)(2,1)S(1)} %get-tuple-element.70), channel_id=1, source_target_pairs={{0,144},{8,152},{16,128},{24,136},{32,176},{40,184},{48,160},{56,1... | collective-permute-start | bytes 196616 | tf_op jit(solution)/shard_map/ppermute | solution.py:29
  31.7 12.7 %collective-permute-start.10 = (bf16[1792,128]{1,0:T(8,128)(2,1)S(1)}, bf16[1792,128]{1,0:T(8,128)(2,1)S(1)}, u32[]{:S(2)}, u32[]{:S(2)}) collective-permute-start(bf16[1792,128]{1,0:T(8,128)(2,1)S(1)} %get-tuple-element.76), channel_id=1, source_target_pairs={{0,48},{8,56},{16,32},{24,40},{32,16},{40,24},{48,0},{56,8},{64,11... | collective-permute-start | bytes 1376264 | tf_op jit(solution)/shard_map/ppermute | solution.py:29
  33.4 11.0 %collective-permute-start.11 = (bf16[128,1408]{1,0:T(8,128)(2,1)S(1)}, bf16[128,1408]{1,0:T(8,128)(2,1)S(1)}, u32[]{:S(2)}, u32[]{:S(2)}) collective-permute-start(bf16[128,1408]{1,0:T(8,128)(2,1)S(1)} %get-tuple-element.77), channel_id=1, source_target_pairs={{0,16},{8,24},{16,0},{24,8},{32,48},{40,56},{48,32},{56,40},{64,80... | collective-permute-start | bytes 1081352 | tf_op jit(solution)/shard_map/ppermute | solution.py:29
  35.3 9.2 %collective-permute-start.9 = (bf16[64,1408]{1,0:T(8,128)(2,1)S(1)}, bf16[64,1408]{1,0:T(8,128)(2,1)S(1)}, u32[]{:S(2)}, u32[]{:S(2)}) collective-permute-start(bf16[64,1408]{1,0:T(8,128)(2,1)S(1)} %get-tuple-element.75), channel_id=1, source_target_pairs={{0,128},{8,136},{16,144},{24,152},{32,160},{40,168},{48,176},{56,1... | collective-permute-start | bytes 540680 | tf_op jit(solution)/shard_map/ppermute | solution.py:29
  36.8 5.0 %collective-permute-start.7 = (bf16[4,16,1024]{2,1,0:T(8,128)(2,1)S(1)}, bf16[4,16,1024]{2,1,0:T(8,128)(2,1)S(1)}, u32[]{:S(2)}, u32[]{:S(2)}) collective-permute-start(bf16[4,16,1024]{2,1,0:T(8,128)(2,1)S(1)} %get-tuple-element.73.near_ref), channel_id=1, source_target_pairs={{0,2},{1,3},{2,0},{3,1},{4,6},{5,7},{6,4},{7,5},{8,10},{9,11},{10,... | collective-permute-start | bytes 393224 | tf_op jit(solution)/shard_map/ppermute | solution.py:29
  38.3 6.2 %collective-permute-start.8 = (bf16[4,16,1024]{2,1,0:T(8,128)(2,1)S(1)}, bf16[4,16,1024]{2,1,0:T(8,128)(2,1)S(1)}, u32[]{:S(2)}, u32[]{:S(2)}) collective-permute-start(bf16[4,16,1024]{2,1,0:T(8,128)(2,1)S(1)} %get-tuple-element.74.far_ref), channel_id=1, source_target_pairs={{0,6},{1,7},{2,4},{3,5},{4,2},{5,3},{6,0},{7,1},{8,14},{9,15},{10,... | collective-permute-start | bytes 393224 | tf_op jit(solution)/shard_map/ppermute | solution.py:29
  45.9 7.4 %collective-permute-start.14 = (bf16[128,1408]{1,0:T(8,128)(2,1)S(1)}, bf16[128,1408]{1,0:T(8,128)(2,1)S(1)}, u32[]{:S(2)}, u32[]{:S(2)}) collective-permute-start(bf16[128,1408]{1,0:T(8,128)(2,1)S(1)} %get-tuple-element.81.refs_1_), channel_id=1, source_target_pairs={{0,16},{8,24},{16,0},{24,8},{32,48},{40,56},{48,32},{56,40},{64,80... | collective-permute-start | bytes 1081352 | tf_op jit(solution)/shard_map/ppermute | solution.py:29
  46.6 7.6 %collective-permute-start.12 = (bf16[2,4,16,1024]{3,2,1,0:T(8,128)(2,1)S(1)}, bf16[2,4,16,1024]{3,2,1,0:T(8,128)(2,1)S(1)}, u32[]{:S(2)}, u32[]{:S(2)}) collective-permute-start(bf16[2,4,16,1024]{3,2,1,0:T(8,128)(2,1)S(1)} %get-tuple-element.78.refs_1_), channel_id=1, source_target_pairs={{0,6},{1,7},{2,4},{3,5},{4,2},{5,3},{6,0},{7,1},{8,14},{9,15},{10,... | collective-permute-start | bytes 786440 | tf_op jit(solution)/shard_map/ppermute | solution.py:29
  48.7 6.4 %collective-permute-start.13 = (bf16[2,4,16,1024]{3,2,1,0:T(8,128)(2,1)S(1)}, bf16[2,4,16,1024]{3,2,1,0:T(8,128)(2,1)S(1)}, u32[]{:S(2)}, u32[]{:S(2)}) collective-permute-start(bf16[2,4,16,1024]{3,2,1,0:T(8,128)(2,1)S(1)} %get-tuple-element.79.refs_3_), channel_id=1, source_target_pairs={{0,2},{1,3},{2,0},{3,1},{4,6},{5,7},{6,4},{7,5},{8,10},{9,11},{10,... | collective-permute-start | bytes 786440 | tf_op jit(solution)/shard_map/ppermute | solution.py:29
  48.7 8.6 %collective-permute-start.16 = (bf16[4,1792,128]{2,1,0:T(8,128)(2,1)}, bf16[4,1792,128]{2,1,0:T(8,128)(2,1)S(1)}, u32[]{:S(2)}, u32[]{:S(2)}) collective-permute-start(bf16[4,1792,128]{2,1,0:T(8,128)(2,1)} %copy-done.2), channel_id=1, source_target_pairs={{0,8},{8,0},{16,24},{24,16},{32,40},{40,32},{48,56},{56,48},{64,72... | collective-permute-start | bytes 5505032 | tf_op jit(solution)/shard_map/ppermute | solution.py:29
  59.5 9.8 %collective-permute-start.19 = (bf16[2,4,16,1024]{3,2,1,0:T(8,128)(2,1)S(1)}, bf16[2,4,16,1024]{3,2,1,0:T(8,128)(2,1)S(1)}, u32[]{:S(2)}, u32[]{:S(2)}) collective-permute-start(bf16[2,4,16,1024]{3,2,1,0:T(8,128)(2,1)S(1)} %get-tuple-element.101), channel_id=1, source_target_pairs={{0,2},{1,3},{2,0},{3,1},{4,6},{5,7},{6,4},{7,5},{8,10},{9,11},{10,... | collective-permute-start | bytes 786440 | tf_op jit(solution)/shard_map/ppermute | solution.py:29
  59.6 9.9 %collective-permute-start.20 = (bf16[2,4,16,1024]{3,2,1,0:T(8,128)(2,1)S(1)}, bf16[2,4,16,1024]{3,2,1,0:T(8,128)(2,1)S(1)}, u32[]{:S(2)}, u32[]{:S(2)}) collective-permute-start(bf16[2,4,16,1024]{3,2,1,0:T(8,128)(2,1)S(1)} %get-tuple-element.104), channel_id=1, source_target_pairs={{0,6},{1,7},{2,4},{3,5},{4,2},{5,3},{6,0},{7,1},{8,14},{9,15},{10,... | collective-permute-start | bytes 786440 | tf_op jit(solution)/shard_map/ppermute | solution.py:29
  61.5 14.6 %collective-permute-start.17 = (bf16[2,896,128]{2,1,0:T(8,128)(2,1)S(1)}, bf16[2,896,128]{2,1,0:T(8,128)(2,1)S(1)}, u32[]{:S(2)}, u32[]{:S(2)}) collective-permute-start(bf16[2,896,128]{2,1,0:T(8,128)(2,1)S(1)} %get-tuple-element.90.refs_6_), channel_id=1, source_target_pairs={{0,48},{8,56},{16,32},{24,40},{32,16},{40,24},{48,0},{56,8},{64,11... | collective-permute-start | bytes 1376264 | tf_op jit(solution)/shard_map/ppermute | solution.py:29
  67.2 8.9 %collective-permute-start.18 = (bf16[2,64,896]{2,1,0:T(8,128)(2,1)S(1)}, bf16[2,64,896]{2,1,0:T(8,128)(2,1)S(1)}, u32[]{:S(2)}, u32[]{:S(2)}) collective-permute-start(bf16[2,64,896]{2,1,0:T(8,128)(2,1)S(1)} %get-tuple-element.99), channel_id=1, source_target_pairs={{0,16},{8,24},{16,0},{24,8},{32,48},{40,56},{48,32},{56,40},{64,80... | collective-permute-start | bytes 688136 | tf_op jit(solution)/shard_map/ppermute | solution.py:29
  69.7 6.4 %collective-permute-start.21 = (bf16[4,16,1024]{2,1,0:T(8,128)(2,1)S(1)}, bf16[4,16,1024]{2,1,0:T(8,128)(2,1)S(1)}, u32[]{:S(2)}, u32[]{:S(2)}) collective-permute-start(bf16[4,16,1024]{2,1,0:T(8,128)(2,1)S(1)} %get-tuple-element.106), channel_id=1, source_target_pairs={{0,6},{1,7},{2,4},{3,5},{4,2},{5,3},{6,0},{7,1},{8,14},{9,15},{10,... | collective-permute-start | bytes 393224 | tf_op jit(solution)/shard_map/ppermute | solution.py:29
  71.0 5.1 %collective-permute-start.22 = (bf16[4,16,1024]{2,1,0:T(8,128)(2,1)S(1)}, bf16[4,16,1024]{2,1,0:T(8,128)(2,1)S(1)}, u32[]{:S(2)}, u32[]{:S(2)}) collective-permute-start(bf16[4,16,1024]{2,1,0:T(8,128)(2,1)S(1)} %get-tuple-element.108), channel_id=1, source_target_pairs={{0,2},{1,3},{2,0},{3,1},{4,6},{5,7},{6,4},{7,5},{8,10},{9,11},{10,... | collective-permute-start | bytes 393224 | tf_op jit(solution)/shard_map/ppermute | solution.py:29
  76.2 21.9 %collective-permute-start.23 = (bf16[2,896,128]{2,1,0:T(8,128)(2,1)S(1)}, bf16[2,896,128]{2,1,0:T(8,128)(2,1)S(1)}, u32[]{:S(2)}, u32[]{:S(2)}) collective-permute-start(bf16[2,896,128]{2,1,0:T(8,128)(2,1)S(1)} %get-tuple-element.111), channel_id=1, source_target_pairs={{0,48},{8,56},{16,32},{24,40},{32,16},{40,24},{48,0},{56,8},{64,11... | collective-permute-start | bytes 1376264 | tf_op jit(solution)/shard_map/ppermute | solution.py:29
  78.4 19.7 %collective-permute-start.24 = (bf16[896,128]{1,0:T(8,128)(2,1)S(1)}, bf16[896,128]{1,0:T(8,128)(2,1)S(1)}, u32[]{:S(2)}, u32[]{:S(2)}) collective-permute-start(bf16[896,128]{1,0:T(8,128)(2,1)S(1)} %get-tuple-element.112), channel_id=1, source_target_pairs={{0,64},{8,72},{16,80},{24,88},{32,96},{40,104},{48,112},{56,120},{... | collective-permute-start | bytes 688136 | tf_op jit(solution)/shard_map/ppermute | solution.py:29
  81.3 16.8 %collective-permute-start.25 = (bf16[2,64,896]{2,1,0:T(8,128)(2,1)S(1)}, bf16[2,64,896]{2,1,0:T(8,128)(2,1)S(1)}, u32[]{:S(2)}, u32[]{:S(2)}) collective-permute-start(bf16[2,64,896]{2,1,0:T(8,128)(2,1)S(1)} %get-tuple-element.113), channel_id=1, source_target_pairs={{0,16},{8,24},{16,0},{24,8},{32,48},{40,56},{48,32},{56,40},{64,80... | collective-permute-start | bytes 688136 | tf_op jit(solution)/shard_map/ppermute | solution.py:29
  82.9 15.2 %collective-permute-start.26 = (bf16[4,16,1024]{2,1,0:T(8,128)(2,1)S(1)}, bf16[4,16,1024]{2,1,0:T(8,128)(2,1)S(1)}, u32[]{:S(2)}, u32[]{:S(2)}) collective-permute-start(bf16[4,16,1024]{2,1,0:T(8,128)(2,1)S(1)} %get-tuple-element.115), channel_id=1, source_target_pairs={{0,1},{1,0},{2,3},{3,2},{4,5},{5,4},{6,7},{7,6},{8,9},{9,8},{10,11... | collective-permute-start | bytes 393224 | tf_op jit(solution)/shard_map/ppermute | solution.py:29
  87.8 10.2 %collective-permute-start.27 = (bf16[64,896]{1,0:T(8,128)(2,1)S(1)}, bf16[64,896]{1,0:T(8,128)(2,1)S(1)}, u32[]{:S(2)}, u32[]{:S(2)}) collective-permute-start(bf16[64,896]{1,0:T(8,128)(2,1)S(1)} %get-tuple-element.116), channel_id=1, source_target_pairs={{0,128},{8,136},{16,144},{24,152},{32,160},{40,168},{48,176},{56,1... | collective-permute-start | bytes 344072 | tf_op jit(solution)/shard_map/ppermute | solution.py:29
  98.2 12.3 %collective-permute-start.28 = (bf16[896,128]{1,0:T(8,128)(2,1)S(1)}, bf16[896,128]{1,0:T(8,128)(2,1)S(1)}, u32[]{:S(2)}, u32[]{:S(2)}) collective-permute-start(bf16[896,128]{1,0:T(8,128)(2,1)S(1)} %get-tuple-element.117), channel_id=1, source_target_pairs={{0,64},{8,72},{16,80},{24,88},{32,96},{40,104},{48,112},{56,120},{... | collective-permute-start | bytes 688136 | tf_op jit(solution)/shard_map/ppermute | solution.py:29
  98.3 12.2 %collective-permute-start.29 = (bf16[64,896]{1,0:T(8,128)(2,1)S(1)}, bf16[64,896]{1,0:T(8,128)(2,1)S(1)}, u32[]{:S(2)}, u32[]{:S(2)}) collective-permute-start(bf16[64,896]{1,0:T(8,128)(2,1)S(1)} %get-tuple-element.119), channel_id=1, source_target_pairs={{0,128},{8,136},{16,144},{24,152},{32,160},{40,168},{48,176},{56,1... | collective-permute-start | bytes 344072 | tf_op jit(solution)/shard_map/ppermute | solution.py:29
  101.0 4.4 %collective-permute-start.30 = (bf16[16,1024]{1,0:T(8,128)(2,1)S(1)}, bf16[16,1024]{1,0:T(8,128)(2,1)S(1)}, u32[]{:S(2)}, u32[]{:S(2)}) collective-permute-start(bf16[16,1024]{1,0:T(8,128)(2,1)S(1)} %get-tuple-element.123), channel_id=1, source_target_pairs={{0,16},{8,24},{16,0},{24,8},{32,48},{40,56},{48,32},{56,40},{64,80... | collective-permute-start | bytes 98312 | tf_op jit(solution)/shard_map/ppermute | solution.py:29
  102.5 5.0 %collective-permute-start.31 = (bf16[16,1024]{1,0:T(8,128)(2,1)S(1)}, bf16[16,1024]{1,0:T(8,128)(2,1)S(1)}, u32[]{:S(2)}, u32[]{:S(2)}) collective-permute-start(bf16[16,1024]{1,0:T(8,128)(2,1)S(1)} %get-tuple-element.124), channel_id=1, source_target_pairs={{0,128},{8,136},{16,144},{24,152},{32,160},{40,168},{48,176},{56,1... | collective-permute-start | bytes 98312 | tf_op jit(solution)/shard_map/ppermute | solution.py:29
  102.7 7.8 %collective-permute-start.32 = (bf16[16,1024]{1,0:T(8,128)(2,1)S(1)}, bf16[16,1024]{1,0:T(8,128)(2,1)S(1)}, u32[]{:S(2)}, u32[]{:S(2)}) collective-permute-start(bf16[16,1024]{1,0:T(8,128)(2,1)S(1)} %get-tuple-element.125), channel_id=1, source_target_pairs={{0,144},{8,152},{16,128},{24,136},{32,176},{40,184},{48,160},{56,1... | collective-permute-start | bytes 98312 | tf_op jit(solution)/shard_map/ppermute | solution.py:29
  (7 other events, 13.1 us)
